TPU v7x, 32 devices: a whole 2x2x4 slice. The times are simulated.
32 devices in a mesh: tm: 2 (over y), space: 16 (over z, x, core).
Axes of the slice: x: 2, y: 2, z: 4, core: 2. Of those that a mesh axis runs over, the one named last changes fastest.
Arguments:
- snapshots: bfloat16 [128, 128, 4096], P('tm', None, 'space'), as said below
- frequencies: int32 [4], replicated, may hold values from 1 to 63, as said below
- offsets: int32 [128], P('tm'), may hold values from 0 to 16383
Outputs:
- modes: float32 [4, 2, 128, 4096], P('tm', None, None, 'space')
Inputs may be any that keep to these rules, and one draw needn't show every extreme that they name: `frequencies`: the kept frequency indices are distinct and include 1 and 63. `snapshots`: snapshot values of the record.
All inputs are finite; a program needn't handle non-finite values.
Results may differ from a plain program's by a relative error of at most 0.0041.
Values may be sent and summed in bfloat16 or wider, within the bound.
No kernel may reach another device: no remote copies, remote signals or barrier semaphores. Data moves between devices by JAX's collectives and lax.ppermute only.
A program may use at most 64 MiB of HBM per device.

v0:
```python
import math

import jax
import jax.numpy as jnp
from jax import lax
from jax.sharding import PartitionSpec as P


def make_angle_table(frequencies, length):
    positions = jnp.arange(length, dtype=jnp.int32)
    turn_counts = frequencies[None, :] * positions[:, None] % length
    radians = turn_counts.astype(jnp.float32) * (2.0 * math.pi / length)
    window = 0.5 - 0.5 * jnp.cos(positions.astype(jnp.float32) * (2.0 * math.pi / length))
    cosine_cols = window[:, None] * jnp.cos(radians)
    sine_cols = window[:, None] * jnp.sin(radians)
    return jnp.concatenate([cosine_cols, sine_cols], axis=1).astype(jnp.bfloat16)


def embed_gram(gram_real, gram_imag):
    top_rows = jnp.stack([gram_real, -gram_imag], axis=-1)
    low_rows = jnp.stack([gram_imag, gram_real], axis=-1)
    order = gram_real.shape[0]
    return jnp.stack([top_rows, low_rows], axis=1).reshape(2 * order, 2 * order)


def local_gram(real_rows, imag_rows):
    real_gram = jnp.dot(real_rows, real_rows.T, preferred_element_type=jnp.float32) + jnp.dot(
        imag_rows, imag_rows.T, preferred_element_type=jnp.float32
    )
    cross = jnp.dot(imag_rows, real_rows.T, preferred_element_type=jnp.float32)
    imag_gram = cross - cross.T
    return jnp.stack([real_gram, imag_gram])


def unpack_gram(packed):
    return (packed[0], packed[1])


def finish_modes(packed, real_rows, imag_rows, total_cells):
    gram_real, gram_imag = unpack_gram(packed)
    embedded = embed_gram(gram_real / total_cells, gram_imag / total_cells)
    lower_factor = jnp.linalg.cholesky(embedded)
    order = real_rows.shape[0]
    cells_here = real_rows.shape[1]
    stacked_rows = (
        jnp.stack([real_rows, imag_rows], axis=1).reshape(2 * order, cells_here).astype(jnp.float32)
    )
    solved = lax.linalg.triangular_solve(lower_factor, stacked_rows, left_side=True, lower=True)
    return jnp.transpose(solved.reshape(order, 2, cells_here), (1, 0, 2))


def local(snapshots, frequencies, offsets):
    length = snapshots.shape[1]
    count_all = frequencies.shape[0]
    angle_table = make_angle_table(frequencies, length)
    projected = jnp.einsum(
        "btc,tk->kbc", snapshots, angle_table, preferred_element_type=jnp.float32
    )
    cos_part = projected[:count_all]
    sin_part = projected[count_all:]
    turn_counts = frequencies[:, None] * offsets[None, :] % length
    phase = turn_counts.astype(jnp.float32) * (2.0 * math.pi / length)
    cos_phase = jnp.cos(phase)[:, :, None]
    sin_phase = jnp.sin(phase)[:, :, None]
    real_part = cos_part * cos_phase - sin_part * sin_phase
    imag_part = -(sin_part * cos_phase + cos_part * sin_phase)
    stacked = jnp.stack([real_part, imag_part]).astype(jnp.bfloat16)
    regrouped = lax.all_to_all(stacked, "tm", split_axis=1, concat_axis=2, tiled=True)
    cells_here = regrouped.shape[3]
    total_cells = cells_here * lax.axis_size("space")
    per_freq = [
        (regrouped[0, slot_index], regrouped[1, slot_index])
        for slot_index in range(regrouped.shape[1])
    ]
    local_grams = jnp.stack([local_gram(real_rows, imag_rows) for real_rows, imag_rows in per_freq])
    summed = lax.psum(local_grams, "space")
    results = [
        finish_modes(
            summed[slot_index], per_freq[slot_index][0], per_freq[slot_index][1], total_cells
        )
        for slot_index in range(len(per_freq))
    ]
    return jnp.stack(results)


def solution(mesh):
    placed = (P("tm", None, "space"), P(), P("tm"))
    return jax.shard_map(
        local, mesh=mesh, in_specs=placed, out_specs=P("tm", None, None, "space"), check_vma=False
    )
```

profile of v0, /device:TPU:0, one launch (start us, length us, event | category | flops | bytes accessed | tf_op | source)
XLA Modules:
  0.0 290.4 jit_solution(9716850305125664532)
XLA Ops:
  6.6 0.8 multiply_convert_fusion.1
  7.4 0.8 fusion.56
  8.1 0.1 copy.47
  8.3 2.8 fusion.52
  11.2 0.3 fusion.8
  11.5 0.2 pad_maximum_fusion.1
  11.6 0.7 copy.49
  12.4 4.2 %all-to-all-start = ((bf16[2,4,64,256]{3,2,0,1:T(8,128)(2,1)}), bf16[2,4,64,256]{3,2,0,1:T(8,128)(2,1)S(1)}, u32[]{:S(2)}, u32[]{:S(2)}) async-start(bf16[2,4,64,256]{3,2,0,1:T(8,128)(2,1)} %copy.49), calls=%async_computation | async-start | bytes 524288 | tf_op jit(solution)/shard_map/all_to_all | solution.py:68
  16.6 5.9 %all-to-all-done = bf16[2,4,64,256]{3,2,0,1:T(8,128)(2,1)S(1)} async-done(((bf16[2,4,64,256]{3,2,0,1:T(8,128)(2,1)}), bf16[2,4,64,256]{3,2,0,1:T(8,128)(2,1)S(1)}, u32[]{:S(2)}, u32[]{:S(2)}) %all-to-all-start) | async-done | bytes 262176 | tf_op jit(solution)/shard_map/all_to_all | solution.py:68
  22.5 0.1 fusion.25
  22.6 0.2 fusion.32
  22.8 0.2 fusion.29
  23.0 0.2 fusion.36
  23.4 0.2 fusion
  23.6 0.2 fusion.1
  23.8 0.7 pad_maximum_fusion.2
  24.6 0.2 copy.56
  24.8 0.2 reshape.206
  25.0 0.2 copy.60
  25.2 0.2 reshape.207
  25.4 88.6 %all-reduce.3.cloned.1.call-done = f32[2,2,128,128]{3,2,1,0:T(8,128)} async-done(((f32[2,2,128,128]{3,2,1,0:T(8,128)}), f32[2,2,128,128]{3,2,1,0:T(8,128)}) %all-reduce.3.cloned.1.call-update) | async-done | bytes 262160 | tf_op jit(solution)/shard_map/psum | solution.py:76
  114.0 1.0 fusion.20
  114.9 0.9 fusion.58
  115.9 8.8 %copy.54 = f32[128,2,128,2]{3,2,1,0:T(8,128)} copy(f32[128,2,128,2]{2,0,3,1:T(8,128)S(1)} %pad_maximum_fusion.3) | data formatting | bytes 524288 | tf_op jit(solution)/shard_map/stack | solution.py:23
  124.7 12.7 %reshape.178 = f32[256,256]{1,0:T(8,128)S(1)} reshape(f32[128,2,128,2]{3,2,1,0:T(8,128)} %copy.54) | data formatting | bytes 524288 | tf_op jit(solution)/shard_map/reshape | solution.py:23
  137.4 0.1 copy.55
  137.6 11.7 %cholesky.130 = f32[128,128]{1,0:T(8,128)S(1)} custom-call(f32[128,128]{1,0:T(8,128)S(1)} %cholesky.194), custom_call_target="Cholesky" | custom-call | tf_op jit(solution)/shard_map/jit(cholesky)/cholesky | solution.py:42
  149.4 9.8 %custom-call.13 = f32[1,128,128]{1,2,0:T(8,128)S(1)} custom-call(f32[1,128,128]{2,1,0:T(8,128)S(1)} %get-tuple-element.58), custom_call_target="InvertDiagBlocksLowerTriangular" | custom-call | tf_op jit(solution)/shard_map/jit(cholesky)/cholesky | solution.py:42
  159.2 0.2 constant_dynamic-update-slice_fusion.3
  159.4 0.3 convolution_subtract_fusion.3
  159.7 11.7 %cholesky.147 = f32[128,128]{1,0:T(8,128)S(1)} custom-call(f32[128,128]{1,0:T(8,128)S(1)} %convolution_subtract_fusion.3), custom_call_target="Cholesky" | custom-call | tf_op jit(solution)/shard_map/jit(cholesky)/cholesky | solution.py:42
  171.4 0.7 compare_reduce_fusion.2
  172.2 0.6 compare_reduce_fusion.3
  174.2 4.1 %while.4 = (s32[]{:T(128)}, f32[256,256]{1,0:T(8,128)S(1)}, s32[2,2]{1,0:T(2,128)S(1)}, f32[2,128,128]{2,1,0:T(8,128)S(1)}, s32[]{:T(128)}) while((s32[]{:T(128)}, f32[256,256]{1,0:T(8,128)S(1)}, s32[2,2]{1,0:T(2,128)S(1)}, f32[2,128,128]{2,1,0:T(8,128)S(1)}, s32[]{:T(128)}) %tuple.59), condition=%wide.while_cond, body=%wide.while_body.sunk | while | flops 2 | bytes 131181 | solution.py:48
  174.3 0.6 fusion.73
  174.9 1.4 bitcast_dynamic-update-slice_fusion.4
  176.3 0.6 fusion.73
  176.9 1.4 bitcast_dynamic-update-slice_fusion.4
  178.4 19.9 %custom-call.14 = f32[2,128,128]{1,2,0:T(8,128)S(1)} custom-call(f32[2,128,128]{2,1,0:T(8,128)S(1)} %get-tuple-element.21), custom_call_target="InvertDiagBlocksLowerTriangular" | custom-call | tf_op jit(solution)/shard_map/triangular_solve/custom-call.0 | solution.py:48
  198.3 0.3 fusion.6
  198.6 0.3 convolution_subtract_fusion.1
  198.9 0.3 fusion.17
  199.2 0.1 reshape.179
  199.4 8.7 %copy.58 = f32[128,2,128,2]{3,2,1,0:T(8,128)} copy(f32[128,2,128,2]{2,0,3,1:T(8,128)S(1)} %pad_maximum_fusion.5) | data formatting | bytes 524288 | tf_op jit(solution)/shard_map/stack | solution.py:23
  208.1 12.7 %reshape.180 = f32[256,256]{1,0:T(8,128)S(1)} reshape(f32[128,2,128,2]{3,2,1,0:T(8,128)} %copy.58) | data formatting | bytes 524288 | tf_op jit(solution)/shard_map/reshape | solution.py:23
  220.8 0.1 copy.59
  221.0 11.7 %cholesky.164 = f32[128,128]{1,0:T(8,128)S(1)} custom-call(f32[128,128]{1,0:T(8,128)S(1)} %cholesky.197), custom_call_target="Cholesky" | custom-call | tf_op jit(solution)/shard_map/jit(cholesky)/cholesky | solution.py:42
  232.8 9.8 %custom-call.15 = f32[1,128,128]{1,2,0:T(8,128)S(1)} custom-call(f32[1,128,128]{2,1,0:T(8,128)S(1)} %get-tuple-element.64), custom_call_target="InvertDiagBlocksLowerTriangular" | custom-call | tf_op jit(solution)/shard_map/jit(cholesky)/cholesky | solution.py:42
  242.6 0.2 constant_dynamic-update-slice_fusion.1
  242.8 0.3 convolution_subtract_fusion.2
  243.1 11.7 %cholesky.181 = f32[128,128]{1,0:T(8,128)S(1)} custom-call(f32[128,128]{1,0:T(8,128)S(1)} %convolution_subtract_fusion.2), custom_call_target="Cholesky" | custom-call | tf_op jit(solution)/shard_map/jit(cholesky)/cholesky | solution.py:42
  254.8 0.7 compare_reduce_fusion
  255.5 0.6 compare_reduce_fusion.1
  257.6 4.1 %while.5 = (s32[]{:T(128)}, f32[256,256]{1,0:T(8,128)S(1)}, s32[2,2]{1,0:T(2,128)S(1)}, f32[2,128,128]{2,1,0:T(8,128)S(1)}, s32[]{:T(128)}) while((s32[]{:T(128)}, f32[256,256]{1,0:T(8,128)S(1)}, s32[2,2]{1,0:T(2,128)S(1)}, f32[2,128,128]{2,1,0:T(8,128)S(1)}, s32[]{:T(128)}) %tuple.64), condition=%wide.while_cond.clone, body=%wide.while_body.clone.sunk | while | flops 2 | bytes 131181 | solution.py:48
  257.6 0.6 fusion.74
  258.2 1.4 bitcast_dynamic-update-slice_fusion.5
  259.6 0.6 fusion.74
  260.2 1.4 bitcast_dynamic-update-slice_fusion.5
  261.7 19.9 %custom-call.16 = f32[2,128,128]{1,2,0:T(8,128)S(1)} custom-call(f32[2,128,128]{2,1,0:T(8,128)S(1)} %get-tuple-element.22), custom_call_target="InvertDiagBlocksLowerTriangular" | custom-call | tf_op jit(solution)/shard_map/triangular_solve/custom-call.0 | solution.py:48
  281.6 0.3 fusion.4
  281.9 0.3 convolution_subtract_fusion
  282.2 0.3 fusion.11
  282.6 0.1 reshape.181
  282.7 0.8 pad_maximum_fusion
  (40 shorter events, 1.1 us)
Async XLA Ops:
  12.4 10.1 %all-to-all-start = ((bf16[2,4,64,256]{3,2,0,1:T(8,128)(2,1)}), bf16[2,4,64,256]{3,2,0,1:T(8,128)(2,1)S(1)}, u32[]{:S(2)}, u32[]{:S(2)}) async-start(bf16[2,4,64,256]{3,2,0,1:T(8,128)(2,1)} %copy.49), calls=%async_computation | async-start | bytes 524288 | tf_op jit(solution)/shard_map/all_to_all | solution.py:68
  16.6 97.4 %all-reduce.3.cloned.1.call-start = ((), (), s32[]{:S(2)}) async-start(), calls=%async_computation.1 | async-start | bytes 524288 | tf_op jit(solution)/shard_map/psum | solution.py:76
Sparse Core Ops, SparseCore 0:
  24.6 89.2 all-reduce.2
where the time goes:
time: 291 us; the launch traced here: 290 us
  other arithmetic  115 us (40%)
  waiting for transfers between devices  94.5 us (32%)
  local copies, waits for them, and re-layouts  53.6 us (18%)
  between operations  16.5 us (6%)
  matrix products  6.52 us (2%)
  starting transfers between devices  4.24 us (1%)
    psum x1, waiting for transfers between devices, local(): summed = lax.psum(local_grams, 'space')  88.6 us
    another operation x14, other arithmetic, finish_modes(): lower_factor = jnp.linalg.cholesky(embedded)  69.3 us
    another operation x7, other arithmetic, finish_modes(): lax.linalg.triangular_solve(lower_factor, stacked_rows, left_side=True, l...  39.9 us
    reshape x4, local copies, waits for them, and re-layouts, embed_gram(): return jnp.stack([top_rows, low_rows], axis=1).reshape(2 * order, 2 * order)  25.6 us
    another operation x2, local copies, waits for them, and re-layouts, embed_gram(): return jnp.stack([top_rows, low_rows], axis=1).reshape(2 * order, 2 * order)  17.5 us
    another operation x15, local copies, waits for them, and re-layouts, finish_modes(): lax.linalg.triangular_solve(lower_factor, stacked_rows, left_side=True, l...  8.21 us
    all_to_all x1, waiting for transfers between devices, local(): lax.all_to_all(stacked, 'tm', split_axis=1, concat_axis=2, tiled=True)  5.87 us
  transfers between devices with their start and end apart: 2, of which 2 were waited for; matrix products, arithmetic and copies ran while one was open for 0% of the time, Pallas kernels for 0%

commit v1 on v0

v1 whole, which is shorter than its diff:
```python
import functools
import math

import jax
import jax.numpy as jnp
from jax import lax
from jax.experimental import pallas as pl
from jax.experimental.pallas import tpu as pltpu
from jax.sharding import PartitionSpec as P

TILE = 8
CHUNK = 16
VMEM_LIMIT = 48 * 1024 * 1024


def whole_vmem(count):
    return [pl.BlockSpec(memory_space=pltpu.VMEM)] * count


def rows_of(shape):
    return lax.broadcasted_iota(jnp.int32, shape, 0)


def lanes_of(shape):
    return lax.broadcasted_iota(jnp.int32, shape, 1)


def project_kernel(groups, freq_ref, offset_ref, snap_ref, *refs):
    outs, (held, sems) = refs[:groups], refs[groups:]
    blocks, length, cells = snap_ref.shape
    chunks = blocks // CHUNK
    copies = []
    for step in range(chunks):
        part = pl.ds(step * CHUNK, CHUNK)
        copies.append(pltpu.make_async_copy(snap_ref.at[part], held.at[part], sems.at[step]))
        copies[-1].start()

    count = freq_ref.shape[0]
    per_group = count // groups
    first = lax.axis_index("tm") * per_group if groups > 1 else 0
    picked = [freq_ref[lax.rem(first + j, count)] for j in range(count)]

    def turned(moments):
        row = rows_of((2 * count, moments.shape[1]))
        freq = jnp.zeros(row.shape, jnp.int32)
        for j in range(count):
            freq = jnp.where((row == j) | (row == j + count), picked[j], freq)
        turns = lax.rem(freq * moments, length)
        turns = jnp.where(row >= count, turns - length // 4, turns)
        return jnp.cos(turns.astype(jnp.float32) * (2.0 * math.pi / length))

    moments = lanes_of((2 * count, length))
    window = 0.5 - 0.5 * jnp.cos(moments.astype(jnp.float32) * (2.0 * math.pi / length))
    table = window * turned(moments)
    tile_row = rows_of((TILE, length))
    table_rows = []
    for j in range(2 * count):
        spread = jnp.broadcast_to(table[j : j + 1, :], (TILE, length))
        table_rows.append(
            jnp.concatenate([jnp.where(tile_row == b, spread, 0.0) for b in range(TILE)], axis=1)
        )
    spread_table = jnp.concatenate(table_rows, axis=0).astype(jnp.bfloat16)
    phases = turned(jnp.broadcast_to(offset_ref[...], (2 * count, blocks))).T

    for step in range(chunks):
        copies[step].wait()
        parts = []
        for half in range(CHUNK // TILE):
            start = step * CHUNK + half * TILE
            data = held[start : start + TILE].reshape(TILE * length, cells)
            projected = jnp.dot(spread_table, data, preferred_element_type=jnp.float32)
            turn = phases[start : start + TILE]
            pairs = []
            for j in range(count):
                cos_part = projected[j * TILE : (j + 1) * TILE]
                sin_part = projected[(count + j) * TILE : (count + j + 1) * TILE]
                cos_phase = turn[:, j : j + 1]
                sin_phase = turn[:, count + j : count + j + 1]
                pairs.append(
                    (
                        cos_part * cos_phase - sin_part * sin_phase,
                        -(sin_part * cos_phase + cos_part * sin_phase),
                    )
                )
            parts.append(pairs)
        for j in range(count):
            for p in range(2):
                value = jnp.concatenate([pairs[j][p] for pairs in parts], axis=0)
                target = outs[j // per_group]
                target[j % per_group, p, step * CHUNK : (step + 1) * CHUNK, :] = value.astype(
                    jnp.bfloat16
                )


def project(snapshots, frequencies, offsets, groups):
    blocks, length, cells = snapshots.shape
    count = frequencies.shape[0]
    shape = jax.ShapeDtypeStruct((count // groups, 2, blocks, cells), jnp.bfloat16)
    return pl.pallas_call(
        functools.partial(project_kernel, groups),
        out_shape=[shape] * groups,
        in_specs=[
            pl.BlockSpec(memory_space=pltpu.SMEM),
            pl.BlockSpec(memory_space=pltpu.VMEM),
            pl.BlockSpec(memory_space=pl.ANY),
        ],
        out_specs=whole_vmem(groups),
        scratch_shapes=[
            pltpu.VMEM(snapshots.shape, snapshots.dtype),
            pltpu.SemaphoreType.DMA((blocks // CHUNK,)),
        ],
        compiler_params=pltpu.CompilerParams(vmem_limit_bytes=VMEM_LIMIT),
        name="project",
    )(frequencies, offsets.reshape(1, blocks), snapshots)


def gram_kernel(halves, scale, *refs):
    pieces = refs[: 2 * halves]
    held_ref, keep_ref, send_ref, other, packed = refs[2 * halves :]
    count = held_ref.shape[0]
    order = held_ref.shape[2]
    first = lax.axis_index("tm") if halves > 1 else 0
    size = order // halves
    for s, target in ((0, held_ref), (1, other)):
        for h in range(halves):
            place = pl.ds(pl.multiple_of(lax.rem(first + h, halves) * size, size), size)
            target[:, :, place, :] = pieces[s * halves + h][...]
    lower = rows_of((order, order)) >= lanes_of((order, order))
    turn = (((1,), (1,)), ((), ()))
    for f in range(count):
        real = jnp.concatenate([held_ref[f, 0], other[f, 0]], axis=1)
        imag = jnp.concatenate([held_ref[f, 1], other[f, 1]], axis=1)
        both = jnp.concatenate([real, imag], axis=1)
        crossed = jnp.concatenate([imag, -real], axis=1)
        gram_real = lax.dot_general(both, both, turn, preferred_element_type=jnp.float32)
        gram_imag = lax.dot_general(crossed, both, turn, preferred_element_type=jnp.float32)
        packed[f] = jnp.where(lower, gram_real, gram_imag) * scale
    bit = lax.rem(lax.axis_index("space"), 2)
    part = count // 2
    keep_ref[...] = packed[pl.ds(bit * part, part)]
    send_ref[...] = packed[pl.ds((1 - bit) * part, part)]


def gram(pieces, halves, scale):
    count, _, size, cells = pieces[0].shape
    order = size * halves
    held = jax.ShapeDtypeStruct((count, 2, order, cells), jnp.bfloat16)
    half = jax.ShapeDtypeStruct((count // 2, order, order), jnp.float32)
    return pl.pallas_call(
        functools.partial(gram_kernel, halves, scale),
        out_shape=[held, half, half],
        in_specs=whole_vmem(len(pieces)),
        out_specs=whole_vmem(3),
        scratch_shapes=[
            pltpu.VMEM(held.shape, held.dtype),
            pltpu.VMEM((count, order, order), jnp.float32),
        ],
        compiler_params=pltpu.CompilerParams(vmem_limit_bytes=VMEM_LIMIT),
        name="gram",
    )(*pieces)


def spread_row(tile, p):
    return jnp.broadcast_to(tile[p : p + 1, :], tile.shape)


def spread_lane(tile, p):
    return jnp.broadcast_to(tile[:, p : p + 1], tile.shape)


def invert_factor(packed, out_ref, slot):
    order = packed.shape[0]
    shape = (TILE, order)
    tiles = order // TILE
    flipped = packed.T
    row, lane = rows_of((order, order)), lanes_of((order, order))
    full_real = jnp.where(row >= lane, packed, flipped)
    full_imag = jnp.where(row < lane, packed, jnp.where(row == lane, 0.0, -flipped))
    real = [full_real[t * TILE : (t + 1) * TILE] for t in range(tiles)]
    imag = [full_imag[t * TILE : (t + 1) * TILE] for t in range(tiles)]
    tile_row, tile_lane = rows_of(shape), lanes_of(shape)
    at_row = [tile_row == p for p in range(TILE)]
    for k in range(tiles):
        base = k * TILE
        inside = (tile_lane >= base) & (tile_lane < base + TILE)
        col_real = [spread_lane(real[k], base + q) for q in range(TILE)]
        col_imag = [spread_lane(imag[k], base + q) for q in range(TILE)]
        here_real = jnp.where(inside, jnp.where(tile_lane == base + tile_row, 1.0, 0.0), real[k])
        here_imag = jnp.where(inside, 0.0, imag[k])
        done_real, done_imag = here_real, here_imag
        for p in range(TILE):
            pivot = spread_row(col_real[p], p)
            inverse = 1.0 / pivot
            root = lax.rsqrt(pivot)
            done_real = jnp.where(at_row[p], here_real * root, done_real)
            done_imag = jnp.where(at_row[p], here_imag * root, done_imag)
            lead_real, lead_imag = col_real[p], col_imag[p]

            def eliminate(a_real, a_imag):
                top_real = spread_row(a_real, p) * inverse
                top_imag = spread_row(a_imag, p) * inverse
                new_real = a_real - (lead_real * top_real - lead_imag * top_imag)
                new_imag = a_imag - (lead_real * top_imag + lead_imag * top_real)
                return (
                    jnp.where(at_row[p], top_real, new_real),
                    jnp.where(at_row[p], top_imag, new_imag),
                )

            for q in range(p + 1, TILE):
                col_real[q], col_imag[q] = eliminate(col_real[q], col_imag[q])
            here_real, here_imag = eliminate(here_real, here_imag)
        keep = tile_lane < base + TILE
        out_ref[slot, 0, base : base + TILE, :] = jnp.where(keep, done_real, 0.0)
        out_ref[slot, 1, base : base + TILE, :] = jnp.where(keep, done_imag, 0.0)
        if k + 1 < tiles:
            rows_real = [spread_row(here_real, p) for p in range(TILE)]
            rows_imag = [spread_row(here_imag, p) for p in range(TILE)]
        for t in range(k + 1, tiles):
            a_real = jnp.where(inside, 0.0, real[t])
            a_imag = jnp.where(inside, 0.0, imag[t])
            for p in range(TILE):
                lead_real = spread_lane(real[t], base + p)
                lead_imag = spread_lane(imag[t], base + p)
                a_real = a_real - lead_real * rows_real[p] + lead_imag * rows_imag[p]
                a_imag = a_imag - lead_real * rows_imag[p] - lead_imag * rows_real[p]
            real[t], imag[t] = a_real, a_imag


def factor_kernel(terms, *refs):
    out_ref = refs[terms]
    total = refs[0][...]
    for r in refs[1:terms]:
        total = total + r[...]
    for slot in range(total.shape[0]):
        invert_factor(total[slot], out_ref, slot)


def factor(terms):
    count, order, _ = terms[0].shape
    return pl.pallas_call(
        functools.partial(factor_kernel, len(terms)),
        out_shape=jax.ShapeDtypeStruct((count, 2, order, order), jnp.float32),
        in_specs=whole_vmem(len(terms)),
        out_specs=pl.BlockSpec(memory_space=pltpu.VMEM),
        compiler_params=pltpu.CompilerParams(vmem_limit_bytes=VMEM_LIMIT),
        name="factor",
    )(*terms)


def apply_kernel(own_ref, sent_ref, held_ref, out_ref):
    part = own_ref.shape[0]
    order = held_ref.shape[2]
    bit = lax.rem(lax.axis_index("space"), 2)
    for which, source in ((bit, own_ref), (1 - bit, sent_ref)):
        for slot in range(part):
            f = which * part + slot
            real, imag = source[slot, 0], source[slot, 1]
            full = jnp.concatenate(
                [
                    jnp.concatenate([real, -imag], axis=1),
                    jnp.concatenate([imag, real], axis=1),
                ],
                axis=0,
            )
            high = full.astype(jnp.bfloat16)
            low = (full - high.astype(jnp.float32)).astype(jnp.bfloat16)
            data = held_ref[f].reshape(2 * order, held_ref.shape[3])
            value = jnp.dot(high, data, preferred_element_type=jnp.float32) + jnp.dot(
                low, data, preferred_element_type=jnp.float32
            )
            out_ref[f] = value.reshape(held_ref.shape[1:])


def apply(own, sent, held):
    return pl.pallas_call(
        apply_kernel,
        out_shape=jax.ShapeDtypeStruct(held.shape, jnp.float32),
        in_specs=whole_vmem(3),
        out_specs=pl.BlockSpec(memory_space=pltpu.VMEM),
        compiler_params=pltpu.CompilerParams(vmem_limit_bytes=VMEM_LIMIT),
        name="apply",
    )(own, sent, held)


def swap(value, size, mask):
    return lax.ppermute(value, "space", [(i, i ^ mask) for i in range(size)])


def swap_both(value, size, mask):
    pairs = [(t * size + i, (1 - t) * size + (i ^ mask)) for t in range(2) for i in range(size)]
    return lax.ppermute(value, ("tm", "space"), pairs)


def local(snapshots, frequencies, offsets):
    halves = lax.axis_size("tm")
    size = lax.axis_size("space")
    scale = 1.0 / (snapshots.shape[2] * size)
    if halves == 2:
        mine, theirs = project(snapshots, frequencies, offsets, 2)
        pieces = [
            mine,
            swap_both(theirs, size, 0),
            swap(mine, size, 2),
            swap_both(theirs, size, 2),
        ]
        held, keep, send = gram(pieces, 2, scale)
    else:
        (coeffs,) = project(snapshots, frequencies, offsets, 1)
        regrouped = lax.all_to_all(coeffs, "tm", split_axis=0, concat_axis=2, tiled=True)
        held, keep, send = gram([regrouped, swap(regrouped, size, 2)], 1, scale)
    total = keep + swap(send, size, 1)
    terms = [total]
    bit = 4
    while bit < size:
        total = functools.reduce(jnp.add, terms)
        masks = [bit, 2 * bit, 3 * bit] if 2 * bit < size else [bit]
        terms = [total] + [swap(total, size, mask) for mask in masks]
        bit *= 4
    own = factor(terms)
    return apply(own, swap(own, size, 1), held)


def solution(mesh):
    placed = (P("tm", None, "space"), P(), P("tm"))
    return jax.shard_map(
        local, mesh=mesh, in_specs=placed, out_specs=P("tm", None, None, "space"), check_vma=False
    )
```

time: 291 us -> 37.1 us (0.13)
  other arithmetic: 115 us -> 0.01 us
  waiting for transfers between devices: 94.5 us -> 15.1 us
  local copies, waits for them, and re-layouts: 53.6 us -> 3.5 us
  between operations: 16.5 us -> 0.04 us
  Pallas kernels: 0 us -> 9.17 us
  matrix products: 6.52 us -> 0 us
  starting transfers between devices: 4.24 us -> 9.14 us
    another operation x33 -> x0, other arithmetic: 112 us -> none  [the longest x14 69.3 us: finish_modes(): lower_factor = jnp.linalg.cholesky(embedded)]
    psum x1 -> x0, waiting for transfers between devices: 88.6 us -> none  [local(): summed = lax.psum(local_grams, 'space')]
    another operation x23 -> x0, local copies, waits for them, and re-layouts: 26.5 us -> none  [the longest x2 17.5 us: embed_gram(): return jnp.stack([top_rows, low_rows], axis=1).reshape(2 * order, 2 * order)]
    reshape x8 -> x0, local copies, waits for them, and re-layouts: 26 us -> none  [the longest x4 25.6 us: embed_gram(): return jnp.stack([top_rows, low_rows], axis=1).reshape(2 * order, 2 * order)]
    ppermute x0 -> x8, waiting for transfers between devices: none -> 15.1 us  [the longest x6 10 us: swap(): return lax.ppermute(value, 'space', [(i, i ^ mask) for i in range(size)])]
    pallas_call x0 -> x4, Pallas kernels: none -> 9.17 us  [the longest x1 5.3 us: factor(): pl.pallas_call(functools.partial(factor_kernel, len(terms)), out_shape=ja...]
    ppermute x0 -> x8, starting transfers between devices: none -> 9.14 us  [the longest x6 7.6 us: swap(): return lax.ppermute(value, 'space', [(i, i ^ mask) for i in range(size)])]
    all_to_all x1 -> x0, waiting for transfers between devices: 5.87 us -> none  [local(): lax.all_to_all(stacked, 'tm', split_axis=1, concat_axis=2, tiled=True)]
  transfers between devices with their start and end apart: 2 -> 8, of which waited for: 2 -> 7; matrix products, arithmetic and copies ran while one was open for 0% -> 0% of each run, Pallas kernels for 0% -> 0%
where the time goes in v1:
time: 37.1 us; the launch traced here: 37 us
  waiting for transfers between devices  15.1 us (41%)
  Pallas kernels  9.17 us (25%)
  starting transfers between devices  9.14 us (25%)
  local copies, waits for them, and re-layouts  3.5 us (9%)
    ppermute x6, waiting for transfers between devices, swap(): return lax.ppermute(value, 'space', [(i, i ^ mask) for i in range(size)])  10 us
    ppermute x6, starting transfers between devices, swap(): return lax.ppermute(value, 'space', [(i, i ^ mask) for i in range(size)])  7.6 us
    pallas_call x1, Pallas kernels, factor(): pl.pallas_call(functools.partial(factor_kernel, len(terms)), out_shape=ja...  5.3 us
    ppermute x2, waiting for transfers between devices, swap_both(): return lax.ppermute(value, ('tm', 'space'), pairs)  5.07 us
    unnamed x6, local copies, waits for them, and re-layouts  3.5 us
    pallas_call x1, Pallas kernels, project(): pl.pallas_call(functools.partial(project_kernel, groups), out_shape=[shap...  2.26 us
    ppermute x2, starting transfers between devices, swap_both(): return lax.ppermute(value, ('tm', 'space'), pairs)  1.54 us
    pallas_call x1, Pallas kernels, apply(): pl.pallas_call(apply_kernel, out_shape=jax.ShapeDtypeStruct(held.shape, j...  1.11 us
  transfers between devices with their start and end apart: 8, of which 7 were waited for; matrix products, arithmetic and copies ran while one was open for 0% of the time, Pallas kernels for 0%

profile of v1, /device:TPU:0, one launch (start us, length us, event | category | flops | bytes accessed | tf_op | source)
XLA Modules:
  0.0 37.0 jit_solution(11640553718537811146)
XLA Ops:
  0.0 0.0 copy-start
  0.0 2.2 %copy-done = bf16[64,128,256]{2,1,0:T(8,128)(2,1)S(1)} copy-done((bf16[64,128,256]{2,1,0:T(8,128)(2,1)S(1)}, bf16[64,128,256]{2,1,0:T(8,128)(2,1)}, u32[]{:S(2)}) %copy-start) | copy-done | bytes 4194328
  2.2 0.0 copy-start.1
  2.2 0.7 %copy-done.1 = s32[4]{0:T(128)S(1)} copy-done((s32[4]{0:T(128)S(1)}, s32[4]{0:T(128)}, u32[]{:S(2)}) %copy-start.1) | copy-done | bytes 40
  2.8 0.0 copy-start.2
  2.8 0.7 %copy-done.2 = s32[64]{0:T(128)S(1)} copy-done((s32[64]{0:T(128)S(1)}, s32[64]{0:T(128)}, u32[]{:S(2)}) %copy-start.2) | copy-done | bytes 280
  3.5 2.3 %project.1 = (bf16[2,2,64,256]{3,2,1,0:T(8,128)(2,1)S(1)}, bf16[2,2,64,256]{3,2,1,0:T(8,128)(2,1)S(1)}) custom-call(s32[4]{0:T(128)S(1)} %copy-done.1, s32[1,64]{1,0:T(1,128)S(1)} %bitcast.1, bf16[64,128,256]{2,1,0:T(8,128)(2,1)S(1)} %copy-done), custom_call_target="tpu_custom_call" | custom-call | tf_op jit(solution)/shard_map/project/pallas_call | solution.py:99
  5.8 3.0 %collective-permute-start.1 = (bf16[2,2,64,256]{3,2,1,0:T(8,128)(2,1)S(1)}, bf16[2,2,64,256]{3,2,1,0:T(8,128)(2,1)S(1)}, u32[]{:S(2)}, u32[]{:S(2)}) collective-permute-start(bf16[2,2,64,256]{3,2,1,0:T(8,128)(2,1)S(1)} %get-tuple-element.10.refs_0_), channel_id=1, source_target_pairs={{0,2},{1,3},{2,0},{3,1},{4,6},{5,7},{6,4},{7,5},{8,10},{9,11},{10,... | collective-permute-start | bytes 393224 | tf_op jit(solution)/shard_map/ppermute | solution.py:286
  8.8 1.5 %collective-permute-start.2 = (bf16[2,2,64,256]{3,2,1,0:T(8,128)(2,1)S(1)}, bf16[2,2,64,256]{3,2,1,0:T(8,128)(2,1)S(1)}, u32[]{:S(2)}, u32[]{:S(2)}) collective-permute-start(bf16[2,2,64,256]{3,2,1,0:T(8,128)(2,1)S(1)} %get-tuple-element.11), channel_id=1, source_target_pairs={{0,18},{1,19},{2,16},{3,17},{4,22},{5,23},{6,20},{7,21},{8,26},{9,... | collective-permute-start | bytes 393224 | tf_op jit(solution)/shard_map/ppermute | solution.py:291
  10.3 0.1 collective-permute-start
  10.3 2.4 %collective-permute-done.1.refs_2_ = bf16[2,2,64,256]{3,2,1,0:T(8,128)(2,1)S(1)} collective-permute-done((bf16[2,2,64,256]{3,2,1,0:T(8,128)(2,1)S(1)}, bf16[2,2,64,256]{3,2,1,0:T(8,128)(2,1)S(1)}, u32[]{:S(2)}, u32[]{:S(2)}) %collective-permute-start.1) | collective-permute-done | bytes 131104 | tf_op jit(solution)/shard_map/ppermute | solution.py:286
  12.7 3.7 %collective-permute-done.2.refs_3_ = bf16[2,2,64,256]{3,2,1,0:T(8,128)(2,1)S(1)} collective-permute-done((bf16[2,2,64,256]{3,2,1,0:T(8,128)(2,1)S(1)}, bf16[2,2,64,256]{3,2,1,0:T(8,128)(2,1)S(1)}, u32[]{:S(2)}, u32[]{:S(2)}) %collective-permute-start.2) | collective-permute-done | bytes 131104 | tf_op jit(solution)/shard_map/ppermute | solution.py:291
  16.4 1.4 %collective-permute-done.refs_1_ = bf16[2,2,64,256]{3,2,1,0:T(8,128)(2,1)S(1)} collective-permute-done((bf16[2,2,64,256]{3,2,1,0:T(8,128)(2,1)S(1)}, bf16[2,2,64,256]{3,2,1,0:T(8,128)(2,1)S(1)}, u32[]{:S(2)}, u32[]{:S(2)}) %collective-permute-start) | collective-permute-done | bytes 131104 | tf_op jit(solution)/shard_map/ppermute | solution.py:291
  17.7 0.5 %gram.1 = (bf16[2,2,128,256]{3,2,1,0:T(8,128)(2,1)S(1)}, f32[1,128,128]{2,1,0:T(8,128)S(1)}, f32[1,128,128]{2,1,0:T(8,128)S(1)}) custom-call(bf16[2,2,64,256]{3,2,1,0:T(8,128)(2,1)S(1)} %get-tuple-element.10.refs_0_, bf16[2,2,64,256]{3,2,1,0:T(8,128)(2,1)S(1)} %collective-permute-done.refs_1_, bf16[2,2,64,256]{3,2,1,0:T(8,128)(2,1)S(1)} %collective-permute-done.1.refs_2_, ...), custom_call_target="tpu_custom_call" | custom-call | tf_op jit(solution)/shard_map/gram/pallas_call | solution.py:149
  18.3 0.1 collective-permute-start.3
  18.3 1.2 %collective-permute-done.3 = f32[1,128,128]{2,1,0:T(8,128)S(1)} collective-permute-done((f32[1,128,128]{2,1,0:T(8,128)S(1)}, f32[1,128,128]{2,1,0:T(8,128)S(1)}, u32[]{:S(2)}, u32[]{:S(2)}) %collective-permute-start.3) | collective-permute-done | bytes 65568 | tf_op jit(solution)/shard_map/ppermute | solution.py:286
  19.6 3.7 %collective-permute-start.6 = (f32[1,128,128]{2,1,0:T(8,128)S(1)}, f32[1,128,128]{2,1,0:T(8,128)S(1)}, u32[]{:S(2)}, u32[]{:S(2)}) collective-permute-start(f32[1,128,128]{2,1,0:T(8,128)S(1)} %add.3.refs_0_), channel_id=1, source_target_pairs={{0,12},{1,13},{2,14},{3,15},{4,8},{5,9},{6,10},{7,11},{8,4},{9,5},... | collective-permute-start | bytes 196616 | tf_op jit(solution)/shard_map/ppermute | solution.py:286
  23.3 0.0 collective-permute-start.5
  23.3 0.8 %collective-permute-start.4 = (f32[1,128,128]{2,1,0:T(8,128)S(1)}, f32[1,128,128]{2,1,0:T(8,128)S(1)}, u32[]{:S(2)}, u32[]{:S(2)}) collective-permute-start(f32[1,128,128]{2,1,0:T(8,128)S(1)} %add.3.refs_0_), channel_id=1, source_target_pairs={{0,4},{1,5},{2,6},{3,7},{4,0},{5,1},{6,2},{7,3},{8,12},{9,13},{10,... | collective-permute-start | bytes 196616 | tf_op jit(solution)/shard_map/ppermute | solution.py:286
  24.0 1.9 %collective-permute-done.6.refs_3_ = f32[1,128,128]{2,1,0:T(8,128)S(1)} collective-permute-done((f32[1,128,128]{2,1,0:T(8,128)S(1)}, f32[1,128,128]{2,1,0:T(8,128)S(1)}, u32[]{:S(2)}, u32[]{:S(2)}) %collective-permute-start.6) | collective-permute-done | bytes 65568 | tf_op jit(solution)/shard_map/ppermute | solution.py:286
  25.9 3.2 %collective-permute-done.5.refs_2_ = f32[1,128,128]{2,1,0:T(8,128)S(1)} collective-permute-done((f32[1,128,128]{2,1,0:T(8,128)S(1)}, f32[1,128,128]{2,1,0:T(8,128)S(1)}, u32[]{:S(2)}, u32[]{:S(2)}) %collective-permute-start.5) | collective-permute-done | bytes 65568 | tf_op jit(solution)/shard_map/ppermute | solution.py:286
  29.1 0.0 collective-permute-done.4.refs_1_
  29.1 5.3 %factor.1.own_ref = f32[1,2,128,128]{3,2,1,0:T(8,128)S(1)} custom-call(f32[1,128,128]{2,1,0:T(8,128)S(1)} %add.3.refs_0_, f32[1,128,128]{2,1,0:T(8,128)S(1)} %collective-permute-done.4.refs_1_, f32[1,128,128]{2,1,0:T(8,128)S(1)} %collective-permute-done.5.refs_2_, f32[1,128,128]{2,1,0:T(8,128)S(1)} %collective-permute-done.6.refs_3_), custom_call_target="tpu_custom_call" | custom-call | tf_op jit(solution)/shard_map/factor/pallas_call | solution.py:240
  34.4 0.1 collective-permute-start.7
  34.5 1.3 %collective-permute-done.7.sent_ref = f32[1,2,128,128]{3,2,1,0:T(8,128)S(1)} collective-permute-done((f32[1,2,128,128]{3,2,1,0:T(8,128)S(1)}, f32[1,2,128,128]{3,2,1,0:T(8,128)S(1)}, u32[]{:S(2)}, u32[]{:S(2)}) %collective-permute-start.7) | collective-permute-done | bytes 131104 | tf_op jit(solution)/shard_map/ppermute | solution.py:286
  35.9 1.1 %apply.1 = f32[2,2,128,256]{3,2,1,0:T(8,128)} custom-call(f32[1,2,128,128]{3,2,1,0:T(8,128)S(1)} %factor.1.own_ref, f32[1,2,128,128]{3,2,1,0:T(8,128)S(1)} %collective-permute-done.7.sent_ref, bf16[2,2,128,256]{3,2,1,0:T(8,128)(2,1)S(1)} %get-tuple-element.14.held_ref), custom_call_target="tpu_custom_call" | custom-call | tf_op jit(solution)/shard_map/apply/pallas_call | solution.py:275
  (1 shorter events, 0.0 us)
Async XLA Ops:
  0.0 2.2 %copy-start = (bf16[64,128,256]{2,1,0:T(8,128)(2,1)S(1)}, bf16[64,128,256]{2,1,0:T(8,128)(2,1)}, u32[]{:S(2)}) copy-start(bf16[64,128,256]{2,1,0:T(8,128)(2,1)} %snap_ref.1) | copy-start | bytes 12582916
  2.2 0.7 %copy-start.1 = (s32[4]{0:T(128)S(1)}, s32[4]{0:T(128)}, u32[]{:S(2)}) copy-start(s32[4]{0:T(128)} %freq_ref.1) | copy-start | bytes 52
  2.8 0.7 %copy-start.2 = (s32[64]{0:T(128)S(1)}, s32[64]{0:T(128)}, u32[]{:S(2)}) copy-start(s32[64]{0:T(128)} %param.5) | copy-start | bytes 772
  5.8 6.9 %collective-permute-start.1 = (bf16[2,2,64,256]{3,2,1,0:T(8,128)(2,1)S(1)}, bf16[2,2,64,256]{3,2,1,0:T(8,128)(2,1)S(1)}, u32[]{:S(2)}, u32[]{:S(2)}) collective-permute-start(bf16[2,2,64,256]{3,2,1,0:T(8,128)(2,1)S(1)} %get-tuple-element.10.refs_0_), channel_id=1, source_target_pairs={{0,2},{1,3},{2,0},{3,1},{4,6},{5,7},{6,4},{7,5},{8,10},{9,11},{10,... | collective-permute-start | bytes 393224 | tf_op jit(solution)/shard_map/ppermute | solution.py:286
  8.8 7.6 %collective-permute-start.2 = (bf16[2,2,64,256]{3,2,1,0:T(8,128)(2,1)S(1)}, bf16[2,2,64,256]{3,2,1,0:T(8,128)(2,1)S(1)}, u32[]{:S(2)}, u32[]{:S(2)}) collective-permute-start(bf16[2,2,64,256]{3,2,1,0:T(8,128)(2,1)S(1)} %get-tuple-element.11), channel_id=1, source_target_pairs={{0,18},{1,19},{2,16},{3,17},{4,22},{5,23},{6,20},{7,21},{8,26},{9,... | collective-permute-start | bytes 393224 | tf_op jit(solution)/shard_map/ppermute | solution.py:291
  10.3 7.5 %collective-permute-start = (bf16[2,2,64,256]{3,2,1,0:T(8,128)(2,1)S(1)}, bf16[2,2,64,256]{3,2,1,0:T(8,128)(2,1)S(1)}, u32[]{:S(2)}, u32[]{:S(2)}) collective-permute-start(bf16[2,2,64,256]{3,2,1,0:T(8,128)(2,1)S(1)} %get-tuple-element.11), channel_id=1, source_target_pairs={{0,16},{1,17},{2,18},{3,19},{4,20},{5,21},{6,22},{7,23},{8,24},{9,... | collective-permute-start | bytes 393224 | tf_op jit(solution)/shard_map/ppermute | solution.py:291
  18.3 1.3 %collective-permute-start.3 = (f32[1,128,128]{2,1,0:T(8,128)S(1)}, f32[1,128,128]{2,1,0:T(8,128)S(1)}, u32[]{:S(2)}, u32[]{:S(2)}) collective-permute-start(f32[1,128,128]{2,1,0:T(8,128)S(1)} %get-tuple-element.13), channel_id=1, source_target_pairs={{0,1},{1,0},{2,3},{3,2},{4,5},{5,4},{6,7},{7,6},{8,9},{9,8},{10,11... | collective-permute-start | bytes 196616 | tf_op jit(solution)/shard_map/ppermute | solution.py:286
  19.6 6.4 %collective-permute-start.6 = (f32[1,128,128]{2,1,0:T(8,128)S(1)}, f32[1,128,128]{2,1,0:T(8,128)S(1)}, u32[]{:S(2)}, u32[]{:S(2)}) collective-permute-start(f32[1,128,128]{2,1,0:T(8,128)S(1)} %add.3.refs_0_), channel_id=1, source_target_pairs={{0,12},{1,13},{2,14},{3,15},{4,8},{5,9},{6,10},{7,11},{8,4},{9,5},... | collective-permute-start | bytes 196616 | tf_op jit(solution)/shard_map/ppermute | solution.py:286
  23.3 5.9 %collective-permute-start.5 = (f32[1,128,128]{2,1,0:T(8,128)S(1)}, f32[1,128,128]{2,1,0:T(8,128)S(1)}, u32[]{:S(2)}, u32[]{:S(2)}) collective-permute-start(f32[1,128,128]{2,1,0:T(8,128)S(1)} %add.3.refs_0_), channel_id=1, source_target_pairs={{0,8},{1,9},{2,10},{3,11},{4,12},{5,13},{6,14},{7,15},{8,0},{9,1},... | collective-permute-start | bytes 196616 | tf_op jit(solution)/shard_map/ppermute | solution.py:286
  23.3 5.9 %collective-permute-start.4 = (f32[1,128,128]{2,1,0:T(8,128)S(1)}, f32[1,128,128]{2,1,0:T(8,128)S(1)}, u32[]{:S(2)}, u32[]{:S(2)}) collective-permute-start(f32[1,128,128]{2,1,0:T(8,128)S(1)} %add.3.refs_0_), channel_id=1, source_target_pairs={{0,4},{1,5},{2,6},{3,7},{4,0},{5,1},{6,2},{7,3},{8,12},{9,13},{10,... | collective-permute-start | bytes 196616 | tf_op jit(solution)/shard_map/ppermute | solution.py:286
  34.4 1.4 %collective-permute-start.7 = (f32[1,2,128,128]{3,2,1,0:T(8,128)S(1)}, f32[1,2,128,128]{3,2,1,0:T(8,128)S(1)}, u32[]{:S(2)}, u32[]{:S(2)}) collective-permute-start(f32[1,2,128,128]{3,2,1,0:T(8,128)S(1)} %factor.1.own_ref), channel_id=1, source_target_pairs={{0,1},{1,0},{2,3},{3,2},{4,5},{5,4},{6,7},{7,6},{8,9},{9,8},{10,11... | collective-permute-start | bytes 393224 | tf_op jit(solution)/shard_map/ppermute | solution.py:286

commit v2 on v1

--- a/solution.py
+++ b/solution.py
@@ -11,6 +11,7 @@
 TILE = 8
 CHUNK = 16
 VMEM_LIMIT = 48 * 1024 * 1024
+PROJECT_VMEM_LIMIT = 60 * 1024 * 1024
 
 
 def whole_vmem(count):
@@ -25,16 +26,24 @@
     return lax.broadcasted_iota(jnp.int32, shape, 1)
 
 
-def project_kernel(groups, freq_ref, offset_ref, snap_ref, *refs):
-    outs, (held, sems) = refs[:groups], refs[groups:]
+def project_kernel(groups, freq_in, offset_in, snap_ref, *refs):
+    outs, (freq_ref, offset_ref, held, sems) = refs[:groups], refs[groups:]
     blocks, length, cells = snap_ref.shape
-    chunks = blocks // CHUNK
+    chunks = blocks // TILE
+    small = [
+        pltpu.make_async_copy(freq_in, freq_ref, sems.at[chunks]),
+        pltpu.make_async_copy(offset_in, offset_ref, sems.at[chunks + 1]),
+    ]
+    for copy in small:
+        copy.start()
     copies = []
     for step in range(chunks):
-        part = pl.ds(step * CHUNK, CHUNK)
+        part = pl.ds(step * TILE, TILE)
         copies.append(pltpu.make_async_copy(snap_ref.at[part], held.at[part], sems.at[step]))
         copies[-1].start()
 
+    for copy in small:
+        copy.wait()
     count = freq_ref.shape[0]
     per_group = count // groups
     first = lax.axis_index("tm") * per_group if groups > 1 else 0
@@ -62,10 +71,10 @@
     spread_table = jnp.concatenate(table_rows, axis=0).astype(jnp.bfloat16)
     phases = turned(jnp.broadcast_to(offset_ref[...], (2 * count, blocks))).T
 
-    for step in range(chunks):
-        copies[step].wait()
+    for step in range(blocks // CHUNK):
         parts = []
         for half in range(CHUNK // TILE):
+            copies[step * (CHUNK // TILE) + half].wait()
             start = step * CHUNK + half * TILE
             data = held[start : start + TILE].reshape(TILE * length, cells)
             projected = jnp.dot(spread_table, data, preferred_element_type=jnp.float32)
@@ -99,17 +108,15 @@
     return pl.pallas_call(
         functools.partial(project_kernel, groups),
         out_shape=[shape] * groups,
-        in_specs=[
-            pl.BlockSpec(memory_space=pltpu.SMEM),
-            pl.BlockSpec(memory_space=pltpu.VMEM),
-            pl.BlockSpec(memory_space=pl.ANY),
-        ],
+        in_specs=[pl.BlockSpec(memory_space=pltpu.HBM)] * 3,
         out_specs=whole_vmem(groups),
         scratch_shapes=[
+            pltpu.SMEM((count,), jnp.int32),
+            pltpu.VMEM((1, blocks), jnp.int32),
             pltpu.VMEM(snapshots.shape, snapshots.dtype),
-            pltpu.SemaphoreType.DMA((blocks // CHUNK,)),
+            pltpu.SemaphoreType.DMA((blocks // TILE + 2,)),
         ],
-        compiler_params=pltpu.CompilerParams(vmem_limit_bytes=VMEM_LIMIT),
+        compiler_params=pltpu.CompilerParams(vmem_limit_bytes=PROJECT_VMEM_LIMIT),
         name="project",
     )(frequencies, offsets.reshape(1, blocks), snapshots)
 

time: 37.1 us -> 36.5 us (0.984)
  local copies, waits for them, and re-layouts: 3.5 us -> 0.9 us
  Pallas kernels: 9.17 us -> 11 us
    unnamed x6 -> x2, local copies, waits for them, and re-layouts: 3.5 us -> 0.9 us
    pallas_call x1, Pallas kernels: 2.26 us -> 4.06 us  [project(): pl.pallas_call(functools.partial(project_kernel, groups), out_shape=[shap...]
where the time goes in v2:
time: 36.5 us; the launch traced here: 36.4 us
  waiting for transfers between devices  15.3 us (42%)
  Pallas kernels  11 us (30%)
  starting transfers between devices  9.13 us (25%)
  local copies, waits for them, and re-layouts  0.9 us (2%)
    ppermute x6, waiting for transfers between devices, swap(): return lax.ppermute(value, 'space', [(i, i ^ mask) for i in range(size)])  10.4 us
    ppermute x6, starting transfers between devices, swap(): return lax.ppermute(value, 'space', [(i, i ^ mask) for i in range(size)])  7.59 us
    pallas_call x1, Pallas kernels, factor(): pl.pallas_call(functools.partial(factor_kernel, len(terms)), out_shape=ja...  5.3 us
    ppermute x2, waiting for transfers between devices, swap_both(): return lax.ppermute(value, ('tm', 'space'), pairs)  4.97 us
    pallas_call x1, Pallas kernels, project(): pl.pallas_call(functools.partial(project_kernel, groups), out_shape=[shap...  4.06 us
    ppermute x2, starting transfers between devices, swap_both(): return lax.ppermute(value, ('tm', 'space'), pairs)  1.54 us
    pallas_call x1, Pallas kernels, apply(): pl.pallas_call(apply_kernel, out_shape=jax.ShapeDtypeStruct(held.shape, j...  1.11 us
    unnamed x2, local copies, waits for them, and re-layouts  0.9 us
  transfers between devices with their start and end apart: 8, of which 7 were waited for; matrix products, arithmetic and copies ran while one was open for 0% of the time, Pallas kernels for 0%

profile of v2, /device:TPU:0, one launch (start us, length us, event | category | flops | bytes accessed | tf_op | source)
XLA Modules:
  0.0 36.4 jit_solution(17463464904785691785)
XLA Ops:
  0.0 4.1 %project.1 = (bf16[2,2,64,256]{3,2,1,0:T(8,128)(2,1)}, bf16[2,2,64,256]{3,2,1,0:T(8,128)(2,1)}) custom-call(s32[4]{0:T(128)} %freq_in.1, s32[1,64]{1,0:T(1,128)} %bitcast.1, bf16[64,128,256]{2,1,0:T(8,128)(2,1)} %snap_ref.1), custom_call_target="tpu_custom_call" | custom-call | tf_op jit(solution)/shard_map/project/pallas_call | solution.py:108
  4.1 3.0 %collective-permute-start.1 = (bf16[2,2,64,256]{3,2,1,0:T(8,128)(2,1)}, bf16[2,2,64,256]{3,2,1,0:T(8,128)(2,1)S(1)}, u32[]{:S(2)}, u32[]{:S(2)}) collective-permute-start(bf16[2,2,64,256]{3,2,1,0:T(8,128)(2,1)} %get-tuple-element.10.refs_0_), channel_id=1, source_target_pairs={{0,2},{1,3},{2,0},{3,1},{4,6},{5,7},{6,4},{7,5},{8,10},{9,11},{10,... | collective-permute-start | bytes 393224 | tf_op jit(solution)/shard_map/ppermute | solution.py:293
  7.1 1.5 %collective-permute-start.2 = (bf16[2,2,64,256]{3,2,1,0:T(8,128)(2,1)}, bf16[2,2,64,256]{3,2,1,0:T(8,128)(2,1)S(1)}, u32[]{:S(2)}, u32[]{:S(2)}) collective-permute-start(bf16[2,2,64,256]{3,2,1,0:T(8,128)(2,1)} %get-tuple-element.11), channel_id=1, source_target_pairs={{0,18},{1,19},{2,16},{3,17},{4,22},{5,23},{6,20},{7,21},{8,26},{9,... | collective-permute-start | bytes 393224 | tf_op jit(solution)/shard_map/ppermute | solution.py:298
  8.6 0.1 collective-permute-start
  8.6 2.7 %collective-permute-done.1.refs_2_ = bf16[2,2,64,256]{3,2,1,0:T(8,128)(2,1)S(1)} collective-permute-done((bf16[2,2,64,256]{3,2,1,0:T(8,128)(2,1)}, bf16[2,2,64,256]{3,2,1,0:T(8,128)(2,1)S(1)}, u32[]{:S(2)}, u32[]{:S(2)}) %collective-permute-start.1) | collective-permute-done | bytes 131104 | tf_op jit(solution)/shard_map/ppermute | solution.py:293
  11.3 3.6 %collective-permute-done.2.refs_3_ = bf16[2,2,64,256]{3,2,1,0:T(8,128)(2,1)S(1)} collective-permute-done((bf16[2,2,64,256]{3,2,1,0:T(8,128)(2,1)}, bf16[2,2,64,256]{3,2,1,0:T(8,128)(2,1)S(1)}, u32[]{:S(2)}, u32[]{:S(2)}) %collective-permute-start.2) | collective-permute-done | bytes 131104 | tf_op jit(solution)/shard_map/ppermute | solution.py:298
  14.9 1.4 %collective-permute-done.refs_1_ = bf16[2,2,64,256]{3,2,1,0:T(8,128)(2,1)S(1)} collective-permute-done((bf16[2,2,64,256]{3,2,1,0:T(8,128)(2,1)}, bf16[2,2,64,256]{3,2,1,0:T(8,128)(2,1)S(1)}, u32[]{:S(2)}, u32[]{:S(2)}) %collective-permute-start) | collective-permute-done | bytes 131104 | tf_op jit(solution)/shard_map/ppermute | solution.py:298
  16.3 0.0 copy-start
  16.3 0.9 %copy-done = bf16[2,2,64,256]{3,2,1,0:T(8,128)(2,1)S(1)} copy-done((bf16[2,2,64,256]{3,2,1,0:T(8,128)(2,1)S(1)}, bf16[2,2,64,256]{3,2,1,0:T(8,128)(2,1)}, u32[]{:S(2)}) %copy-start) | copy-done | bytes 131096
  17.2 0.5 %gram.1 = (bf16[2,2,128,256]{3,2,1,0:T(8,128)(2,1)S(1)}, f32[1,128,128]{2,1,0:T(8,128)S(1)}, f32[1,128,128]{2,1,0:T(8,128)S(1)}) custom-call(bf16[2,2,64,256]{3,2,1,0:T(8,128)(2,1)S(1)} %copy-done, bf16[2,2,64,256]{3,2,1,0:T(8,128)(2,1)S(1)} %collective-permute-done.refs_1_, bf16[2,2,64,256]{3,2,1,0:T(8,128)(2,1)S(1)} %collective-permute-done.1.refs_2_, ...), custom_call_target="tpu_custom_call" | custom-call | tf_op jit(solution)/shard_map/gram/pallas_call | solution.py:156
  17.7 0.1 collective-permute-start.3
  17.8 1.2 %collective-permute-done.3 = f32[1,128,128]{2,1,0:T(8,128)S(1)} collective-permute-done((f32[1,128,128]{2,1,0:T(8,128)S(1)}, f32[1,128,128]{2,1,0:T(8,128)S(1)}, u32[]{:S(2)}, u32[]{:S(2)}) %collective-permute-start.3) | collective-permute-done | bytes 65568 | tf_op jit(solution)/shard_map/ppermute | solution.py:293
  19.0 3.7 %collective-permute-start.6 = (f32[1,128,128]{2,1,0:T(8,128)S(1)}, f32[1,128,128]{2,1,0:T(8,128)S(1)}, u32[]{:S(2)}, u32[]{:S(2)}) collective-permute-start(f32[1,128,128]{2,1,0:T(8,128)S(1)} %add.3.refs_0_), channel_id=1, source_target_pairs={{0,12},{1,13},{2,14},{3,15},{4,8},{5,9},{6,10},{7,11},{8,4},{9,5},... | collective-permute-start | bytes 196616 | tf_op jit(solution)/shard_map/ppermute | solution.py:293
  22.7 0.0 collective-permute-start.5
  22.7 0.8 %collective-permute-start.4 = (f32[1,128,128]{2,1,0:T(8,128)S(1)}, f32[1,128,128]{2,1,0:T(8,128)S(1)}, u32[]{:S(2)}, u32[]{:S(2)}) collective-permute-start(f32[1,128,128]{2,1,0:T(8,128)S(1)} %add.3.refs_0_), channel_id=1, source_target_pairs={{0,4},{1,5},{2,6},{3,7},{4,0},{5,1},{6,2},{7,3},{8,12},{9,13},{10,... | collective-permute-start | bytes 196616 | tf_op jit(solution)/shard_map/ppermute | solution.py:293
  23.5 1.9 %collective-permute-done.6.refs_3_ = f32[1,128,128]{2,1,0:T(8,128)S(1)} collective-permute-done((f32[1,128,128]{2,1,0:T(8,128)S(1)}, f32[1,128,128]{2,1,0:T(8,128)S(1)}, u32[]{:S(2)}, u32[]{:S(2)}) %collective-permute-start.6) | collective-permute-done | bytes 65568 | tf_op jit(solution)/shard_map/ppermute | solution.py:293
  25.3 3.2 %collective-permute-done.5.refs_2_ = f32[1,128,128]{2,1,0:T(8,128)S(1)} collective-permute-done((f32[1,128,128]{2,1,0:T(8,128)S(1)}, f32[1,128,128]{2,1,0:T(8,128)S(1)}, u32[]{:S(2)}, u32[]{:S(2)}) %collective-permute-start.5) | collective-permute-done | bytes 65568 | tf_op jit(solution)/shard_map/ppermute | solution.py:293
  28.6 0.0 collective-permute-done.4.refs_1_
  28.6 5.3 %factor.1.own_ref = f32[1,2,128,128]{3,2,1,0:T(8,128)S(1)} custom-call(f32[1,128,128]{2,1,0:T(8,128)S(1)} %add.3.refs_0_, f32[1,128,128]{2,1,0:T(8,128)S(1)} %collective-permute-done.4.refs_1_, f32[1,128,128]{2,1,0:T(8,128)S(1)} %collective-permute-done.5.refs_2_, f32[1,128,128]{2,1,0:T(8,128)S(1)} %collective-permute-done.6.refs_3_), custom_call_target="tpu_custom_call" | custom-call | tf_op jit(solution)/shard_map/factor/pallas_call | solution.py:247
  33.9 0.1 collective-permute-start.7
  34.0 1.3 %collective-permute-done.7.sent_ref = f32[1,2,128,128]{3,2,1,0:T(8,128)S(1)} collective-permute-done((f32[1,2,128,128]{3,2,1,0:T(8,128)S(1)}, f32[1,2,128,128]{3,2,1,0:T(8,128)S(1)}, u32[]{:S(2)}, u32[]{:S(2)}) %collective-permute-start.7) | collective-permute-done | bytes 131104 | tf_op jit(solution)/shard_map/ppermute | solution.py:293
  35.3 1.1 %apply.1 = f32[2,2,128,256]{3,2,1,0:T(8,128)} custom-call(f32[1,2,128,128]{3,2,1,0:T(8,128)S(1)} %factor.1.own_ref, f32[1,2,128,128]{3,2,1,0:T(8,128)S(1)} %collective-permute-done.7.sent_ref, bf16[2,2,128,256]{3,2,1,0:T(8,128)(2,1)S(1)} %get-tuple-element.14.held_ref), custom_call_target="tpu_custom_call" | custom-call | tf_op jit(solution)/shard_map/apply/pallas_call | solution.py:282
  (1 shorter events, 0.0 us)
Async XLA Ops:
  4.1 7.2 %collective-permute-start.1 = (bf16[2,2,64,256]{3,2,1,0:T(8,128)(2,1)}, bf16[2,2,64,256]{3,2,1,0:T(8,128)(2,1)S(1)}, u32[]{:S(2)}, u32[]{:S(2)}) collective-permute-start(bf16[2,2,64,256]{3,2,1,0:T(8,128)(2,1)} %get-tuple-element.10.refs_0_), channel_id=1, source_target_pairs={{0,2},{1,3},{2,0},{3,1},{4,6},{5,7},{6,4},{7,5},{8,10},{9,11},{10,... | collective-permute-start | bytes 393224 | tf_op jit(solution)/shard_map/ppermute | solution.py:293
  7.1 7.8 %collective-permute-start.2 = (bf16[2,2,64,256]{3,2,1,0:T(8,128)(2,1)}, bf16[2,2,64,256]{3,2,1,0:T(8,128)(2,1)S(1)}, u32[]{:S(2)}, u32[]{:S(2)}) collective-permute-start(bf16[2,2,64,256]{3,2,1,0:T(8,128)(2,1)} %get-tuple-element.11), channel_id=1, source_target_pairs={{0,18},{1,19},{2,16},{3,17},{4,22},{5,23},{6,20},{7,21},{8,26},{9,... | collective-permute-start | bytes 393224 | tf_op jit(solution)/shard_map/ppermute | solution.py:298
  8.6 7.7 %collective-permute-start = (bf16[2,2,64,256]{3,2,1,0:T(8,128)(2,1)}, bf16[2,2,64,256]{3,2,1,0:T(8,128)(2,1)S(1)}, u32[]{:S(2)}, u32[]{:S(2)}) collective-permute-start(bf16[2,2,64,256]{3,2,1,0:T(8,128)(2,1)} %get-tuple-element.11), channel_id=1, source_target_pairs={{0,16},{1,17},{2,18},{3,19},{4,20},{5,21},{6,22},{7,23},{8,24},{9,... | collective-permute-start | bytes 393224 | tf_op jit(solution)/shard_map/ppermute | solution.py:298
  16.3 0.9 %copy-start = (bf16[2,2,64,256]{3,2,1,0:T(8,128)(2,1)S(1)}, bf16[2,2,64,256]{3,2,1,0:T(8,128)(2,1)}, u32[]{:S(2)}) copy-start(bf16[2,2,64,256]{3,2,1,0:T(8,128)(2,1)} %get-tuple-element.10.refs_0_) | copy-start | bytes 393220
  17.7 1.3 %collective-permute-start.3 = (f32[1,128,128]{2,1,0:T(8,128)S(1)}, f32[1,128,128]{2,1,0:T(8,128)S(1)}, u32[]{:S(2)}, u32[]{:S(2)}) collective-permute-start(f32[1,128,128]{2,1,0:T(8,128)S(1)} %get-tuple-element.13), channel_id=1, source_target_pairs={{0,1},{1,0},{2,3},{3,2},{4,5},{5,4},{6,7},{7,6},{8,9},{9,8},{10,11... | collective-permute-start | bytes 196616 | tf_op jit(solution)/shard_map/ppermute | solution.py:293
  19.0 6.3 %collective-permute-start.6 = (f32[1,128,128]{2,1,0:T(8,128)S(1)}, f32[1,128,128]{2,1,0:T(8,128)S(1)}, u32[]{:S(2)}, u32[]{:S(2)}) collective-permute-start(f32[1,128,128]{2,1,0:T(8,128)S(1)} %add.3.refs_0_), channel_id=1, source_target_pairs={{0,12},{1,13},{2,14},{3,15},{4,8},{5,9},{6,10},{7,11},{8,4},{9,5},... | collective-permute-start | bytes 196616 | tf_op jit(solution)/shard_map/ppermute | solution.py:293
  22.7 5.9 %collective-permute-start.5 = (f32[1,128,128]{2,1,0:T(8,128)S(1)}, f32[1,128,128]{2,1,0:T(8,128)S(1)}, u32[]{:S(2)}, u32[]{:S(2)}) collective-permute-start(f32[1,128,128]{2,1,0:T(8,128)S(1)} %add.3.refs_0_), channel_id=1, source_target_pairs={{0,8},{1,9},{2,10},{3,11},{4,12},{5,13},{6,14},{7,15},{8,0},{9,1},... | collective-permute-start | bytes 196616 | tf_op jit(solution)/shard_map/ppermute | solution.py:293
  22.7 5.9 %collective-permute-start.4 = (f32[1,128,128]{2,1,0:T(8,128)S(1)}, f32[1,128,128]{2,1,0:T(8,128)S(1)}, u32[]{:S(2)}, u32[]{:S(2)}) collective-permute-start(f32[1,128,128]{2,1,0:T(8,128)S(1)} %add.3.refs_0_), channel_id=1, source_target_pairs={{0,4},{1,5},{2,6},{3,7},{4,0},{5,1},{6,2},{7,3},{8,12},{9,13},{10,... | collective-permute-start | bytes 196616 | tf_op jit(solution)/shard_map/ppermute | solution.py:293
  33.9 1.4 %collective-permute-start.7 = (f32[1,2,128,128]{3,2,1,0:T(8,128)S(1)}, f32[1,2,128,128]{3,2,1,0:T(8,128)S(1)}, u32[]{:S(2)}, u32[]{:S(2)}) collective-permute-start(f32[1,2,128,128]{3,2,1,0:T(8,128)S(1)} %factor.1.own_ref), channel_id=1, source_target_pairs={{0,1},{1,0},{2,3},{3,2},{4,5},{5,4},{6,7},{7,6},{8,9},{9,8},{10,11... | collective-permute-start | bytes 393224 | tf_op jit(solution)/shard_map/ppermute | solution.py:293

commit v3 on v2

--- a/solution.py
+++ b/solution.py
@@ -10,8 +10,7 @@
 
 TILE = 8
 CHUNK = 16
-VMEM_LIMIT = 48 * 1024 * 1024
-PROJECT_VMEM_LIMIT = 60 * 1024 * 1024
+VMEM_LIMIT = 32 * 1024 * 1024
 
 
 def whole_vmem(count):
@@ -104,7 +103,11 @@
 def project(snapshots, frequencies, offsets, groups):
     blocks, length, cells = snapshots.shape
     count = frequencies.shape[0]
-    shape = jax.ShapeDtypeStruct((count // groups, 2, blocks, cells), jnp.bfloat16)
+    shape = pltpu.VMEM((count // groups, 2, blocks, cells), jnp.bfloat16)
+    operands = [
+        pltpu.with_memory_space_constraint(operand, pltpu.HBM)
+        for operand in (frequencies, offsets.reshape(1, blocks), snapshots)
+    ]
     return pl.pallas_call(
         functools.partial(project_kernel, groups),
         out_shape=[shape] * groups,
@@ -116,9 +119,9 @@
             pltpu.VMEM(snapshots.shape, snapshots.dtype),
             pltpu.SemaphoreType.DMA((blocks // TILE + 2,)),
         ],
-        compiler_params=pltpu.CompilerParams(vmem_limit_bytes=PROJECT_VMEM_LIMIT),
+        compiler_params=pltpu.CompilerParams(vmem_limit_bytes=VMEM_LIMIT),
         name="project",
-    )(frequencies, offsets.reshape(1, blocks), snapshots)
+    )(*operands)
 
 
 def gram_kernel(halves, scale, *refs):

time: 36.5 us -> 34.7 us (0.951)
  local copies, waits for them, and re-layouts: 0.9 us -> 0 us
  Pallas kernels: 11 us -> 10.3 us
    unnamed x2 -> x0, local copies, waits for them, and re-layouts: 0.9 us -> none
    pallas_call x1, Pallas kernels: 4.06 us -> 3.38 us  [project(): pl.pallas_call(functools.partial(project_kernel, groups), out_shape=[shap...]
where the time goes in v3:
time: 34.7 us; the launch traced here: 34.6 us
  waiting for transfers between devices  15.1 us (44%)
  Pallas kernels  10.3 us (30%)
  starting transfers between devices  9.13 us (26%)
    ppermute x6, waiting for transfers between devices, swap(): return lax.ppermute(value, 'space', [(i, i ^ mask) for i in range(size)])  10 us
    ppermute x6, starting transfers between devices, swap(): return lax.ppermute(value, 'space', [(i, i ^ mask) for i in range(size)])  7.59 us
    pallas_call x1, Pallas kernels, factor(): pl.pallas_call(functools.partial(factor_kernel, len(terms)), out_shape=ja...  5.3 us
    ppermute x2, waiting for transfers between devices, swap_both(): return lax.ppermute(value, ('tm', 'space'), pairs)  5.07 us
    pallas_call x1, Pallas kernels, project(): pl.pallas_call(functools.partial(project_kernel, groups), out_shape=[shap...  3.38 us
    ppermute x2, starting transfers between devices, swap_both(): return lax.ppermute(value, ('tm', 'space'), pairs)  1.54 us
    pallas_call x1, Pallas kernels, apply(): pl.pallas_call(apply_kernel, out_shape=jax.ShapeDtypeStruct(held.shape, j...  1.11 us
  transfers between devices with their start and end apart: 8, of which 7 were waited for; matrix products, arithmetic and copies ran while one was open for 0% of the time, Pallas kernels for 0%

profile of v3, /device:TPU:0, one launch (start us, length us, event | category | flops | bytes accessed | tf_op | source)
XLA Modules:
  0.0 34.6 jit_solution(16654068600929299362)
XLA Ops:
  0.0 3.4 %project.1 = (bf16[2,2,64,256]{3,2,1,0:T(8,128)(2,1)S(1)}, bf16[2,2,64,256]{3,2,1,0:T(8,128)(2,1)S(1)}) custom-call(s32[4]{0:T(128)} %freq_in.1, s32[1,64]{1,0:T(1,128)} %bitcast.1, bf16[64,128,256]{2,1,0:T(8,128)(2,1)} %snap_ref.1), custom_call_target="tpu_custom_call" | custom-call | tf_op jit(solution)/shard_map/project/pallas_call | solution.py:111
  3.4 3.0 %collective-permute-start.1 = (bf16[2,2,64,256]{3,2,1,0:T(8,128)(2,1)S(1)}, bf16[2,2,64,256]{3,2,1,0:T(8,128)(2,1)S(1)}, u32[]{:S(2)}, u32[]{:S(2)}) collective-permute-start(bf16[2,2,64,256]{3,2,1,0:T(8,128)(2,1)S(1)} %get-tuple-element.10.refs_0_), channel_id=1, source_target_pairs={{0,2},{1,3},{2,0},{3,1},{4,6},{5,7},{6,4},{7,5},{8,10},{9,11},{10,... | collective-permute-start | bytes 393224 | tf_op jit(solution)/shard_map/ppermute | solution.py:296
  6.4 1.5 %collective-permute-start.2 = (bf16[2,2,64,256]{3,2,1,0:T(8,128)(2,1)S(1)}, bf16[2,2,64,256]{3,2,1,0:T(8,128)(2,1)S(1)}, u32[]{:S(2)}, u32[]{:S(2)}) collective-permute-start(bf16[2,2,64,256]{3,2,1,0:T(8,128)(2,1)S(1)} %get-tuple-element.11), channel_id=1, source_target_pairs={{0,18},{1,19},{2,16},{3,17},{4,22},{5,23},{6,20},{7,21},{8,26},{9,... | collective-permute-start | bytes 393224 | tf_op jit(solution)/shard_map/ppermute | solution.py:301
  7.9 0.0 collective-permute-start
  7.9 2.4 %collective-permute-done.1.refs_2_ = bf16[2,2,64,256]{3,2,1,0:T(8,128)(2,1)S(1)} collective-permute-done((bf16[2,2,64,256]{3,2,1,0:T(8,128)(2,1)S(1)}, bf16[2,2,64,256]{3,2,1,0:T(8,128)(2,1)S(1)}, u32[]{:S(2)}, u32[]{:S(2)}) %collective-permute-start.1) | collective-permute-done | bytes 131104 | tf_op jit(solution)/shard_map/ppermute | solution.py:296
  10.3 3.7 %collective-permute-done.2.refs_3_ = bf16[2,2,64,256]{3,2,1,0:T(8,128)(2,1)S(1)} collective-permute-done((bf16[2,2,64,256]{3,2,1,0:T(8,128)(2,1)S(1)}, bf16[2,2,64,256]{3,2,1,0:T(8,128)(2,1)S(1)}, u32[]{:S(2)}, u32[]{:S(2)}) %collective-permute-start.2) | collective-permute-done | bytes 131104 | tf_op jit(solution)/shard_map/ppermute | solution.py:301
  14.0 1.4 %collective-permute-done.refs_1_ = bf16[2,2,64,256]{3,2,1,0:T(8,128)(2,1)S(1)} collective-permute-done((bf16[2,2,64,256]{3,2,1,0:T(8,128)(2,1)S(1)}, bf16[2,2,64,256]{3,2,1,0:T(8,128)(2,1)S(1)}, u32[]{:S(2)}, u32[]{:S(2)}) %collective-permute-start) | collective-permute-done | bytes 131104 | tf_op jit(solution)/shard_map/ppermute | solution.py:301
  15.4 0.5 %gram.1 = (bf16[2,2,128,256]{3,2,1,0:T(8,128)(2,1)S(1)}, f32[1,128,128]{2,1,0:T(8,128)S(1)}, f32[1,128,128]{2,1,0:T(8,128)S(1)}) custom-call(bf16[2,2,64,256]{3,2,1,0:T(8,128)(2,1)S(1)} %get-tuple-element.10.refs_0_, bf16[2,2,64,256]{3,2,1,0:T(8,128)(2,1)S(1)} %collective-permute-done.refs_1_, bf16[2,2,64,256]{3,2,1,0:T(8,128)(2,1)S(1)} %collective-permute-done.1.refs_2_, ...), custom_call_target="tpu_custom_call" | custom-call | tf_op jit(solution)/shard_map/gram/pallas_call | solution.py:159
  15.9 0.1 collective-permute-start.3
  15.9 1.2 %collective-permute-done.3 = f32[1,128,128]{2,1,0:T(8,128)S(1)} collective-permute-done((f32[1,128,128]{2,1,0:T(8,128)S(1)}, f32[1,128,128]{2,1,0:T(8,128)S(1)}, u32[]{:S(2)}, u32[]{:S(2)}) %collective-permute-start.3) | collective-permute-done | bytes 65568 | tf_op jit(solution)/shard_map/ppermute | solution.py:296
  17.2 3.7 %collective-permute-start.6 = (f32[1,128,128]{2,1,0:T(8,128)S(1)}, f32[1,128,128]{2,1,0:T(8,128)S(1)}, u32[]{:S(2)}, u32[]{:S(2)}) collective-permute-start(f32[1,128,128]{2,1,0:T(8,128)S(1)} %add.3.refs_0_), channel_id=1, source_target_pairs={{0,12},{1,13},{2,14},{3,15},{4,8},{5,9},{6,10},{7,11},{8,4},{9,5},... | collective-permute-start | bytes 196616 | tf_op jit(solution)/shard_map/ppermute | solution.py:296
  20.9 0.0 collective-permute-start.5
  20.9 0.8 %collective-permute-start.4 = (f32[1,128,128]{2,1,0:T(8,128)S(1)}, f32[1,128,128]{2,1,0:T(8,128)S(1)}, u32[]{:S(2)}, u32[]{:S(2)}) collective-permute-start(f32[1,128,128]{2,1,0:T(8,128)S(1)} %add.3.refs_0_), channel_id=1, source_target_pairs={{0,4},{1,5},{2,6},{3,7},{4,0},{5,1},{6,2},{7,3},{8,12},{9,13},{10,... | collective-permute-start | bytes 196616 | tf_op jit(solution)/shard_map/ppermute | solution.py:296
  21.7 1.9 %collective-permute-done.6.refs_3_ = f32[1,128,128]{2,1,0:T(8,128)S(1)} collective-permute-done((f32[1,128,128]{2,1,0:T(8,128)S(1)}, f32[1,128,128]{2,1,0:T(8,128)S(1)}, u32[]{:S(2)}, u32[]{:S(2)}) %collective-permute-start.6) | collective-permute-done | bytes 65568 | tf_op jit(solution)/shard_map/ppermute | solution.py:296
  23.5 3.2 %collective-permute-done.5.refs_2_ = f32[1,128,128]{2,1,0:T(8,128)S(1)} collective-permute-done((f32[1,128,128]{2,1,0:T(8,128)S(1)}, f32[1,128,128]{2,1,0:T(8,128)S(1)}, u32[]{:S(2)}, u32[]{:S(2)}) %collective-permute-start.5) | collective-permute-done | bytes 65568 | tf_op jit(solution)/shard_map/ppermute | solution.py:296
  26.8 0.0 collective-permute-done.4.refs_1_
  26.8 5.3 %factor.1.own_ref = f32[1,2,128,128]{3,2,1,0:T(8,128)S(1)} custom-call(f32[1,128,128]{2,1,0:T(8,128)S(1)} %add.3.refs_0_, f32[1,128,128]{2,1,0:T(8,128)S(1)} %collective-permute-done.4.refs_1_, f32[1,128,128]{2,1,0:T(8,128)S(1)} %collective-permute-done.5.refs_2_, f32[1,128,128]{2,1,0:T(8,128)S(1)} %collective-permute-done.6.refs_3_), custom_call_target="tpu_custom_call" | custom-call | tf_op jit(solution)/shard_map/factor/pallas_call | solution.py:250
  32.1 0.1 collective-permute-start.7
  32.1 1.3 %collective-permute-done.7.sent_ref = f32[1,2,128,128]{3,2,1,0:T(8,128)S(1)} collective-permute-done((f32[1,2,128,128]{3,2,1,0:T(8,128)S(1)}, f32[1,2,128,128]{3,2,1,0:T(8,128)S(1)}, u32[]{:S(2)}, u32[]{:S(2)}) %collective-permute-start.7) | collective-permute-done | bytes 131104 | tf_op jit(solution)/shard_map/ppermute | solution.py:296
  33.5 1.1 %apply.1 = f32[2,2,128,256]{3,2,1,0:T(8,128)} custom-call(f32[1,2,128,128]{3,2,1,0:T(8,128)S(1)} %factor.1.own_ref, f32[1,2,128,128]{3,2,1,0:T(8,128)S(1)} %collective-permute-done.7.sent_ref, bf16[2,2,128,256]{3,2,1,0:T(8,128)(2,1)S(1)} %get-tuple-element.14.held_ref), custom_call_target="tpu_custom_call" | custom-call | tf_op jit(solution)/shard_map/apply/pallas_call | solution.py:285
  (1 shorter events, 0.0 us)
Async XLA Ops:
  3.4 6.9 %collective-permute-start.1 = (bf16[2,2,64,256]{3,2,1,0:T(8,128)(2,1)S(1)}, bf16[2,2,64,256]{3,2,1,0:T(8,128)(2,1)S(1)}, u32[]{:S(2)}, u32[]{:S(2)}) collective-permute-start(bf16[2,2,64,256]{3,2,1,0:T(8,128)(2,1)S(1)} %get-tuple-element.10.refs_0_), channel_id=1, source_target_pairs={{0,2},{1,3},{2,0},{3,1},{4,6},{5,7},{6,4},{7,5},{8,10},{9,11},{10,... | collective-permute-start | bytes 393224 | tf_op jit(solution)/shard_map/ppermute | solution.py:296
  6.4 7.6 %collective-permute-start.2 = (bf16[2,2,64,256]{3,2,1,0:T(8,128)(2,1)S(1)}, bf16[2,2,64,256]{3,2,1,0:T(8,128)(2,1)S(1)}, u32[]{:S(2)}, u32[]{:S(2)}) collective-permute-start(bf16[2,2,64,256]{3,2,1,0:T(8,128)(2,1)S(1)} %get-tuple-element.11), channel_id=1, source_target_pairs={{0,18},{1,19},{2,16},{3,17},{4,22},{5,23},{6,20},{7,21},{8,26},{9,... | collective-permute-start | bytes 393224 | tf_op jit(solution)/shard_map/ppermute | solution.py:301
  7.9 7.5 %collective-permute-start = (bf16[2,2,64,256]{3,2,1,0:T(8,128)(2,1)S(1)}, bf16[2,2,64,256]{3,2,1,0:T(8,128)(2,1)S(1)}, u32[]{:S(2)}, u32[]{:S(2)}) collective-permute-start(bf16[2,2,64,256]{3,2,1,0:T(8,128)(2,1)S(1)} %get-tuple-element.11), channel_id=1, source_target_pairs={{0,16},{1,17},{2,18},{3,19},{4,20},{5,21},{6,22},{7,23},{8,24},{9,... | collective-permute-start | bytes 393224 | tf_op jit(solution)/shard_map/ppermute | solution.py:301
  15.9 1.3 %collective-permute-start.3 = (f32[1,128,128]{2,1,0:T(8,128)S(1)}, f32[1,128,128]{2,1,0:T(8,128)S(1)}, u32[]{:S(2)}, u32[]{:S(2)}) collective-permute-start(f32[1,128,128]{2,1,0:T(8,128)S(1)} %get-tuple-element.13), channel_id=1, source_target_pairs={{0,1},{1,0},{2,3},{3,2},{4,5},{5,4},{6,7},{7,6},{8,9},{9,8},{10,11... | collective-permute-start | bytes 196616 | tf_op jit(solution)/shard_map/ppermute | solution.py:296
  17.2 6.3 %collective-permute-start.6 = (f32[1,128,128]{2,1,0:T(8,128)S(1)}, f32[1,128,128]{2,1,0:T(8,128)S(1)}, u32[]{:S(2)}, u32[]{:S(2)}) collective-permute-start(f32[1,128,128]{2,1,0:T(8,128)S(1)} %add.3.refs_0_), channel_id=1, source_target_pairs={{0,12},{1,13},{2,14},{3,15},{4,8},{5,9},{6,10},{7,11},{8,4},{9,5},... | collective-permute-start | bytes 196616 | tf_op jit(solution)/shard_map/ppermute | solution.py:296
  20.9 5.9 %collective-permute-start.5 = (f32[1,128,128]{2,1,0:T(8,128)S(1)}, f32[1,128,128]{2,1,0:T(8,128)S(1)}, u32[]{:S(2)}, u32[]{:S(2)}) collective-permute-start(f32[1,128,128]{2,1,0:T(8,128)S(1)} %add.3.refs_0_), channel_id=1, source_target_pairs={{0,8},{1,9},{2,10},{3,11},{4,12},{5,13},{6,14},{7,15},{8,0},{9,1},... | collective-permute-start | bytes 196616 | tf_op jit(solution)/shard_map/ppermute | solution.py:296
  20.9 5.9 %collective-permute-start.4 = (f32[1,128,128]{2,1,0:T(8,128)S(1)}, f32[1,128,128]{2,1,0:T(8,128)S(1)}, u32[]{:S(2)}, u32[]{:S(2)}) collective-permute-start(f32[1,128,128]{2,1,0:T(8,128)S(1)} %add.3.refs_0_), channel_id=1, source_target_pairs={{0,4},{1,5},{2,6},{3,7},{4,0},{5,1},{6,2},{7,3},{8,12},{9,13},{10,... | collective-permute-start | bytes 196616 | tf_op jit(solution)/shard_map/ppermute | solution.py:296
  32.1 1.4 %collective-permute-start.7 = (f32[1,2,128,128]{3,2,1,0:T(8,128)S(1)}, f32[1,2,128,128]{3,2,1,0:T(8,128)S(1)}, u32[]{:S(2)}, u32[]{:S(2)}) collective-permute-start(f32[1,2,128,128]{3,2,1,0:T(8,128)S(1)} %factor.1.own_ref), channel_id=1, source_target_pairs={{0,1},{1,0},{2,3},{3,2},{4,5},{5,4},{6,7},{7,6},{8,9},{9,8},{10,11... | collective-permute-start | bytes 393224 | tf_op jit(solution)/shard_map/ppermute | solution.py:296

commit v4 on v3

--- a/solution.py
+++ b/solution.py
@@ -74,6 +74,7 @@
         parts = []
         for half in range(CHUNK // TILE):
             copies[step * (CHUNK // TILE) + half].wait()
+        for half in range(CHUNK // TILE):
             start = step * CHUNK + half * TILE
             data = held[start : start + TILE].reshape(TILE * length, cells)
             projected = jnp.dot(spread_table, data, preferred_element_type=jnp.float32)
@@ -125,21 +126,19 @@
 
 
 def gram_kernel(halves, scale, *refs):
-    pieces = refs[: 2 * halves]
-    held_ref, keep_ref, send_ref, other, packed = refs[2 * halves :]
+    pieces = refs[:halves]
+    held_ref, keep_ref, send_ref, packed = refs[halves:]
     count = held_ref.shape[0]
     order = held_ref.shape[2]
     first = lax.axis_index("tm") if halves > 1 else 0
     size = order // halves
-    for s, target in ((0, held_ref), (1, other)):
-        for h in range(halves):
-            place = pl.ds(pl.multiple_of(lax.rem(first + h, halves) * size, size), size)
-            target[:, :, place, :] = pieces[s * halves + h][...]
+    for h in range(halves):
+        place = pl.ds(pl.multiple_of(lax.rem(first + h, halves) * size, size), size)
+        held_ref[:, :, place, :] = pieces[h][...]
     lower = rows_of((order, order)) >= lanes_of((order, order))
     turn = (((1,), (1,)), ((), ()))
     for f in range(count):
-        real = jnp.concatenate([held_ref[f, 0], other[f, 0]], axis=1)
-        imag = jnp.concatenate([held_ref[f, 1], other[f, 1]], axis=1)
+        real, imag = held_ref[f, 0], held_ref[f, 1]
         both = jnp.concatenate([real, imag], axis=1)
         crossed = jnp.concatenate([imag, -real], axis=1)
         gram_real = lax.dot_general(both, both, turn, preferred_element_type=jnp.float32)
@@ -162,7 +161,6 @@
         in_specs=whole_vmem(len(pieces)),
         out_specs=whole_vmem(3),
         scratch_shapes=[
-            pltpu.VMEM(held.shape, held.dtype),
             pltpu.VMEM((count, order, order), jnp.float32),
         ],
         compiler_params=pltpu.CompilerParams(vmem_limit_bytes=VMEM_LIMIT),
@@ -296,31 +294,21 @@
     return lax.ppermute(value, "space", [(i, i ^ mask) for i in range(size)])
 
 
-def swap_both(value, size, mask):
-    pairs = [(t * size + i, (1 - t) * size + (i ^ mask)) for t in range(2) for i in range(size)]
-    return lax.ppermute(value, ("tm", "space"), pairs)
-
-
 def local(snapshots, frequencies, offsets):
     halves = lax.axis_size("tm")
     size = lax.axis_size("space")
     scale = 1.0 / (snapshots.shape[2] * size)
     if halves == 2:
         mine, theirs = project(snapshots, frequencies, offsets, 2)
-        pieces = [
-            mine,
-            swap_both(theirs, size, 0),
-            swap(mine, size, 2),
-            swap_both(theirs, size, 2),
-        ]
+        pieces = [mine, lax.ppermute(theirs, "tm", [(0, 1), (1, 0)])]
         held, keep, send = gram(pieces, 2, scale)
     else:
         (coeffs,) = project(snapshots, frequencies, offsets, 1)
         regrouped = lax.all_to_all(coeffs, "tm", split_axis=0, concat_axis=2, tiled=True)
-        held, keep, send = gram([regrouped, swap(regrouped, size, 2)], 1, scale)
+        held, keep, send = gram([regrouped], 1, scale)
     total = keep + swap(send, size, 1)
     terms = [total]
-    bit = 4
+    bit = 2
     while bit < size:
         total = functools.reduce(jnp.add, terms)
         masks = [bit, 2 * bit, 3 * bit] if 2 * bit < size else [bit]

time: 34.7 us -> 31.5 us (0.908)
  waiting for transfers between devices: 15.1 us -> 12.6 us
  Pallas kernels: 10.3 us -> 9.31 us
    ppermute x2 -> x1, waiting for transfers between devices: 5.07 us -> 3.5 us  [local(): pieces = [mine, lax.ppermute(theirs, 'tm', [(0, 1), (1, 0)])]]
    ppermute x2 -> x1, starting transfers between devices: 1.54 us -> 3.03 us  [local(): pieces = [mine, lax.ppermute(theirs, 'tm', [(0, 1), (1, 0)])]]
    ppermute x6, starting transfers between devices: 7.59 us -> 6.35 us  [swap(): return lax.ppermute(value, 'space', [(i, i ^ mask) for i in range(size)])]
    ppermute x6, waiting for transfers between devices: 10 us -> 9.1 us  [swap(): return lax.ppermute(value, 'space', [(i, i ^ mask) for i in range(size)])]
    pallas_call x1, Pallas kernels: 3.38 us -> 2.56 us  [project(): pl.pallas_call(functools.partial(project_kernel, groups), out_shape=[shap...]
  transfers between devices with their start and end apart: 8 -> 7, of which waited for: 7 -> 7; matrix products, arithmetic and copies ran while one was open for 0% -> 0% of each run, Pallas kernels for 0% -> 0%
where the time goes in v4:
time: 31.5 us; the launch traced here: 31.4 us
  waiting for transfers between devices  12.6 us (40%)
  starting transfers between devices  9.38 us (30%)
  Pallas kernels  9.31 us (30%)
    ppermute x6, waiting for transfers between devices, swap(): return lax.ppermute(value, 'space', [(i, i ^ mask) for i in range(size)])  9.1 us
    ppermute x6, starting transfers between devices, swap(): return lax.ppermute(value, 'space', [(i, i ^ mask) for i in range(size)])  6.35 us
    pallas_call x1, Pallas kernels, factor(): pl.pallas_call(functools.partial(factor_kernel, len(terms)), out_shape=ja...  5.3 us
    ppermute x1, waiting for transfers between devices, local(): pieces = [mine, lax.ppermute(theirs, 'tm', [(0, 1), (1, 0)])]  3.5 us
    ppermute x1, starting transfers between devices, local(): pieces = [mine, lax.ppermute(theirs, 'tm', [(0, 1), (1, 0)])]  3.03 us
    pallas_call x1, Pallas kernels, project(): pl.pallas_call(functools.partial(project_kernel, groups), out_shape=[shap...  2.56 us
    pallas_call x1, Pallas kernels, apply(): pl.pallas_call(apply_kernel, out_shape=jax.ShapeDtypeStruct(held.shape, j...  1.11 us
  transfers between devices with their start and end apart: 7, of which 7 were waited for; matrix products, arithmetic and copies ran while one was open for 0% of the time, Pallas kernels for 0%

profile of v4, /device:TPU:0, one launch (start us, length us, event | category | flops | bytes accessed | tf_op | source)
XLA Modules:
  0.0 31.4 jit_solution(16598225767503919200)
XLA Ops:
  0.0 2.6 %project.1 = (bf16[2,2,64,256]{3,2,1,0:T(8,128)(2,1)S(1)}, bf16[2,2,64,256]{3,2,1,0:T(8,128)(2,1)S(1)}) custom-call(s32[4]{0:T(128)} %freq_in.1, s32[1,64]{1,0:T(1,128)} %bitcast.1, bf16[64,128,256]{2,1,0:T(8,128)(2,1)} %snap_ref.1), custom_call_target="tpu_custom_call" | custom-call | tf_op jit(solution)/shard_map/project/pallas_call | solution.py:112
  2.6 3.0 %collective-permute-start = (bf16[2,2,64,256]{3,2,1,0:T(8,128)(2,1)S(1)}, bf16[2,2,64,256]{3,2,1,0:T(8,128)(2,1)S(1)}, u32[]{:S(2)}, u32[]{:S(2)}) collective-permute-start(bf16[2,2,64,256]{3,2,1,0:T(8,128)(2,1)S(1)} %get-tuple-element.11), channel_id=1, source_target_pairs={{0,16},{16,0},{1,17},{17,1},{2,18},{18,2},{3,19},{19,3},{4,20},{20... | collective-permute-start | bytes 393224 | tf_op jit(solution)/shard_map/ppermute | solution.py:303
  5.6 3.5 %collective-permute-done.refs_1_ = bf16[2,2,64,256]{3,2,1,0:T(8,128)(2,1)S(1)} collective-permute-done((bf16[2,2,64,256]{3,2,1,0:T(8,128)(2,1)S(1)}, bf16[2,2,64,256]{3,2,1,0:T(8,128)(2,1)S(1)}, u32[]{:S(2)}, u32[]{:S(2)}) %collective-permute-start) | collective-permute-done | bytes 131104 | tf_op jit(solution)/shard_map/ppermute | solution.py:303
  9.1 0.4 %gram.1 = (bf16[2,2,128,256]{3,2,1,0:T(8,128)(2,1)S(1)}, f32[1,128,128]{2,1,0:T(8,128)S(1)}, f32[1,128,128]{2,1,0:T(8,128)S(1)}) custom-call(bf16[2,2,64,256]{3,2,1,0:T(8,128)(2,1)S(1)} %get-tuple-element.10.refs_0_, bf16[2,2,64,256]{3,2,1,0:T(8,128)(2,1)S(1)} %collective-permute-done.refs_1_), custom_call_target="tpu_custom_call" | custom-call | tf_op jit(solution)/shard_map/gram/pallas_call | solution.py:158
  9.4 0.1 collective-permute-start.1
  9.5 1.2 %collective-permute-done.1 = f32[1,128,128]{2,1,0:T(8,128)S(1)} collective-permute-done((f32[1,128,128]{2,1,0:T(8,128)S(1)}, f32[1,128,128]{2,1,0:T(8,128)S(1)}, u32[]{:S(2)}, u32[]{:S(2)}) %collective-permute-start.1) | collective-permute-done | bytes 65568 | tf_op jit(solution)/shard_map/ppermute | solution.py:294
  10.8 2.8 %collective-permute-start.4 = (f32[1,128,128]{2,1,0:T(8,128)S(1)}, f32[1,128,128]{2,1,0:T(8,128)S(1)}, u32[]{:S(2)}, u32[]{:S(2)}) collective-permute-start(f32[1,128,128]{2,1,0:T(8,128)S(1)} %add.12), channel_id=1, source_target_pairs={{0,6},{1,7},{2,4},{3,5},{4,2},{5,3},{6,0},{7,1},{8,14},{9,15},{10,... | collective-permute-start | bytes 196616 | tf_op jit(solution)/shard_map/ppermute | solution.py:294
  13.6 0.4 %collective-permute-start.3 = (f32[1,128,128]{2,1,0:T(8,128)S(1)}, f32[1,128,128]{2,1,0:T(8,128)S(1)}, u32[]{:S(2)}, u32[]{:S(2)}) collective-permute-start(f32[1,128,128]{2,1,0:T(8,128)S(1)} %add.12), channel_id=1, source_target_pairs={{0,4},{1,5},{2,6},{3,7},{4,0},{5,1},{6,2},{7,3},{8,12},{9,13},{10,... | collective-permute-start | bytes 196616 | tf_op jit(solution)/shard_map/ppermute | solution.py:294
  14.0 0.3 %collective-permute-start.2 = (f32[1,128,128]{2,1,0:T(8,128)S(1)}, f32[1,128,128]{2,1,0:T(8,128)S(1)}, u32[]{:S(2)}, u32[]{:S(2)}) collective-permute-start(f32[1,128,128]{2,1,0:T(8,128)S(1)} %add.12), channel_id=1, source_target_pairs={{0,2},{1,3},{2,0},{3,1},{4,6},{5,7},{6,4},{7,5},{8,10},{9,11},{10,... | collective-permute-start | bytes 196616 | tf_op jit(solution)/shard_map/ppermute | solution.py:294
  14.3 1.7 %collective-permute-done.4 = f32[1,128,128]{2,1,0:T(8,128)S(1)} collective-permute-done((f32[1,128,128]{2,1,0:T(8,128)S(1)}, f32[1,128,128]{2,1,0:T(8,128)S(1)}, u32[]{:S(2)}, u32[]{:S(2)}) %collective-permute-start.4) | collective-permute-done | bytes 65568 | tf_op jit(solution)/shard_map/ppermute | solution.py:294
  16.0 1.8 %collective-permute-done.3 = f32[1,128,128]{2,1,0:T(8,128)S(1)} collective-permute-done((f32[1,128,128]{2,1,0:T(8,128)S(1)}, f32[1,128,128]{2,1,0:T(8,128)S(1)}, u32[]{:S(2)}, u32[]{:S(2)}) %collective-permute-start.3) | collective-permute-done | bytes 65568 | tf_op jit(solution)/shard_map/ppermute | solution.py:294
  17.8 0.4 %collective-permute-done.2 = f32[1,128,128]{2,1,0:T(8,128)S(1)} collective-permute-done((f32[1,128,128]{2,1,0:T(8,128)S(1)}, f32[1,128,128]{2,1,0:T(8,128)S(1)}, u32[]{:S(2)}, u32[]{:S(2)}) %collective-permute-start.2) | collective-permute-done | bytes 65568 | tf_op jit(solution)/shard_map/ppermute | solution.py:294
  18.3 2.7 %collective-permute-start.5 = (f32[1,128,128]{2,1,0:T(8,128)S(1)}, f32[1,128,128]{2,1,0:T(8,128)S(1)}, u32[]{:S(2)}, u32[]{:S(2)}) collective-permute-start(f32[1,128,128]{2,1,0:T(8,128)S(1)} %add_add_fusion.refs_0_), channel_id=1, source_target_pairs={{0,8},{1,9},{2,10},{3,11},{4,12},{5,13},{6,14},{7,15},{8,0},{9,1},... | collective-permute-start | bytes 196616 | tf_op jit(solution)/shard_map/ppermute | solution.py:294
  21.0 2.6 %collective-permute-done.5.refs_1_ = f32[1,128,128]{2,1,0:T(8,128)S(1)} collective-permute-done((f32[1,128,128]{2,1,0:T(8,128)S(1)}, f32[1,128,128]{2,1,0:T(8,128)S(1)}, u32[]{:S(2)}, u32[]{:S(2)}) %collective-permute-start.5) | collective-permute-done | bytes 65568 | tf_op jit(solution)/shard_map/ppermute | solution.py:294
  23.5 5.3 %factor.1.own_ref = f32[1,2,128,128]{3,2,1,0:T(8,128)S(1)} custom-call(f32[1,128,128]{2,1,0:T(8,128)S(1)} %add_add_fusion.refs_0_, f32[1,128,128]{2,1,0:T(8,128)S(1)} %collective-permute-done.5.refs_1_), custom_call_target="tpu_custom_call" | custom-call | tf_op jit(solution)/shard_map/factor/pallas_call | solution.py:248
  28.8 0.1 collective-permute-start.6
  28.9 1.3 %collective-permute-done.6.sent_ref = f32[1,2,128,128]{3,2,1,0:T(8,128)S(1)} collective-permute-done((f32[1,2,128,128]{3,2,1,0:T(8,128)S(1)}, f32[1,2,128,128]{3,2,1,0:T(8,128)S(1)}, u32[]{:S(2)}, u32[]{:S(2)}) %collective-permute-start.6) | collective-permute-done | bytes 131104 | tf_op jit(solution)/shard_map/ppermute | solution.py:294
  30.2 1.1 %apply.1 = f32[2,2,128,256]{3,2,1,0:T(8,128)} custom-call(f32[1,2,128,128]{3,2,1,0:T(8,128)S(1)} %factor.1.own_ref, f32[1,2,128,128]{3,2,1,0:T(8,128)S(1)} %collective-permute-done.6.sent_ref, bf16[2,2,128,256]{3,2,1,0:T(8,128)(2,1)S(1)} %get-tuple-element.14.held_ref), custom_call_target="tpu_custom_call" | custom-call | tf_op jit(solution)/shard_map/apply/pallas_call | solution.py:283
  (2 shorter events, 0.0 us)
Async XLA Ops:
  2.6 6.5 %collective-permute-start = (bf16[2,2,64,256]{3,2,1,0:T(8,128)(2,1)S(1)}, bf16[2,2,64,256]{3,2,1,0:T(8,128)(2,1)S(1)}, u32[]{:S(2)}, u32[]{:S(2)}) collective-permute-start(bf16[2,2,64,256]{3,2,1,0:T(8,128)(2,1)S(1)} %get-tuple-element.11), channel_id=1, source_target_pairs={{0,16},{16,0},{1,17},{17,1},{2,18},{18,2},{3,19},{19,3},{4,20},{20... | collective-permute-start | bytes 393224 | tf_op jit(solution)/shard_map/ppermute | solution.py:303
  9.4 1.3 %collective-permute-start.1 = (f32[1,128,128]{2,1,0:T(8,128)S(1)}, f32[1,128,128]{2,1,0:T(8,128)S(1)}, u32[]{:S(2)}, u32[]{:S(2)}) collective-permute-start(f32[1,128,128]{2,1,0:T(8,128)S(1)} %get-tuple-element.13), channel_id=1, source_target_pairs={{0,1},{1,0},{2,3},{3,2},{4,5},{5,4},{6,7},{7,6},{8,9},{9,8},{10,11... | collective-permute-start | bytes 196616 | tf_op jit(solution)/shard_map/ppermute | solution.py:294
  10.8 5.2 %collective-permute-start.4 = (f32[1,128,128]{2,1,0:T(8,128)S(1)}, f32[1,128,128]{2,1,0:T(8,128)S(1)}, u32[]{:S(2)}, u32[]{:S(2)}) collective-permute-start(f32[1,128,128]{2,1,0:T(8,128)S(1)} %add.12), channel_id=1, source_target_pairs={{0,6},{1,7},{2,4},{3,5},{4,2},{5,3},{6,0},{7,1},{8,14},{9,15},{10,... | collective-permute-start | bytes 196616 | tf_op jit(solution)/shard_map/ppermute | solution.py:294
  13.6 4.3 %collective-permute-start.3 = (f32[1,128,128]{2,1,0:T(8,128)S(1)}, f32[1,128,128]{2,1,0:T(8,128)S(1)}, u32[]{:S(2)}, u32[]{:S(2)}) collective-permute-start(f32[1,128,128]{2,1,0:T(8,128)S(1)} %add.12), channel_id=1, source_target_pairs={{0,4},{1,5},{2,6},{3,7},{4,0},{5,1},{6,2},{7,3},{8,12},{9,13},{10,... | collective-permute-start | bytes 196616 | tf_op jit(solution)/shard_map/ppermute | solution.py:294
  14.0 4.3 %collective-permute-start.2 = (f32[1,128,128]{2,1,0:T(8,128)S(1)}, f32[1,128,128]{2,1,0:T(8,128)S(1)}, u32[]{:S(2)}, u32[]{:S(2)}) collective-permute-start(f32[1,128,128]{2,1,0:T(8,128)S(1)} %add.12), channel_id=1, source_target_pairs={{0,2},{1,3},{2,0},{3,1},{4,6},{5,7},{6,4},{7,5},{8,10},{9,11},{10,... | collective-permute-start | bytes 196616 | tf_op jit(solution)/shard_map/ppermute | solution.py:294
  18.3 5.2 %collective-permute-start.5 = (f32[1,128,128]{2,1,0:T(8,128)S(1)}, f32[1,128,128]{2,1,0:T(8,128)S(1)}, u32[]{:S(2)}, u32[]{:S(2)}) collective-permute-start(f32[1,128,128]{2,1,0:T(8,128)S(1)} %add_add_fusion.refs_0_), channel_id=1, source_target_pairs={{0,8},{1,9},{2,10},{3,11},{4,12},{5,13},{6,14},{7,15},{8,0},{9,1},... | collective-permute-start | bytes 196616 | tf_op jit(solution)/shard_map/ppermute | solution.py:294
  28.8 1.4 %collective-permute-start.6 = (f32[1,2,128,128]{3,2,1,0:T(8,128)S(1)}, f32[1,2,128,128]{3,2,1,0:T(8,128)S(1)}, u32[]{:S(2)}, u32[]{:S(2)}) collective-permute-start(f32[1,2,128,128]{3,2,1,0:T(8,128)S(1)} %factor.1.own_ref), channel_id=1, source_target_pairs={{0,1},{1,0},{2,3},{3,2},{4,5},{5,4},{6,7},{7,6},{8,9},{9,8},{10,11... | collective-permute-start | bytes 393224 | tf_op jit(solution)/shard_map/ppermute | solution.py:294

commit v5 on v4

--- a/solution.py
+++ b/solution.py
@@ -173,65 +173,144 @@
 
 
 def spread_lane(tile, p):
-    return jnp.broadcast_to(tile[:, p : p + 1], tile.shape)
+    return jnp.take_along_axis(tile, jnp.full(tile.shape, p, jnp.int32), axis=1)
+
+
+def add_up(terms):
+    while len(terms) > 1:
+        pairs = [a + b for a, b in zip(terms[::2], terms[1::2])]
+        terms = pairs + terms[len(pairs) * 2 :]
+    return terms[0]
+
+
+def column_pairs(tile, base):
+    return [tuple(spread_lane(part, base + p) for part in tile) for p in range(TILE)]
+
+
+def row_pairs(tile):
+    return [tuple(spread_row(part, p) for part in tile) for p in range(TILE)]
+
+
+def subtract_product(tile, columns, rows):
+    pairs = list(zip(columns, rows))
+    return (
+        tile[0] - add_up([cr * rr - ci * ri for (cr, ci), (rr, ri) in pairs]),
+        tile[1] - add_up([cr * ri + ci * rr for (cr, ci), (rr, ri) in pairs]),
+    )
+
+
+def clear_lanes(tile, low, high):
+    lane = lanes_of(tile[0].shape)
+    cleared = (lane >= low) & (lane < high)
+    return tuple(jnp.where(cleared, 0.0, part) for part in tile)
+
+
+def eliminate_tile(tile, base):
+    shape = tile[0].shape
+    row = rows_of(shape)
+    columns = column_pairs(tile, base)
+    real, imag = clear_lanes(tile, base, base + TILE)
+    real = jnp.where(lanes_of(shape) == base + row, 1.0, real)
+    done_real, done_imag = real, imag
+    inverses = jnp.ones(shape, jnp.float32)
+    for p in range(TILE):
+        here = row == p
+        pivot = spread_row(columns[p][0], p)
+        inverse = 1.0 / pivot
+        root = lax.rsqrt(pivot)
+        done_real = jnp.where(here, real * root, done_real)
+        done_imag = jnp.where(here, imag * root, done_imag)
+        inverses = jnp.where(here, inverse, inverses)
+        lead_real, lead_imag = (jnp.where(here, 0.0, part) * inverse for part in columns[p])
+
+        def reduce_rows(a_real, a_imag):
+            top_real, top_imag = spread_row(a_real, p), spread_row(a_imag, p)
+            return (
+                a_real - (lead_real * top_real - lead_imag * top_imag),
+                a_imag - (lead_real * top_imag + lead_imag * top_real),
+            )
+
+        for q in range(p + 1, TILE):
+            columns[q] = reduce_rows(*columns[q])
+        real, imag = reduce_rows(real, imag)
+    return (done_real, done_imag), (real * inverses, imag * inverses)
+
+
+def three_parts(value):
+    parts = []
+    for _ in range(3):
+        parts.append(value.astype(jnp.bfloat16))
+        value = value - parts[-1].astype(jnp.float32)
+    return parts
+
+
+def outer_product(real, imag):
+    reals, imags = three_parts(real), three_parts(imag)
+    left = [jnp.concatenate(pair, axis=0) for pair in zip(reals, imags)]
+    right = [
+        jnp.concatenate(
+            [jnp.concatenate([a, b], axis=1), jnp.concatenate([b, -a], axis=1)], axis=0
+        )
+        for a, b in zip(reals, imags)
+    ]
+    chosen = [(0, 0), (0, 1), (1, 0), (0, 2), (2, 0), (1, 1)]
+    return lax.dot_general(
+        jnp.concatenate([left[a] for a, _ in chosen], axis=0),
+        jnp.concatenate([right[b] for _, b in chosen], axis=0),
+        (((0,), (0,)), ((), ())),
+        preferred_element_type=jnp.float32,
+    )
 
 
 def invert_factor(packed, out_ref, slot):
     order = packed.shape[0]
-    shape = (TILE, order)
-    tiles = order // TILE
+    count = order // TILE
     flipped = packed.T
     row, lane = rows_of((order, order)), lanes_of((order, order))
     full_real = jnp.where(row >= lane, packed, flipped)
     full_imag = jnp.where(row < lane, packed, jnp.where(row == lane, 0.0, -flipped))
-    real = [full_real[t * TILE : (t + 1) * TILE] for t in range(tiles)]
-    imag = [full_imag[t * TILE : (t + 1) * TILE] for t in range(tiles)]
-    tile_row, tile_lane = rows_of(shape), lanes_of(shape)
-    at_row = [tile_row == p for p in range(TILE)]
-    for k in range(tiles):
-        base = k * TILE
-        inside = (tile_lane >= base) & (tile_lane < base + TILE)
-        col_real = [spread_lane(real[k], base + q) for q in range(TILE)]
-        col_imag = [spread_lane(imag[k], base + q) for q in range(TILE)]
-        here_real = jnp.where(inside, jnp.where(tile_lane == base + tile_row, 1.0, 0.0), real[k])
-        here_imag = jnp.where(inside, 0.0, imag[k])
-        done_real, done_imag = here_real, here_imag
-        for p in range(TILE):
-            pivot = spread_row(col_real[p], p)
-            inverse = 1.0 / pivot
-            root = lax.rsqrt(pivot)
-            done_real = jnp.where(at_row[p], here_real * root, done_real)
-            done_imag = jnp.where(at_row[p], here_imag * root, done_imag)
-            lead_real, lead_imag = col_real[p], col_imag[p]
-
-            def eliminate(a_real, a_imag):
-                top_real = spread_row(a_real, p) * inverse
-                top_imag = spread_row(a_imag, p) * inverse
-                new_real = a_real - (lead_real * top_real - lead_imag * top_imag)
-                new_imag = a_imag - (lead_real * top_imag + lead_imag * top_real)
-                return (
-                    jnp.where(at_row[p], top_real, new_real),
-                    jnp.where(at_row[p], top_imag, new_imag),
-                )
-
-            for q in range(p + 1, TILE):
-                col_real[q], col_imag[q] = eliminate(col_real[q], col_imag[q])
-            here_real, here_imag = eliminate(here_real, here_imag)
-        keep = tile_lane < base + TILE
-        out_ref[slot, 0, base : base + TILE, :] = jnp.where(keep, done_real, 0.0)
-        out_ref[slot, 1, base : base + TILE, :] = jnp.where(keep, done_imag, 0.0)
-        if k + 1 < tiles:
-            rows_real = [spread_row(here_real, p) for p in range(TILE)]
-            rows_imag = [spread_row(here_imag, p) for p in range(TILE)]
-        for t in range(k + 1, tiles):
-            a_real = jnp.where(inside, 0.0, real[t])
-            a_imag = jnp.where(inside, 0.0, imag[t])
-            for p in range(TILE):
-                lead_real = spread_lane(real[t], base + p)
-                lead_imag = spread_lane(imag[t], base + p)
-                a_real = a_real - lead_real * rows_real[p] + lead_imag * rows_imag[p]
-                a_imag = a_imag - lead_real * rows_imag[p] - lead_imag * rows_real[p]
-            real[t], imag[t] = a_real, a_imag
+    tiles = [
+        (full_real[t * TILE : (t + 1) * TILE], full_imag[t * TILE : (t + 1) * TILE])
+        for t in range(count)
+    ]
+
+    def store(done, base):
+        kept = clear_lanes(done, base + TILE, order)
+        out_ref[slot, 0, base : base + TILE, :] = kept[0]
+        out_ref[slot, 1, base : base + TILE, :] = kept[1]
+
+    for first in range(0, count, 2):
+        second = first + 1
+        base, middle, end = first * TILE, second * TILE, (second + 1) * TILE
+        near = [t for t in (first + 2, first + 3) if t < count]
+        columns = column_pairs(tiles[second], base)
+        upper_done, upper = eliminate_tile(tiles[first], base)
+        store(upper_done, base)
+        tiles[second] = subtract_product(
+            clear_lanes(tiles[second], base, middle), columns, row_pairs(upper)
+        )
+        back = column_pairs(upper, middle)
+        near_columns = [
+            column_pairs(tiles[t], base) + column_pairs(tiles[t], middle) for t in near
+        ]
+        lower_done, lower = eliminate_tile(tiles[second], middle)
+        store(lower_done, middle)
+        if not near:
+            break
+        lower_rows = row_pairs(lower)
+        upper = subtract_product(clear_lanes(upper, middle, end), back, lower_rows)
+        both_rows = row_pairs(upper) + lower_rows
+        for t, lead in zip(near, near_columns):
+            tiles[t] = subtract_product(clear_lanes(tiles[t], base, end), lead, both_rows)
+        if first + 4 < count:
+            upper_done = clear_lanes(upper_done, middle, end)
+            change = outer_product(
+                *(jnp.concatenate(pair, axis=0) for pair in zip(upper_done, lower_done))
+            )
+            for t in range(first + 4, count):
+                real, imag = clear_lanes(tiles[t], base, end)
+                part = change[t * TILE : (t + 1) * TILE]
+                tiles[t] = (real - part[:, :order], imag - part[:, order:])
 
 
 def factor_kernel(terms, *refs):
@@ -255,39 +334,54 @@
     )(*terms)
 
 
-def apply_kernel(own_ref, sent_ref, held_ref, out_ref):
-    part = own_ref.shape[0]
-    order = held_ref.shape[2]
+def apply_kernel(other, factor_ref, held_ref, *refs):
+    out_ref, value_ref, sems = refs[-3:]
+    part = factor_ref.shape[0]
     bit = lax.rem(lax.axis_index("space"), 2)
-    for which, source in ((bit, own_ref), (1 - bit, sent_ref)):
-        for slot in range(part):
-            f = which * part + slot
-            real, imag = source[slot, 0], source[slot, 1]
-            full = jnp.concatenate(
-                [
-                    jnp.concatenate([real, -imag], axis=1),
-                    jnp.concatenate([imag, real], axis=1),
-                ],
-                axis=0,
-            )
+    which = 1 - bit if other else bit
+    copies = []
+    for slot in range(part):
+        f = which * part + slot
+        real, imag = factor_ref[slot, 0], factor_ref[slot, 1]
+        data = held_ref[f].reshape(2 * held_ref.shape[2], held_ref.shape[3])
+        for p, full in enumerate(
+            (jnp.concatenate([real, -imag], axis=1), jnp.concatenate([imag, real], axis=1))
+        ):
             high = full.astype(jnp.bfloat16)
             low = (full - high.astype(jnp.float32)).astype(jnp.bfloat16)
-            data = held_ref[f].reshape(2 * order, held_ref.shape[3])
-            value = jnp.dot(high, data, preferred_element_type=jnp.float32) + jnp.dot(
+            value_ref[slot, p] = jnp.dot(high, data, preferred_element_type=jnp.float32) + jnp.dot(
                 low, data, preferred_element_type=jnp.float32
             )
-            out_ref[f] = value.reshape(held_ref.shape[1:])
-
-
-def apply(own, sent, held):
+            copies.append(
+                pltpu.make_async_copy(
+                    value_ref.at[slot, p], out_ref.at[f, p], sems.at[2 * slot + p]
+                )
+            )
+            copies[-1].start()
+    for copy in copies:
+        copy.wait()
+
+
+def apply(factor_part, held, earlier=None):
+    part = factor_part.shape[0]
+    operands = [factor_part, held]
+    aliases = {}
+    if earlier is not None:
+        aliases = {len(operands): 0}
+        operands.append(pltpu.with_memory_space_constraint(earlier, pltpu.HBM))
     return pl.pallas_call(
-        apply_kernel,
-        out_shape=jax.ShapeDtypeStruct(held.shape, jnp.float32),
-        in_specs=whole_vmem(3),
-        out_specs=pl.BlockSpec(memory_space=pltpu.VMEM),
+        functools.partial(apply_kernel, earlier is not None),
+        out_shape=pltpu.HBM(held.shape, jnp.float32),
+        in_specs=whole_vmem(2) + [pl.BlockSpec(memory_space=pltpu.HBM)] * len(aliases),
+        out_specs=pl.BlockSpec(memory_space=pltpu.HBM),
+        scratch_shapes=[
+            pltpu.VMEM((part,) + held.shape[1:], jnp.float32),
+            pltpu.SemaphoreType.DMA((2 * part,)),
+        ],
+        input_output_aliases=aliases,
         compiler_params=pltpu.CompilerParams(vmem_limit_bytes=VMEM_LIMIT),
         name="apply",
-    )(own, sent, held)
+    )(*operands)
 
 
 def swap(value, size, mask):
@@ -315,7 +409,8 @@
         terms = [total] + [swap(total, size, mask) for mask in masks]
         bit *= 4
     own = factor(terms)
-    return apply(own, swap(own, size, 1), held)
+    sent = swap(own, size, 1)
+    return apply(sent, held, apply(own, held))
 
 
 def solution(mesh):

time: 31.5 us -> 29.4 us (0.933)
  Pallas kernels: 9.31 us -> 8.16 us
  waiting for transfers between devices: 12.6 us -> 11.6 us
    pallas_call x1, Pallas kernels: 5.3 us -> 3.34 us  [factor(): pl.pallas_call(functools.partial(factor_kernel, len(terms)), out_shape=ja...]
    ppermute x6, waiting for transfers between devices: 9.1 us -> 8.13 us  [swap(): return lax.ppermute(value, 'space', [(i, i ^ mask) for i in range(size)])]
    pallas_call x1 -> x2, Pallas kernels: 1.11 us -> 1.92 us  [apply(): pl.pallas_call(functools.partial(apply_kernel, earlier is not None), out_...]
  transfers between devices with their start and end apart: 7 -> 7, of which waited for: 7 -> 7; matrix products, arithmetic and copies ran while one was open for 0% -> 0% of each run, Pallas kernels for 0% -> 3%
where the time goes in v5:
time: 29.4 us; the launch traced here: 29.2 us
  waiting for transfers between devices  11.6 us (39%)
  starting transfers between devices  9.38 us (32%)
  Pallas kernels  8.16 us (28%)
    ppermute x6, waiting for transfers between devices, swap(): return lax.ppermute(value, 'space', [(i, i ^ mask) for i in range(size)])  8.13 us
    ppermute x6, starting transfers between devices, swap(): return lax.ppermute(value, 'space', [(i, i ^ mask) for i in range(size)])  6.35 us
    ppermute x1, waiting for transfers between devices, local(): pieces = [mine, lax.ppermute(theirs, 'tm', [(0, 1), (1, 0)])]  3.5 us
    pallas_call x1, Pallas kernels, factor(): pl.pallas_call(functools.partial(factor_kernel, len(terms)), out_shape=ja...  3.34 us
    ppermute x1, starting transfers between devices, local(): pieces = [mine, lax.ppermute(theirs, 'tm', [(0, 1), (1, 0)])]  3.03 us
    pallas_call x1, Pallas kernels, project(): pl.pallas_call(functools.partial(project_kernel, groups), out_shape=[shap...  2.56 us
    pallas_call x2, Pallas kernels, apply(): pl.pallas_call(functools.partial(apply_kernel, earlier is not None), out_...  1.92 us
  transfers between devices with their start and end apart: 7, of which 7 were waited for; matrix products, arithmetic and copies ran while one was open for 0% of the time, Pallas kernels for 3%

profile of v5, /device:TPU:0, one launch (start us, length us, event | category | flops | bytes accessed | tf_op | source)
XLA Modules:
  0.0 29.2 jit_solution(13845985201666618811)
XLA Ops:
  0.0 2.6 %project.1 = (bf16[2,2,64,256]{3,2,1,0:T(8,128)(2,1)S(1)}, bf16[2,2,64,256]{3,2,1,0:T(8,128)(2,1)S(1)}) custom-call(s32[4]{0:T(128)} %freq_in.1, s32[1,64]{1,0:T(1,128)} %bitcast.1, bf16[64,128,256]{2,1,0:T(8,128)(2,1)} %snap_ref.1), custom_call_target="tpu_custom_call" | custom-call | tf_op jit(solution)/shard_map/project/pallas_call | solution.py:112
  2.6 3.0 %collective-permute-start = (bf16[2,2,64,256]{3,2,1,0:T(8,128)(2,1)S(1)}, bf16[2,2,64,256]{3,2,1,0:T(8,128)(2,1)S(1)}, u32[]{:S(2)}, u32[]{:S(2)}) collective-permute-start(bf16[2,2,64,256]{3,2,1,0:T(8,128)(2,1)S(1)} %get-tuple-element.11), channel_id=1, source_target_pairs={{0,16},{16,0},{1,17},{17,1},{2,18},{18,2},{3,19},{19,3},{4,20},{20... | collective-permute-start | bytes 393224 | tf_op jit(solution)/shard_map/ppermute | solution.py:397
  5.6 3.5 %collective-permute-done.refs_1_ = bf16[2,2,64,256]{3,2,1,0:T(8,128)(2,1)S(1)} collective-permute-done((bf16[2,2,64,256]{3,2,1,0:T(8,128)(2,1)S(1)}, bf16[2,2,64,256]{3,2,1,0:T(8,128)(2,1)S(1)}, u32[]{:S(2)}, u32[]{:S(2)}) %collective-permute-start) | collective-permute-done | bytes 131104 | tf_op jit(solution)/shard_map/ppermute | solution.py:397
  9.1 0.4 %gram.1 = (bf16[2,2,128,256]{3,2,1,0:T(8,128)(2,1)S(1)}, f32[1,128,128]{2,1,0:T(8,128)S(1)}, f32[1,128,128]{2,1,0:T(8,128)S(1)}) custom-call(bf16[2,2,64,256]{3,2,1,0:T(8,128)(2,1)S(1)} %get-tuple-element.10.refs_0_, bf16[2,2,64,256]{3,2,1,0:T(8,128)(2,1)S(1)} %collective-permute-done.refs_1_), custom_call_target="tpu_custom_call" | custom-call | tf_op jit(solution)/shard_map/gram/pallas_call | solution.py:158
  9.4 0.1 collective-permute-start.1
  9.5 1.2 %collective-permute-done.1 = f32[1,128,128]{2,1,0:T(8,128)S(1)} collective-permute-done((f32[1,128,128]{2,1,0:T(8,128)S(1)}, f32[1,128,128]{2,1,0:T(8,128)S(1)}, u32[]{:S(2)}, u32[]{:S(2)}) %collective-permute-start.1) | collective-permute-done | bytes 65568 | tf_op jit(solution)/shard_map/ppermute | solution.py:388
  10.8 2.8 %collective-permute-start.4 = (f32[1,128,128]{2,1,0:T(8,128)S(1)}, f32[1,128,128]{2,1,0:T(8,128)S(1)}, u32[]{:S(2)}, u32[]{:S(2)}) collective-permute-start(f32[1,128,128]{2,1,0:T(8,128)S(1)} %add.12), channel_id=1, source_target_pairs={{0,6},{1,7},{2,4},{3,5},{4,2},{5,3},{6,0},{7,1},{8,14},{9,15},{10,... | collective-permute-start | bytes 196616 | tf_op jit(solution)/shard_map/ppermute | solution.py:388
  13.6 0.4 %collective-permute-start.3 = (f32[1,128,128]{2,1,0:T(8,128)S(1)}, f32[1,128,128]{2,1,0:T(8,128)S(1)}, u32[]{:S(2)}, u32[]{:S(2)}) collective-permute-start(f32[1,128,128]{2,1,0:T(8,128)S(1)} %add.12), channel_id=1, source_target_pairs={{0,4},{1,5},{2,6},{3,7},{4,0},{5,1},{6,2},{7,3},{8,12},{9,13},{10,... | collective-permute-start | bytes 196616 | tf_op jit(solution)/shard_map/ppermute | solution.py:388
  14.0 0.3 %collective-permute-start.2 = (f32[1,128,128]{2,1,0:T(8,128)S(1)}, f32[1,128,128]{2,1,0:T(8,128)S(1)}, u32[]{:S(2)}, u32[]{:S(2)}) collective-permute-start(f32[1,128,128]{2,1,0:T(8,128)S(1)} %add.12), channel_id=1, source_target_pairs={{0,2},{1,3},{2,0},{3,1},{4,6},{5,7},{6,4},{7,5},{8,10},{9,11},{10,... | collective-permute-start | bytes 196616 | tf_op jit(solution)/shard_map/ppermute | solution.py:388
  14.3 1.7 %collective-permute-done.4 = f32[1,128,128]{2,1,0:T(8,128)S(1)} collective-permute-done((f32[1,128,128]{2,1,0:T(8,128)S(1)}, f32[1,128,128]{2,1,0:T(8,128)S(1)}, u32[]{:S(2)}, u32[]{:S(2)}) %collective-permute-start.4) | collective-permute-done | bytes 65568 | tf_op jit(solution)/shard_map/ppermute | solution.py:388
  16.0 1.8 %collective-permute-done.3 = f32[1,128,128]{2,1,0:T(8,128)S(1)} collective-permute-done((f32[1,128,128]{2,1,0:T(8,128)S(1)}, f32[1,128,128]{2,1,0:T(8,128)S(1)}, u32[]{:S(2)}, u32[]{:S(2)}) %collective-permute-start.3) | collective-permute-done | bytes 65568 | tf_op jit(solution)/shard_map/ppermute | solution.py:388
  17.8 0.4 %collective-permute-done.2 = f32[1,128,128]{2,1,0:T(8,128)S(1)} collective-permute-done((f32[1,128,128]{2,1,0:T(8,128)S(1)}, f32[1,128,128]{2,1,0:T(8,128)S(1)}, u32[]{:S(2)}, u32[]{:S(2)}) %collective-permute-start.2) | collective-permute-done | bytes 65568 | tf_op jit(solution)/shard_map/ppermute | solution.py:388
  18.3 2.7 %collective-permute-start.5 = (f32[1,128,128]{2,1,0:T(8,128)S(1)}, f32[1,128,128]{2,1,0:T(8,128)S(1)}, u32[]{:S(2)}, u32[]{:S(2)}) collective-permute-start(f32[1,128,128]{2,1,0:T(8,128)S(1)} %add_add_fusion.refs_0_), channel_id=1, source_target_pairs={{0,8},{1,9},{2,10},{3,11},{4,12},{5,13},{6,14},{7,15},{8,0},{9,1},... | collective-permute-start | bytes 196616 | tf_op jit(solution)/shard_map/ppermute | solution.py:388
  21.0 2.6 %collective-permute-done.5.refs_1_ = f32[1,128,128]{2,1,0:T(8,128)S(1)} collective-permute-done((f32[1,128,128]{2,1,0:T(8,128)S(1)}, f32[1,128,128]{2,1,0:T(8,128)S(1)}, u32[]{:S(2)}, u32[]{:S(2)}) %collective-permute-start.5) | collective-permute-done | bytes 65568 | tf_op jit(solution)/shard_map/ppermute | solution.py:388
  23.5 3.3 %factor.1.factor_ref = f32[1,2,128,128]{3,2,1,0:T(8,128)S(1)} custom-call(f32[1,128,128]{2,1,0:T(8,128)S(1)} %add_add_fusion.refs_0_, f32[1,128,128]{2,1,0:T(8,128)S(1)} %collective-permute-done.5.refs_1_), custom_call_target="tpu_custom_call" | custom-call | tf_op jit(solution)/shard_map/factor/pallas_call | solution.py:327
  26.9 0.1 collective-permute-start.6
  27.0 1.0 %apply.2.refs_0_ = f32[2,2,128,256]{3,2,1,0:T(8,128)} custom-call(f32[1,2,128,128]{3,2,1,0:T(8,128)S(1)} %factor.1.factor_ref, bf16[2,2,128,256]{3,2,1,0:T(8,128)(2,1)S(1)} %get-tuple-element.14.held_ref), custom_call_target="tpu_custom_call" | custom-call | tf_op jit(solution)/shard_map/apply/pallas_call | solution.py:372
  27.9 0.4 %collective-permute-done.6.factor_ref = f32[1,2,128,128]{3,2,1,0:T(8,128)S(1)} collective-permute-done((f32[1,2,128,128]{3,2,1,0:T(8,128)S(1)}, f32[1,2,128,128]{3,2,1,0:T(8,128)S(1)}, u32[]{:S(2)}, u32[]{:S(2)}) %collective-permute-start.6) | collective-permute-done | bytes 131104 | tf_op jit(solution)/shard_map/ppermute | solution.py:388
  28.3 1.0 %apply.3 = f32[2,2,128,256]{3,2,1,0:T(8,128)} custom-call(f32[1,2,128,128]{3,2,1,0:T(8,128)S(1)} %collective-permute-done.6.factor_ref, bf16[2,2,128,256]{3,2,1,0:T(8,128)(2,1)S(1)} %get-tuple-element.14.held_ref, f32[2,2,128,256]{3,2,1,0:T(8,128)} %apply.2.refs_0_), custom_call_target="tpu_custom_call", output_to_operand_aliasing={{}: (2, {})} | custom-call | tf_op jit(solution)/shard_map/apply/pallas_call | solution.py:372
  (2 shorter events, 0.0 us)
Async XLA Ops:
  2.6 6.5 %collective-permute-start = (bf16[2,2,64,256]{3,2,1,0:T(8,128)(2,1)S(1)}, bf16[2,2,64,256]{3,2,1,0:T(8,128)(2,1)S(1)}, u32[]{:S(2)}, u32[]{:S(2)}) collective-permute-start(bf16[2,2,64,256]{3,2,1,0:T(8,128)(2,1)S(1)} %get-tuple-element.11), channel_id=1, source_target_pairs={{0,16},{16,0},{1,17},{17,1},{2,18},{18,2},{3,19},{19,3},{4,20},{20... | collective-permute-start | bytes 393224 | tf_op jit(solution)/shard_map/ppermute | solution.py:397
  9.4 1.3 %collective-permute-start.1 = (f32[1,128,128]{2,1,0:T(8,128)S(1)}, f32[1,128,128]{2,1,0:T(8,128)S(1)}, u32[]{:S(2)}, u32[]{:S(2)}) collective-permute-start(f32[1,128,128]{2,1,0:T(8,128)S(1)} %get-tuple-element.13), channel_id=1, source_target_pairs={{0,1},{1,0},{2,3},{3,2},{4,5},{5,4},{6,7},{7,6},{8,9},{9,8},{10,11... | collective-permute-start | bytes 196616 | tf_op jit(solution)/shard_map/ppermute | solution.py:388
  10.8 5.2 %collective-permute-start.4 = (f32[1,128,128]{2,1,0:T(8,128)S(1)}, f32[1,128,128]{2,1,0:T(8,128)S(1)}, u32[]{:S(2)}, u32[]{:S(2)}) collective-permute-start(f32[1,128,128]{2,1,0:T(8,128)S(1)} %add.12), channel_id=1, source_target_pairs={{0,6},{1,7},{2,4},{3,5},{4,2},{5,3},{6,0},{7,1},{8,14},{9,15},{10,... | collective-permute-start | bytes 196616 | tf_op jit(solution)/shard_map/ppermute | solution.py:388
  13.6 4.3 %collective-permute-start.3 = (f32[1,128,128]{2,1,0:T(8,128)S(1)}, f32[1,128,128]{2,1,0:T(8,128)S(1)}, u32[]{:S(2)}, u32[]{:S(2)}) collective-permute-start(f32[1,128,128]{2,1,0:T(8,128)S(1)} %add.12), channel_id=1, source_target_pairs={{0,4},{1,5},{2,6},{3,7},{4,0},{5,1},{6,2},{7,3},{8,12},{9,13},{10,... | collective-permute-start | bytes 196616 | tf_op jit(solution)/shard_map/ppermute | solution.py:388
  14.0 4.3 %collective-permute-start.2 = (f32[1,128,128]{2,1,0:T(8,128)S(1)}, f32[1,128,128]{2,1,0:T(8,128)S(1)}, u32[]{:S(2)}, u32[]{:S(2)}) collective-permute-start(f32[1,128,128]{2,1,0:T(8,128)S(1)} %add.12), channel_id=1, source_target_pairs={{0,2},{1,3},{2,0},{3,1},{4,6},{5,7},{6,4},{7,5},{8,10},{9,11},{10,... | collective-permute-start | bytes 196616 | tf_op jit(solution)/shard_map/ppermute | solution.py:388
  18.3 5.2 %collective-permute-start.5 = (f32[1,128,128]{2,1,0:T(8,128)S(1)}, f32[1,128,128]{2,1,0:T(8,128)S(1)}, u32[]{:S(2)}, u32[]{:S(2)}) collective-permute-start(f32[1,128,128]{2,1,0:T(8,128)S(1)} %add_add_fusion.refs_0_), channel_id=1, source_target_pairs={{0,8},{1,9},{2,10},{3,11},{4,12},{5,13},{6,14},{7,15},{8,0},{9,1},... | collective-permute-start | bytes 196616 | tf_op jit(solution)/shard_map/ppermute | solution.py:388
  26.9 1.4 %collective-permute-start.6 = (f32[1,2,128,128]{3,2,1,0:T(8,128)S(1)}, f32[1,2,128,128]{3,2,1,0:T(8,128)S(1)}, u32[]{:S(2)}, u32[]{:S(2)}) collective-permute-start(f32[1,2,128,128]{3,2,1,0:T(8,128)S(1)} %factor.1.factor_ref), channel_id=1, source_target_pairs={{0,1},{1,0},{2,3},{3,2},{4,5},{5,4},{6,7},{7,6},{8,9},{9,8},{10,11... | collective-permute-start | bytes 393224 | tf_op jit(solution)/shard_map/ppermute | solution.py:388

commit v6 on v5

--- a/solution.py
+++ b/solution.py
@@ -26,7 +26,8 @@
 
 
 def project_kernel(groups, freq_in, offset_in, snap_ref, *refs):
-    outs, (freq_ref, offset_ref, held, sems) = refs[:groups], refs[groups:]
+    outs, tails = refs[:groups], refs[groups:-4]
+    freq_ref, offset_ref, held, sems = refs[-4:]
     blocks, length, cells = snap_ref.shape
     chunks = blocks // TILE
     small = [
@@ -45,8 +46,13 @@
         copy.wait()
     count = freq_ref.shape[0]
     per_group = count // groups
+    part = per_group // 2
     first = lax.axis_index("tm") * per_group if groups > 1 else 0
-    picked = [freq_ref[lax.rem(first + j, count)] for j in range(count)]
+    flip = lax.rem(lax.axis_index("space"), 2) * part if groups > 1 else 0
+    picked = [
+        freq_ref[lax.rem(first + j - j % per_group + lax.rem(j + flip, per_group), count)]
+        for j in range(count)
+    ]
 
     def turned(moments):
         row = rows_of((2 * count, moments.shape[1]))
@@ -95,25 +101,30 @@
         for j in range(count):
             for p in range(2):
                 value = jnp.concatenate([pairs[j][p] for pairs in parts], axis=0)
-                target = outs[j // per_group]
-                target[j % per_group, p, step * CHUNK : (step + 1) * CHUNK, :] = value.astype(
-                    jnp.bfloat16
-                )
+                value = value.astype(jnp.bfloat16)
+                group, slot = divmod(j, per_group)
+                place = slice(step * CHUNK, (step + 1) * CHUNK)
+                outs[group][slot, p, place, :] = value
+                if groups > 1 and slot >= part:
+                    tails[group][slot - part, p, place, :] = value
 
 
 def project(snapshots, frequencies, offsets, groups):
     blocks, length, cells = snapshots.shape
     count = frequencies.shape[0]
-    shape = pltpu.VMEM((count // groups, 2, blocks, cells), jnp.bfloat16)
+    per_group = count // groups
+    shapes = [pltpu.VMEM((per_group, 2, blocks, cells), jnp.bfloat16)] * groups
+    if groups > 1:
+        shapes += [pltpu.VMEM((per_group // 2, 2, blocks, cells), jnp.bfloat16)] * groups
     operands = [
         pltpu.with_memory_space_constraint(operand, pltpu.HBM)
         for operand in (frequencies, offsets.reshape(1, blocks), snapshots)
     ]
     return pl.pallas_call(
         functools.partial(project_kernel, groups),
-        out_shape=[shape] * groups,
+        out_shape=shapes,
         in_specs=[pl.BlockSpec(memory_space=pltpu.HBM)] * 3,
-        out_specs=whole_vmem(groups),
+        out_specs=whole_vmem(len(shapes)),
         scratch_shapes=[
             pltpu.SMEM((count,), jnp.int32),
             pltpu.VMEM((1, blocks), jnp.int32),
@@ -126,46 +137,41 @@
 
 
 def gram_kernel(halves, scale, *refs):
-    pieces = refs[:halves]
-    held_ref, keep_ref, send_ref, packed = refs[halves:]
-    count = held_ref.shape[0]
+    own, beside = refs[:halves], refs[halves : 2 * halves]
+    held_ref, packed_ref, other = refs[2 * halves :]
     order = held_ref.shape[2]
     first = lax.axis_index("tm") if halves > 1 else 0
     size = order // halves
     for h in range(halves):
         place = pl.ds(pl.multiple_of(lax.rem(first + h, halves) * size, size), size)
-        held_ref[:, :, place, :] = pieces[h][...]
+        held_ref[:, :, place, :] = own[h][...]
+        other[:, :, place, :] = beside[h][...]
     lower = rows_of((order, order)) >= lanes_of((order, order))
     turn = (((1,), (1,)), ((), ()))
-    for f in range(count):
-        real, imag = held_ref[f, 0], held_ref[f, 1]
+    for f in range(other.shape[0]):
+        real = jnp.concatenate([held_ref[f, 0], other[f, 0]], axis=1)
+        imag = jnp.concatenate([held_ref[f, 1], other[f, 1]], axis=1)
         both = jnp.concatenate([real, imag], axis=1)
         crossed = jnp.concatenate([imag, -real], axis=1)
         gram_real = lax.dot_general(both, both, turn, preferred_element_type=jnp.float32)
         gram_imag = lax.dot_general(crossed, both, turn, preferred_element_type=jnp.float32)
-        packed[f] = jnp.where(lower, gram_real, gram_imag) * scale
-    bit = lax.rem(lax.axis_index("space"), 2)
-    part = count // 2
-    keep_ref[...] = packed[pl.ds(bit * part, part)]
-    send_ref[...] = packed[pl.ds((1 - bit) * part, part)]
-
-
-def gram(pieces, halves, scale):
-    count, _, size, cells = pieces[0].shape
+        packed_ref[f] = jnp.where(lower, gram_real, gram_imag) * scale
+
+
+def gram(own, beside, scale):
+    halves = len(own)
+    count, _, size, cells = own[0].shape
     order = size * halves
     held = jax.ShapeDtypeStruct((count, 2, order, cells), jnp.bfloat16)
-    half = jax.ShapeDtypeStruct((count // 2, order, order), jnp.float32)
     return pl.pallas_call(
         functools.partial(gram_kernel, halves, scale),
-        out_shape=[held, half, half],
-        in_specs=whole_vmem(len(pieces)),
-        out_specs=whole_vmem(3),
-        scratch_shapes=[
-            pltpu.VMEM((count, order, order), jnp.float32),
-        ],
+        out_shape=[held, jax.ShapeDtypeStruct((count // 2, order, order), jnp.float32)],
+        in_specs=whole_vmem(2 * halves),
+        out_specs=whole_vmem(2),
+        scratch_shapes=[pltpu.VMEM((count // 2,) + held.shape[1:], held.dtype)],
         compiler_params=pltpu.CompilerParams(vmem_limit_bytes=VMEM_LIMIT),
         name="gram",
-    )(*pieces)
+    )(*own, *beside)
 
 
 def spread_row(tile, p):
@@ -343,7 +349,7 @@
     for slot in range(part):
         f = which * part + slot
         real, imag = factor_ref[slot, 0], factor_ref[slot, 1]
-        data = held_ref[f].reshape(2 * held_ref.shape[2], held_ref.shape[3])
+        data = held_ref[part * other + slot].reshape(2 * held_ref.shape[2], held_ref.shape[3])
         for p, full in enumerate(
             (jnp.concatenate([real, -imag], axis=1), jnp.concatenate([imag, real], axis=1))
         ):
@@ -388,19 +394,26 @@
     return lax.ppermute(value, "space", [(i, i ^ mask) for i in range(size)])
 
 
+def swap_corner(value, size):
+    pairs = [(t * size + i, (1 - t) * size + (i ^ 1)) for t in range(2) for i in range(size)]
+    return lax.ppermute(value, ("tm", "space"), pairs)
+
+
 def local(snapshots, frequencies, offsets):
-    halves = lax.axis_size("tm")
     size = lax.axis_size("space")
     scale = 1.0 / (snapshots.shape[2] * size)
-    if halves == 2:
-        mine, theirs = project(snapshots, frequencies, offsets, 2)
-        pieces = [mine, lax.ppermute(theirs, "tm", [(0, 1), (1, 0)])]
-        held, keep, send = gram(pieces, 2, scale)
+    if lax.axis_size("tm") == 2:
+        mine, theirs, mine_tail, theirs_tail = project(snapshots, frequencies, offsets, 2)
+        own = [mine, lax.ppermute(theirs, "tm", [(0, 1), (1, 0)])]
+        beside = [swap(mine_tail, size, 1), swap_corner(theirs_tail, size)]
     else:
         (coeffs,) = project(snapshots, frequencies, offsets, 1)
         regrouped = lax.all_to_all(coeffs, "tm", split_axis=0, concat_axis=2, tiled=True)
-        held, keep, send = gram([regrouped], 1, scale)
-    total = keep + swap(send, size, 1)
+        part = regrouped.shape[0] // 2
+        flipped = jnp.roll(regrouped, part, axis=0)
+        own = [jnp.where(lax.axis_index("space") % 2 == 0, regrouped, flipped)]
+        beside = [swap(own[0][part:], size, 1)]
+    held, total = gram(own, beside, scale)
     terms = [total]
     bit = 2
     while bit < size:

time: 29.4 us -> 28.9 us (0.983)
  waiting for transfers between devices: 11.6 us -> 11 us
    ppermute x6, waiting for transfers between devices: 8.13 us -> 7.83 us  [swap(): return lax.ppermute(value, 'space', [(i, i ^ mask) for i in range(size)])]
    ppermute x1 -> x2, waiting for transfers between devices: 3.5 us -> 3.2 us  [the longest x1 3.2 us: swap_corner(): return lax.ppermute(value, ('tm', 'space'), pairs)]
    ppermute x1 -> x2, starting transfers between devices: 3.03 us -> 3.24 us  [the longest x1 3.03 us: local(): own = [mine, lax.ppermute(theirs, 'tm', [(0, 1), (1, 0)])]]
  transfers between devices with their start and end apart: 7 -> 8, of which waited for: 7 -> 7; matrix products, arithmetic and copies ran while one was open for 0% -> 0% of each run, Pallas kernels for 3% -> 3%
where the time goes in v6:
time: 28.9 us; the launch traced here: 28.7 us
  waiting for transfers between devices  11 us (38%)
  starting transfers between devices  9.52 us (33%)
  Pallas kernels  8.13 us (28%)
    ppermute x6, waiting for transfers between devices, swap(): return lax.ppermute(value, 'space', [(i, i ^ mask) for i in range(size)])  7.83 us
    ppermute x6, starting transfers between devices, swap(): return lax.ppermute(value, 'space', [(i, i ^ mask) for i in range(size)])  6.28 us
    pallas_call x1, Pallas kernels, factor(): pl.pallas_call(functools.partial(factor_kernel, len(terms)), out_shape=ja...  3.34 us
    ppermute x1, waiting for transfers between devices, swap_corner(): return lax.ppermute(value, ('tm', 'space'), pairs)  3.2 us
    ppermute x1, starting transfers between devices, local(): own = [mine, lax.ppermute(theirs, 'tm', [(0, 1), (1, 0)])]  3.03 us
    pallas_call x1, Pallas kernels, project(): pl.pallas_call(functools.partial(project_kernel, groups), out_shape=shape...  2.56 us
    pallas_call x2, Pallas kernels, apply(): pl.pallas_call(functools.partial(apply_kernel, earlier is not None), out_...  1.9 us
  transfers between devices with their start and end apart: 8, of which 7 were waited for; matrix products, arithmetic and copies ran while one was open for 0% of the time, Pallas kernels for 3%

profile of v6, /device:TPU:0, one launch (start us, length us, event | category | flops | bytes accessed | tf_op | source)
XLA Modules:
  0.0 28.7 jit_solution(16665597400555112726)
XLA Ops:
  0.0 2.6 %project.1 = (bf16[2,2,64,256]{3,2,1,0:T(8,128)(2,1)S(1)}, bf16[2,2,64,256]{3,2,1,0:T(8,128)(2,1)S(1)}, bf16[1,2,64,256]{3,2,1,0:T(8,128)(2,1)S(1)}, bf16[1,2,64,256]{3,2,1,0:T(8,128)(2,1)S(1)}) custom-call(s32[4]{0:T(128)} %freq_in.1, s32[1,64]{1,0:T(1,128)} %bitcast.1, bf16[64,128,256]{2,1,0:T(8,128)(2,1)} %snap_ref.1), custom_call_target="tpu_custom_call" | custom-call | tf_op jit(solution)/shard_map/project/pallas_call | solution.py:123
  2.6 3.0 %collective-permute-start = (bf16[2,2,64,256]{3,2,1,0:T(8,128)(2,1)S(1)}, bf16[2,2,64,256]{3,2,1,0:T(8,128)(2,1)S(1)}, u32[]{:S(2)}, u32[]{:S(2)}) collective-permute-start(bf16[2,2,64,256]{3,2,1,0:T(8,128)(2,1)S(1)} %get-tuple-element.12), channel_id=1, source_target_pairs={{0,16},{16,0},{1,17},{17,1},{2,18},{18,2},{3,19},{19,3},{4,20},{20... | collective-permute-start | bytes 393224 | tf_op jit(solution)/shard_map/ppermute | solution.py:407
  5.6 0.0 collective-permute-start.1
  5.6 0.2 collective-permute-start.2
  5.8 1.0 %collective-permute-done.1.refs_2_ = bf16[1,2,64,256]{3,2,1,0:T(8,128)(2,1)S(1)} collective-permute-done((bf16[1,2,64,256]{3,2,1,0:T(8,128)(2,1)S(1)}, bf16[1,2,64,256]{3,2,1,0:T(8,128)(2,1)S(1)}, u32[]{:S(2)}, u32[]{:S(2)}) %collective-permute-start.1) | collective-permute-done | bytes 65568 | tf_op jit(solution)/shard_map/ppermute | solution.py:394
  6.9 3.2 %collective-permute-done.2.refs_3_ = bf16[1,2,64,256]{3,2,1,0:T(8,128)(2,1)S(1)} collective-permute-done((bf16[1,2,64,256]{3,2,1,0:T(8,128)(2,1)S(1)}, bf16[1,2,64,256]{3,2,1,0:T(8,128)(2,1)S(1)}, u32[]{:S(2)}, u32[]{:S(2)}) %collective-permute-start.2) | collective-permute-done | bytes 65568 | tf_op jit(solution)/shard_map/ppermute | solution.py:399
  10.1 0.0 collective-permute-done.refs_1_
  10.1 0.3 %gram.1 = (bf16[2,2,128,256]{3,2,1,0:T(8,128)(2,1)S(1)}, f32[1,128,128]{2,1,0:T(8,128)S(1)}) custom-call(bf16[2,2,64,256]{3,2,1,0:T(8,128)(2,1)S(1)} %get-tuple-element.11.refs_0_, bf16[2,2,64,256]{3,2,1,0:T(8,128)(2,1)S(1)} %collective-permute-done.refs_1_, bf16[1,2,64,256]{3,2,1,0:T(8,128)(2,1)S(1)} %collective-permute-done.1.refs_2_, ...), custom_call_target="tpu_custom_call" | custom-call | tf_op jit(solution)/shard_map/gram/pallas_call | solution.py:166
  10.4 2.5 %collective-permute-start.5 = (f32[1,128,128]{2,1,0:T(8,128)S(1)}, f32[1,128,128]{2,1,0:T(8,128)S(1)}, u32[]{:S(2)}, u32[]{:S(2)}) collective-permute-start(f32[1,128,128]{2,1,0:T(8,128)S(1)} %get-tuple-element.15), channel_id=1, source_target_pairs={{0,6},{1,7},{2,4},{3,5},{4,2},{5,3},{6,0},{7,1},{8,14},{9,15},{10,... | collective-permute-start | bytes 196616 | tf_op jit(solution)/shard_map/ppermute | solution.py:394
  12.9 0.4 %collective-permute-start.4 = (f32[1,128,128]{2,1,0:T(8,128)S(1)}, f32[1,128,128]{2,1,0:T(8,128)S(1)}, u32[]{:S(2)}, u32[]{:S(2)}) collective-permute-start(f32[1,128,128]{2,1,0:T(8,128)S(1)} %get-tuple-element.15), channel_id=1, source_target_pairs={{0,4},{1,5},{2,6},{3,7},{4,0},{5,1},{6,2},{7,3},{8,12},{9,13},{10,... | collective-permute-start | bytes 196616 | tf_op jit(solution)/shard_map/ppermute | solution.py:394
  13.4 0.6 %collective-permute-start.3 = (f32[1,128,128]{2,1,0:T(8,128)S(1)}, f32[1,128,128]{2,1,0:T(8,128)S(1)}, u32[]{:S(2)}, u32[]{:S(2)}) collective-permute-start(f32[1,128,128]{2,1,0:T(8,128)S(1)} %get-tuple-element.15), channel_id=1, source_target_pairs={{0,2},{1,3},{2,0},{3,1},{4,6},{5,7},{6,4},{7,5},{8,10},{9,11},{10,... | collective-permute-start | bytes 196616 | tf_op jit(solution)/shard_map/ppermute | solution.py:394
  14.0 1.8 %collective-permute-done.5 = f32[1,128,128]{2,1,0:T(8,128)S(1)} collective-permute-done((f32[1,128,128]{2,1,0:T(8,128)S(1)}, f32[1,128,128]{2,1,0:T(8,128)S(1)}, u32[]{:S(2)}, u32[]{:S(2)}) %collective-permute-start.5) | collective-permute-done | bytes 65568 | tf_op jit(solution)/shard_map/ppermute | solution.py:394
  15.7 1.6 %collective-permute-done.4 = f32[1,128,128]{2,1,0:T(8,128)S(1)} collective-permute-done((f32[1,128,128]{2,1,0:T(8,128)S(1)}, f32[1,128,128]{2,1,0:T(8,128)S(1)}, u32[]{:S(2)}, u32[]{:S(2)}) %collective-permute-start.4) | collective-permute-done | bytes 65568 | tf_op jit(solution)/shard_map/ppermute | solution.py:394
  17.3 0.4 %collective-permute-done.3 = f32[1,128,128]{2,1,0:T(8,128)S(1)} collective-permute-done((f32[1,128,128]{2,1,0:T(8,128)S(1)}, f32[1,128,128]{2,1,0:T(8,128)S(1)}, u32[]{:S(2)}, u32[]{:S(2)}) %collective-permute-start.3) | collective-permute-done | bytes 65568 | tf_op jit(solution)/shard_map/ppermute | solution.py:394
  17.7 2.7 %collective-permute-start.6 = (f32[1,128,128]{2,1,0:T(8,128)S(1)}, f32[1,128,128]{2,1,0:T(8,128)S(1)}, u32[]{:S(2)}, u32[]{:S(2)}) collective-permute-start(f32[1,128,128]{2,1,0:T(8,128)S(1)} %add_add_fusion.refs_0_), channel_id=1, source_target_pairs={{0,8},{1,9},{2,10},{3,11},{4,12},{5,13},{6,14},{7,15},{8,0},{9,1},... | collective-permute-start | bytes 196616 | tf_op jit(solution)/shard_map/ppermute | solution.py:394
  20.3 2.7 %collective-permute-done.6.refs_1_ = f32[1,128,128]{2,1,0:T(8,128)S(1)} collective-permute-done((f32[1,128,128]{2,1,0:T(8,128)S(1)}, f32[1,128,128]{2,1,0:T(8,128)S(1)}, u32[]{:S(2)}, u32[]{:S(2)}) %collective-permute-start.6) | collective-permute-done | bytes 65568 | tf_op jit(solution)/shard_map/ppermute | solution.py:394
  23.0 3.3 %factor.1.factor_ref = f32[1,2,128,128]{3,2,1,0:T(8,128)S(1)} custom-call(f32[1,128,128]{2,1,0:T(8,128)S(1)} %add_add_fusion.refs_0_, f32[1,128,128]{2,1,0:T(8,128)S(1)} %collective-permute-done.6.refs_1_), custom_call_target="tpu_custom_call" | custom-call | tf_op jit(solution)/shard_map/factor/pallas_call | solution.py:333
  26.4 0.1 collective-permute-start.7
  26.5 0.9 %apply.2.refs_0_ = f32[2,2,128,256]{3,2,1,0:T(8,128)} custom-call(f32[1,2,128,128]{3,2,1,0:T(8,128)S(1)} %factor.1.factor_ref, bf16[2,2,128,256]{3,2,1,0:T(8,128)(2,1)S(1)} %get-tuple-element.16.held_ref), custom_call_target="tpu_custom_call" | custom-call | tf_op jit(solution)/shard_map/apply/pallas_call | solution.py:378
  27.4 0.4 %collective-permute-done.7.factor_ref = f32[1,2,128,128]{3,2,1,0:T(8,128)S(1)} collective-permute-done((f32[1,2,128,128]{3,2,1,0:T(8,128)S(1)}, f32[1,2,128,128]{3,2,1,0:T(8,128)S(1)}, u32[]{:S(2)}, u32[]{:S(2)}) %collective-permute-start.7) | collective-permute-done | bytes 131104 | tf_op jit(solution)/shard_map/ppermute | solution.py:394
  27.8 0.9 %apply.3 = f32[2,2,128,256]{3,2,1,0:T(8,128)} custom-call(f32[1,2,128,128]{3,2,1,0:T(8,128)S(1)} %collective-permute-done.7.factor_ref, bf16[2,2,128,256]{3,2,1,0:T(8,128)(2,1)S(1)} %get-tuple-element.16.held_ref, f32[2,2,128,256]{3,2,1,0:T(8,128)} %apply.2.refs_0_), custom_call_target="tpu_custom_call", output_to_operand_aliasing={{}: (2, {})} | custom-call | tf_op jit(solution)/shard_map/apply/pallas_call | solution.py:378
  (1 shorter events, 0.0 us)
Async XLA Ops:
  2.6 7.5 %collective-permute-start = (bf16[2,2,64,256]{3,2,1,0:T(8,128)(2,1)S(1)}, bf16[2,2,64,256]{3,2,1,0:T(8,128)(2,1)S(1)}, u32[]{:S(2)}, u32[]{:S(2)}) collective-permute-start(bf16[2,2,64,256]{3,2,1,0:T(8,128)(2,1)S(1)} %get-tuple-element.12), channel_id=1, source_target_pairs={{0,16},{16,0},{1,17},{17,1},{2,18},{18,2},{3,19},{19,3},{4,20},{20... | collective-permute-start | bytes 393224 | tf_op jit(solution)/shard_map/ppermute | solution.py:407
  5.6 1.3 %collective-permute-start.1 = (bf16[1,2,64,256]{3,2,1,0:T(8,128)(2,1)S(1)}, bf16[1,2,64,256]{3,2,1,0:T(8,128)(2,1)S(1)}, u32[]{:S(2)}, u32[]{:S(2)}) collective-permute-start(bf16[1,2,64,256]{3,2,1,0:T(8,128)(2,1)S(1)} %get-tuple-element.13), channel_id=1, source_target_pairs={{0,1},{1,0},{2,3},{3,2},{4,5},{5,4},{6,7},{7,6},{8,9},{9,8},{10,11... | collective-permute-start | bytes 196616 | tf_op jit(solution)/shard_map/ppermute | solution.py:394
  5.6 4.4 %collective-permute-start.2 = (bf16[1,2,64,256]{3,2,1,0:T(8,128)(2,1)S(1)}, bf16[1,2,64,256]{3,2,1,0:T(8,128)(2,1)S(1)}, u32[]{:S(2)}, u32[]{:S(2)}) collective-permute-start(bf16[1,2,64,256]{3,2,1,0:T(8,128)(2,1)S(1)} %get-tuple-element.14), channel_id=1, source_target_pairs={{0,17},{1,16},{2,19},{3,18},{4,21},{5,20},{6,23},{7,22},{8,25},{9,... | collective-permute-start | bytes 196616 | tf_op jit(solution)/shard_map/ppermute | solution.py:399
  10.4 5.3 %collective-permute-start.5 = (f32[1,128,128]{2,1,0:T(8,128)S(1)}, f32[1,128,128]{2,1,0:T(8,128)S(1)}, u32[]{:S(2)}, u32[]{:S(2)}) collective-permute-start(f32[1,128,128]{2,1,0:T(8,128)S(1)} %get-tuple-element.15), channel_id=1, source_target_pairs={{0,6},{1,7},{2,4},{3,5},{4,2},{5,3},{6,0},{7,1},{8,14},{9,15},{10,... | collective-permute-start | bytes 196616 | tf_op jit(solution)/shard_map/ppermute | solution.py:394
  12.9 4.4 %collective-permute-start.4 = (f32[1,128,128]{2,1,0:T(8,128)S(1)}, f32[1,128,128]{2,1,0:T(8,128)S(1)}, u32[]{:S(2)}, u32[]{:S(2)}) collective-permute-start(f32[1,128,128]{2,1,0:T(8,128)S(1)} %get-tuple-element.15), channel_id=1, source_target_pairs={{0,4},{1,5},{2,6},{3,7},{4,0},{5,1},{6,2},{7,3},{8,12},{9,13},{10,... | collective-permute-start | bytes 196616 | tf_op jit(solution)/shard_map/ppermute | solution.py:394
  13.4 4.3 %collective-permute-start.3 = (f32[1,128,128]{2,1,0:T(8,128)S(1)}, f32[1,128,128]{2,1,0:T(8,128)S(1)}, u32[]{:S(2)}, u32[]{:S(2)}) collective-permute-start(f32[1,128,128]{2,1,0:T(8,128)S(1)} %get-tuple-element.15), channel_id=1, source_target_pairs={{0,2},{1,3},{2,0},{3,1},{4,6},{5,7},{6,4},{7,5},{8,10},{9,11},{10,... | collective-permute-start | bytes 196616 | tf_op jit(solution)/shard_map/ppermute | solution.py:394
  17.7 5.4 %collective-permute-start.6 = (f32[1,128,128]{2,1,0:T(8,128)S(1)}, f32[1,128,128]{2,1,0:T(8,128)S(1)}, u32[]{:S(2)}, u32[]{:S(2)}) collective-permute-start(f32[1,128,128]{2,1,0:T(8,128)S(1)} %add_add_fusion.refs_0_), channel_id=1, source_target_pairs={{0,8},{1,9},{2,10},{3,11},{4,12},{5,13},{6,14},{7,15},{8,0},{9,1},... | collective-permute-start | bytes 196616 | tf_op jit(solution)/shard_map/ppermute | solution.py:394
  26.4 1.4 %collective-permute-start.7 = (f32[1,2,128,128]{3,2,1,0:T(8,128)S(1)}, f32[1,2,128,128]{3,2,1,0:T(8,128)S(1)}, u32[]{:S(2)}, u32[]{:S(2)}) collective-permute-start(f32[1,2,128,128]{3,2,1,0:T(8,128)S(1)} %factor.1.factor_ref), channel_id=1, source_target_pairs={{0,1},{1,0},{2,3},{3,2},{4,5},{5,4},{6,7},{7,6},{8,9},{9,8},{10,11... | collective-permute-start | bytes 393224 | tf_op jit(solution)/shard_map/ppermute | solution.py:394

commit v7 on v6

--- a/solution.py
+++ b/solution.py
@@ -26,7 +26,7 @@
 
 
 def project_kernel(groups, freq_in, offset_in, snap_ref, *refs):
-    outs, tails = refs[:groups], refs[groups:-4]
+    outs = refs[:-4]
     freq_ref, offset_ref, held, sems = refs[-4:]
     blocks, length, cells = snap_ref.shape
     chunks = blocks // TILE
@@ -102,20 +102,16 @@
             for p in range(2):
                 value = jnp.concatenate([pairs[j][p] for pairs in parts], axis=0)
                 value = value.astype(jnp.bfloat16)
-                group, slot = divmod(j, per_group)
-                place = slice(step * CHUNK, (step + 1) * CHUNK)
-                outs[group][slot, p, place, :] = value
-                if groups > 1 and slot >= part:
-                    tails[group][slot - part, p, place, :] = value
+                target = outs[j * len(outs) // count]
+                slot = j % (count // len(outs))
+                target[slot, p, step * CHUNK : (step + 1) * CHUNK, :] = value
 
 
 def project(snapshots, frequencies, offsets, groups):
     blocks, length, cells = snapshots.shape
     count = frequencies.shape[0]
-    per_group = count // groups
-    shapes = [pltpu.VMEM((per_group, 2, blocks, cells), jnp.bfloat16)] * groups
-    if groups > 1:
-        shapes += [pltpu.VMEM((per_group // 2, 2, blocks, cells), jnp.bfloat16)] * groups
+    pieces = 2 * groups if groups > 1 else 1
+    shapes = [pltpu.VMEM((count // pieces, 2, blocks, cells), jnp.bfloat16)] * pieces
     operands = [
         pltpu.with_memory_space_constraint(operand, pltpu.HBM)
         for operand in (frequencies, offsets.reshape(1, blocks), snapshots)
@@ -136,16 +132,20 @@
     )(*operands)
 
 
+def assemble(pieces, target):
+    halves = len(pieces)
+    size = pieces[0].shape[2]
+    first = lax.axis_index("tm") if halves > 1 else 0
+    for h, piece in enumerate(pieces):
+        place = pl.ds(pl.multiple_of(lax.rem(first + h, halves) * size, size), size)
+        target[:, :, place, :] = piece[...]
+
+
 def gram_kernel(halves, scale, *refs):
-    own, beside = refs[:halves], refs[halves : 2 * halves]
     held_ref, packed_ref, other = refs[2 * halves :]
     order = held_ref.shape[2]
-    first = lax.axis_index("tm") if halves > 1 else 0
-    size = order // halves
-    for h in range(halves):
-        place = pl.ds(pl.multiple_of(lax.rem(first + h, halves) * size, size), size)
-        held_ref[:, :, place, :] = own[h][...]
-        other[:, :, place, :] = beside[h][...]
+    assemble(refs[:halves], held_ref)
+    assemble(refs[halves : 2 * halves], other)
     lower = rows_of((order, order)) >= lanes_of((order, order))
     turn = (((1,), (1,)), ((), ()))
     for f in range(other.shape[0]):
@@ -160,15 +160,15 @@
 
 def gram(own, beside, scale):
     halves = len(own)
-    count, _, size, cells = own[0].shape
+    part, _, size, cells = own[0].shape
     order = size * halves
-    held = jax.ShapeDtypeStruct((count, 2, order, cells), jnp.bfloat16)
+    held = jax.ShapeDtypeStruct((part, 2, order, cells), jnp.bfloat16)
     return pl.pallas_call(
         functools.partial(gram_kernel, halves, scale),
-        out_shape=[held, jax.ShapeDtypeStruct((count // 2, order, order), jnp.float32)],
+        out_shape=[held, jax.ShapeDtypeStruct((part, order, order), jnp.float32)],
         in_specs=whole_vmem(2 * halves),
         out_specs=whole_vmem(2),
-        scratch_shapes=[pltpu.VMEM((count // 2,) + held.shape[1:], held.dtype)],
+        scratch_shapes=[pltpu.VMEM(held.shape, held.dtype)],
         compiler_params=pltpu.CompilerParams(vmem_limit_bytes=VMEM_LIMIT),
         name="gram",
     )(*own, *beside)
@@ -340,16 +340,17 @@
     )(*terms)
 
 
-def apply_kernel(other, factor_ref, held_ref, *refs):
-    out_ref, value_ref, sems = refs[-3:]
-    part = factor_ref.shape[0]
+def apply_kernel(other, halves, factor_ref, *refs):
+    out_ref, data_ref, value_ref, sems = refs[-4:]
+    assemble(refs[:halves], data_ref)
+    part, _, order, cells = data_ref.shape
     bit = lax.rem(lax.axis_index("space"), 2)
     which = 1 - bit if other else bit
     copies = []
     for slot in range(part):
         f = which * part + slot
         real, imag = factor_ref[slot, 0], factor_ref[slot, 1]
-        data = held_ref[part * other + slot].reshape(2 * held_ref.shape[2], held_ref.shape[3])
+        data = data_ref[slot].reshape(2 * order, cells)
         for p, full in enumerate(
             (jnp.concatenate([real, -imag], axis=1), jnp.concatenate([imag, real], axis=1))
         ):
@@ -368,20 +369,23 @@
         copy.wait()
 
 
-def apply(factor_part, held, earlier=None):
-    part = factor_part.shape[0]
-    operands = [factor_part, held]
+def apply(factor_part, pieces, earlier=None):
+    halves = len(pieces)
+    part, _, size, cells = pieces[0].shape
+    order = size * halves
+    operands = [factor_part, *pieces]
     aliases = {}
     if earlier is not None:
         aliases = {len(operands): 0}
         operands.append(pltpu.with_memory_space_constraint(earlier, pltpu.HBM))
     return pl.pallas_call(
-        functools.partial(apply_kernel, earlier is not None),
-        out_shape=pltpu.HBM(held.shape, jnp.float32),
-        in_specs=whole_vmem(2) + [pl.BlockSpec(memory_space=pltpu.HBM)] * len(aliases),
+        functools.partial(apply_kernel, earlier is not None, halves),
+        out_shape=pltpu.HBM((2 * part, 2, order, cells), jnp.float32),
+        in_specs=whole_vmem(1 + halves) + [pl.BlockSpec(memory_space=pltpu.HBM)] * len(aliases),
         out_specs=pl.BlockSpec(memory_space=pltpu.HBM),
         scratch_shapes=[
-            pltpu.VMEM((part,) + held.shape[1:], jnp.float32),
+            pltpu.VMEM((part, 2, order, cells), jnp.bfloat16),
+            pltpu.VMEM((part, 2, order, cells), jnp.float32),
             pltpu.SemaphoreType.DMA((2 * part,)),
         ],
         input_output_aliases=aliases,
@@ -394,6 +398,10 @@
     return lax.ppermute(value, "space", [(i, i ^ mask) for i in range(size)])
 
 
+def swap_tm(value):
+    return lax.ppermute(value, "tm", [(0, 1), (1, 0)])
+
+
 def swap_corner(value, size):
     pairs = [(t * size + i, (1 - t) * size + (i ^ 1)) for t in range(2) for i in range(size)]
     return lax.ppermute(value, ("tm", "space"), pairs)
@@ -403,16 +411,18 @@
     size = lax.axis_size("space")
     scale = 1.0 / (snapshots.shape[2] * size)
     if lax.axis_size("tm") == 2:
-        mine, theirs, mine_tail, theirs_tail = project(snapshots, frequencies, offsets, 2)
-        own = [mine, lax.ppermute(theirs, "tm", [(0, 1), (1, 0)])]
+        mine, mine_tail, theirs, theirs_tail = project(snapshots, frequencies, offsets, 2)
+        own = [mine, swap_tm(theirs)]
         beside = [swap(mine_tail, size, 1), swap_corner(theirs_tail, size)]
+        rest = [mine_tail, swap_tm(theirs_tail)]
     else:
         (coeffs,) = project(snapshots, frequencies, offsets, 1)
         regrouped = lax.all_to_all(coeffs, "tm", split_axis=0, concat_axis=2, tiled=True)
         part = regrouped.shape[0] // 2
         flipped = jnp.roll(regrouped, part, axis=0)
-        own = [jnp.where(lax.axis_index("space") % 2 == 0, regrouped, flipped)]
-        beside = [swap(own[0][part:], size, 1)]
+        ordered = jnp.where(lax.axis_index("space") % 2 == 0, regrouped, flipped)
+        own, rest = [ordered[:part]], [ordered[part:]]
+        beside = [swap(rest[0], size, 1)]
     held, total = gram(own, beside, scale)
     terms = [total]
     bit = 2
@@ -421,9 +431,10 @@
         masks = [bit, 2 * bit, 3 * bit] if 2 * bit < size else [bit]
         terms = [total] + [swap(total, size, mask) for mask in masks]
         bit *= 4
+    terms, rest = lax.optimization_barrier((terms, rest))
     own = factor(terms)
     sent = swap(own, size, 1)
-    return apply(sent, held, apply(own, held))
+    return apply(sent, rest, apply(own, [held]))
 
 
 def solution(mesh):

time: 28.9 us -> 28.1 us (0.972)
  waiting for transfers between devices: 11 us -> 9.18 us
  starting transfers between devices: 9.52 us -> 10.6 us
    ppermute x6, waiting for transfers between devices: 7.83 us -> 5.64 us  [swap(): return lax.ppermute(value, 'space', [(i, i ^ mask) for i in range(size)])]
    ppermute x1 -> x2, waiting for transfers between devices: 0.01 us -> 2.1 us  [swap_tm(): return lax.ppermute(value, 'tm', [(0, 1), (1, 0)])]
    ppermute x1, waiting for transfers between devices: 3.2 us -> 1.44 us  [swap_corner(): return lax.ppermute(value, ('tm', 'space'), pairs)]
    ppermute x1 -> x2, starting transfers between devices: 3.03 us -> 4.08 us  [swap_tm(): return lax.ppermute(value, 'tm', [(0, 1), (1, 0)])]
  transfers between devices with their start and end apart: 8 -> 9, of which waited for: 7 -> 7; matrix products, arithmetic and copies ran while one was open for 0% -> 0% of each run, Pallas kernels for 3% -> 3%
where the time goes in v7:
time: 28.1 us; the launch traced here: 27.9 us
  starting transfers between devices  10.6 us (38%)
  waiting for transfers between devices  9.18 us (33%)
  Pallas kernels  8.13 us (29%)
    ppermute x6, starting transfers between devices, swap(): return lax.ppermute(value, 'space', [(i, i ^ mask) for i in range(size)])  6.28 us
    ppermute x6, waiting for transfers between devices, swap(): return lax.ppermute(value, 'space', [(i, i ^ mask) for i in range(size)])  5.64 us
    ppermute x2, starting transfers between devices, swap_tm(): return lax.ppermute(value, 'tm', [(0, 1), (1, 0)])  4.08 us
    pallas_call x1, Pallas kernels, factor(): pl.pallas_call(functools.partial(factor_kernel, len(terms)), out_shape=ja...  3.34 us
    pallas_call x1, Pallas kernels, project(): pl.pallas_call(functools.partial(project_kernel, groups), out_shape=shape...  2.56 us
    ppermute x2, waiting for transfers between devices, swap_tm(): return lax.ppermute(value, 'tm', [(0, 1), (1, 0)])  2.1 us
    pallas_call x2, Pallas kernels, apply(): pl.pallas_call(functools.partial(apply_kernel, earlier is not None, halve...  1.91 us
    ppermute x1, waiting for transfers between devices, swap_corner(): return lax.ppermute(value, ('tm', 'space'), pairs)  1.44 us
  transfers between devices with their start and end apart: 9, of which 7 were waited for; matrix products, arithmetic and copies ran while one was open for 0% of the time, Pallas kernels for 3%

profile of v7, /device:TPU:0, one launch (start us, length us, event | category | flops | bytes accessed | tf_op | source)
XLA Modules:
  0.0 27.9 jit_solution(13392126626440371870)
XLA Ops:
  0.0 2.6 %project.1 = (bf16[1,2,64,256]{3,2,1,0:T(8,128)(2,1)S(1)}, bf16[1,2,64,256]{3,2,1,0:T(8,128)(2,1)S(1)}, bf16[1,2,64,256]{3,2,1,0:T(8,128)(2,1)S(1)}, bf16[1,2,64,256]{3,2,1,0:T(8,128)(2,1)S(1)}) custom-call(s32[4]{0:T(128)} %freq_in.1, s32[1,64]{1,0:T(1,128)} %bitcast.1, bf16[64,128,256]{2,1,0:T(8,128)(2,1)} %snap_ref.1), custom_call_target="tpu_custom_call" | custom-call | tf_op jit(solution)/shard_map/project/pallas_call | solution.py:119
  2.6 3.0 %collective-permute-start = (bf16[1,2,64,256]{3,2,1,0:T(8,128)(2,1)S(1)}, bf16[1,2,64,256]{3,2,1,0:T(8,128)(2,1)S(1)}, u32[]{:S(2)}, u32[]{:S(2)}) collective-permute-start(bf16[1,2,64,256]{3,2,1,0:T(8,128)(2,1)S(1)} %get-tuple-element.16), channel_id=1, source_target_pairs={{0,16},{16,0},{1,17},{17,1},{2,18},{18,2},{3,19},{19,3},{4,20},{20... | collective-permute-start | bytes 196616 | tf_op jit(solution)/shard_map/ppermute | solution.py:402
  5.6 0.0 collective-permute-start.1
  5.6 0.2 collective-permute-start.2
  5.8 2.1 %collective-permute-done.refs_1_ = bf16[1,2,64,256]{3,2,1,0:T(8,128)(2,1)S(1)} collective-permute-done((bf16[1,2,64,256]{3,2,1,0:T(8,128)(2,1)S(1)}, bf16[1,2,64,256]{3,2,1,0:T(8,128)(2,1)S(1)}, u32[]{:S(2)}, u32[]{:S(2)}) %collective-permute-start) | collective-permute-done | bytes 65568 | tf_op jit(solution)/shard_map/ppermute | solution.py:402
  7.9 0.0 collective-permute-done.1.refs_2_
  7.9 1.4 %collective-permute-done.2.refs_3_ = bf16[1,2,64,256]{3,2,1,0:T(8,128)(2,1)S(1)} collective-permute-done((bf16[1,2,64,256]{3,2,1,0:T(8,128)(2,1)S(1)}, bf16[1,2,64,256]{3,2,1,0:T(8,128)(2,1)S(1)}, u32[]{:S(2)}, u32[]{:S(2)}) %collective-permute-start.2) | collective-permute-done | bytes 65568 | tf_op jit(solution)/shard_map/ppermute | solution.py:407
  9.3 0.3 %gram.1 = (bf16[1,2,128,256]{3,2,1,0:T(8,128)(2,1)S(1)}, f32[1,128,128]{2,1,0:T(8,128)S(1)}) custom-call(bf16[1,2,64,256]{3,2,1,0:T(8,128)(2,1)S(1)} %get-tuple-element.15.refs_0_, bf16[1,2,64,256]{3,2,1,0:T(8,128)(2,1)S(1)} %collective-permute-done.refs_1_, bf16[1,2,64,256]{3,2,1,0:T(8,128)(2,1)S(1)} %collective-permute-done.1.refs_2_, ...), custom_call_target="tpu_custom_call" | custom-call | tf_op jit(solution)/shard_map/gram/pallas_call | solution.py:166
  9.7 2.6 %collective-permute-start.5 = (f32[1,128,128]{2,1,0:T(8,128)S(1)}, f32[1,128,128]{2,1,0:T(8,128)S(1)}, u32[]{:S(2)}, u32[]{:S(2)}) collective-permute-start(f32[1,128,128]{2,1,0:T(8,128)S(1)} %get-tuple-element.19), channel_id=1, source_target_pairs={{0,6},{1,7},{2,4},{3,5},{4,2},{5,3},{6,0},{7,1},{8,14},{9,15},{10,... | collective-permute-start | bytes 196616 | tf_op jit(solution)/shard_map/ppermute | solution.py:398
  12.2 0.4 %collective-permute-start.4 = (f32[1,128,128]{2,1,0:T(8,128)S(1)}, f32[1,128,128]{2,1,0:T(8,128)S(1)}, u32[]{:S(2)}, u32[]{:S(2)}) collective-permute-start(f32[1,128,128]{2,1,0:T(8,128)S(1)} %get-tuple-element.19), channel_id=1, source_target_pairs={{0,4},{1,5},{2,6},{3,7},{4,0},{5,1},{6,2},{7,3},{8,12},{9,13},{10,... | collective-permute-start | bytes 196616 | tf_op jit(solution)/shard_map/ppermute | solution.py:398
  12.7 0.5 %collective-permute-start.3 = (f32[1,128,128]{2,1,0:T(8,128)S(1)}, f32[1,128,128]{2,1,0:T(8,128)S(1)}, u32[]{:S(2)}, u32[]{:S(2)}) collective-permute-start(f32[1,128,128]{2,1,0:T(8,128)S(1)} %get-tuple-element.19), channel_id=1, source_target_pairs={{0,2},{1,3},{2,0},{3,1},{4,6},{5,7},{6,4},{7,5},{8,10},{9,11},{10,... | collective-permute-start | bytes 196616 | tf_op jit(solution)/shard_map/ppermute | solution.py:398
  13.2 1.0 %collective-permute-start.7 = (bf16[1,2,64,256]{3,2,1,0:T(8,128)(2,1)S(1)}, bf16[1,2,64,256]{3,2,1,0:T(8,128)(2,1)S(1)}, u32[]{:S(2)}, u32[]{:S(2)}) collective-permute-start(bf16[1,2,64,256]{3,2,1,0:T(8,128)(2,1)S(1)} %get-tuple-element.18), channel_id=1, source_target_pairs={{0,16},{16,0},{1,17},{17,1},{2,18},{18,2},{3,19},{19,3},{4,20},{20... | collective-permute-start | bytes 196616 | tf_op jit(solution)/shard_map/ppermute | solution.py:402
  14.3 1.0 %collective-permute-done.5 = f32[1,128,128]{2,1,0:T(8,128)S(1)} collective-permute-done((f32[1,128,128]{2,1,0:T(8,128)S(1)}, f32[1,128,128]{2,1,0:T(8,128)S(1)}, u32[]{:S(2)}, u32[]{:S(2)}) %collective-permute-start.5) | collective-permute-done | bytes 65568 | tf_op jit(solution)/shard_map/ppermute | solution.py:398
  15.2 1.3 %collective-permute-done.4 = f32[1,128,128]{2,1,0:T(8,128)S(1)} collective-permute-done((f32[1,128,128]{2,1,0:T(8,128)S(1)}, f32[1,128,128]{2,1,0:T(8,128)S(1)}, u32[]{:S(2)}, u32[]{:S(2)}) %collective-permute-start.4) | collective-permute-done | bytes 65568 | tf_op jit(solution)/shard_map/ppermute | solution.py:398
  16.5 0.4 %collective-permute-done.3 = f32[1,128,128]{2,1,0:T(8,128)S(1)} collective-permute-done((f32[1,128,128]{2,1,0:T(8,128)S(1)}, f32[1,128,128]{2,1,0:T(8,128)S(1)}, u32[]{:S(2)}, u32[]{:S(2)}) %collective-permute-start.3) | collective-permute-done | bytes 65568 | tf_op jit(solution)/shard_map/ppermute | solution.py:398
  17.0 2.7 %collective-permute-start.6 = (f32[1,128,128]{2,1,0:T(8,128)S(1)}, f32[1,128,128]{2,1,0:T(8,128)S(1)}, u32[]{:S(2)}, u32[]{:S(2)}) collective-permute-start(f32[1,128,128]{2,1,0:T(8,128)S(1)} %add_add_fusion.refs_0_), channel_id=1, source_target_pairs={{0,8},{1,9},{2,10},{3,11},{4,12},{5,13},{6,14},{7,15},{8,0},{9,1},... | collective-permute-start | bytes 196616 | tf_op jit(solution)/shard_map/ppermute | solution.py:398
  19.6 0.0 collective-permute-done.7.refs_1_
  19.6 2.6 %collective-permute-done.6.refs_1_ = f32[1,128,128]{2,1,0:T(8,128)S(1)} collective-permute-done((f32[1,128,128]{2,1,0:T(8,128)S(1)}, f32[1,128,128]{2,1,0:T(8,128)S(1)}, u32[]{:S(2)}, u32[]{:S(2)}) %collective-permute-start.6) | collective-permute-done | bytes 65568 | tf_op jit(solution)/shard_map/ppermute | solution.py:398
  22.2 3.3 %factor.1.factor_ref = f32[1,2,128,128]{3,2,1,0:T(8,128)S(1)} custom-call(f32[1,128,128]{2,1,0:T(8,128)S(1)} %add_add_fusion.refs_0_, f32[1,128,128]{2,1,0:T(8,128)S(1)} %collective-permute-done.6.refs_1_), custom_call_target="tpu_custom_call" | custom-call | tf_op jit(solution)/shard_map/factor/pallas_call | solution.py:333
  25.6 0.1 collective-permute-start.8
  25.6 0.9 %apply.2.refs_2_ = f32[2,2,128,256]{3,2,1,0:T(8,128)} custom-call(f32[1,2,128,128]{3,2,1,0:T(8,128)S(1)} %factor.1.factor_ref, bf16[1,2,128,256]{3,2,1,0:T(8,128)(2,1)S(1)} %get-tuple-element.24.refs_0_), custom_call_target="tpu_custom_call" | custom-call | tf_op jit(solution)/shard_map/apply/pallas_call | solution.py:381
  26.6 0.4 %collective-permute-done.8.factor_ref = f32[1,2,128,128]{3,2,1,0:T(8,128)S(1)} collective-permute-done((f32[1,2,128,128]{3,2,1,0:T(8,128)S(1)}, f32[1,2,128,128]{3,2,1,0:T(8,128)S(1)}, u32[]{:S(2)}, u32[]{:S(2)}) %collective-permute-start.8) | collective-permute-done | bytes 131104 | tf_op jit(solution)/shard_map/ppermute | solution.py:398
  27.0 1.0 %apply.3 = f32[2,2,128,256]{3,2,1,0:T(8,128)} custom-call(f32[1,2,128,128]{3,2,1,0:T(8,128)S(1)} %collective-permute-done.8.factor_ref, bf16[1,2,64,256]{3,2,1,0:T(8,128)(2,1)S(1)} %get-tuple-element.22.refs_0_, bf16[1,2,64,256]{3,2,1,0:T(8,128)(2,1)S(1)} %collective-permute-done.7.refs_1_, ...), custom_call_target="tpu_custom_call", output_to_operand_aliasing={{}: (3, {})} | custom-call | tf_op jit(solution)/shard_map/apply/pallas_call | solution.py:381
  (1 shorter events, 0.0 us)
Async XLA Ops:
  2.6 5.3 %collective-permute-start = (bf16[1,2,64,256]{3,2,1,0:T(8,128)(2,1)S(1)}, bf16[1,2,64,256]{3,2,1,0:T(8,128)(2,1)S(1)}, u32[]{:S(2)}, u32[]{:S(2)}) collective-permute-start(bf16[1,2,64,256]{3,2,1,0:T(8,128)(2,1)S(1)} %get-tuple-element.16), channel_id=1, source_target_pairs={{0,16},{16,0},{1,17},{17,1},{2,18},{18,2},{3,19},{19,3},{4,20},{20... | collective-permute-start | bytes 196616 | tf_op jit(solution)/shard_map/ppermute | solution.py:402
  5.6 2.3 %collective-permute-start.1 = (bf16[1,2,64,256]{3,2,1,0:T(8,128)(2,1)S(1)}, bf16[1,2,64,256]{3,2,1,0:T(8,128)(2,1)S(1)}, u32[]{:S(2)}, u32[]{:S(2)}) collective-permute-start(bf16[1,2,64,256]{3,2,1,0:T(8,128)(2,1)S(1)} %get-tuple-element.22.refs_0_), channel_id=1, source_target_pairs={{0,1},{1,0},{2,3},{3,2},{4,5},{5,4},{6,7},{7,6},{8,9},{9,8},{10,11... | collective-permute-start | bytes 196616 | tf_op jit(solution)/shard_map/ppermute | solution.py:398
  5.6 3.7 %collective-permute-start.2 = (bf16[1,2,64,256]{3,2,1,0:T(8,128)(2,1)S(1)}, bf16[1,2,64,256]{3,2,1,0:T(8,128)(2,1)S(1)}, u32[]{:S(2)}, u32[]{:S(2)}) collective-permute-start(bf16[1,2,64,256]{3,2,1,0:T(8,128)(2,1)S(1)} %get-tuple-element.18), channel_id=1, source_target_pairs={{0,17},{1,16},{2,19},{3,18},{4,21},{5,20},{6,23},{7,22},{8,25},{9,... | collective-permute-start | bytes 196616 | tf_op jit(solution)/shard_map/ppermute | solution.py:407
  9.7 5.6 %collective-permute-start.5 = (f32[1,128,128]{2,1,0:T(8,128)S(1)}, f32[1,128,128]{2,1,0:T(8,128)S(1)}, u32[]{:S(2)}, u32[]{:S(2)}) collective-permute-start(f32[1,128,128]{2,1,0:T(8,128)S(1)} %get-tuple-element.19), channel_id=1, source_target_pairs={{0,6},{1,7},{2,4},{3,5},{4,2},{5,3},{6,0},{7,1},{8,14},{9,15},{10,... | collective-permute-start | bytes 196616 | tf_op jit(solution)/shard_map/ppermute | solution.py:398
  12.2 4.3 %collective-permute-start.4 = (f32[1,128,128]{2,1,0:T(8,128)S(1)}, f32[1,128,128]{2,1,0:T(8,128)S(1)}, u32[]{:S(2)}, u32[]{:S(2)}) collective-permute-start(f32[1,128,128]{2,1,0:T(8,128)S(1)} %get-tuple-element.19), channel_id=1, source_target_pairs={{0,4},{1,5},{2,6},{3,7},{4,0},{5,1},{6,2},{7,3},{8,12},{9,13},{10,... | collective-permute-start | bytes 196616 | tf_op jit(solution)/shard_map/ppermute | solution.py:398
  12.7 4.3 %collective-permute-start.3 = (f32[1,128,128]{2,1,0:T(8,128)S(1)}, f32[1,128,128]{2,1,0:T(8,128)S(1)}, u32[]{:S(2)}, u32[]{:S(2)}) collective-permute-start(f32[1,128,128]{2,1,0:T(8,128)S(1)} %get-tuple-element.19), channel_id=1, source_target_pairs={{0,2},{1,3},{2,0},{3,1},{4,6},{5,7},{6,4},{7,5},{8,10},{9,11},{10,... | collective-permute-start | bytes 196616 | tf_op jit(solution)/shard_map/ppermute | solution.py:398
  13.2 6.4 %collective-permute-start.7 = (bf16[1,2,64,256]{3,2,1,0:T(8,128)(2,1)S(1)}, bf16[1,2,64,256]{3,2,1,0:T(8,128)(2,1)S(1)}, u32[]{:S(2)}, u32[]{:S(2)}) collective-permute-start(bf16[1,2,64,256]{3,2,1,0:T(8,128)(2,1)S(1)} %get-tuple-element.18), channel_id=1, source_target_pairs={{0,16},{16,0},{1,17},{17,1},{2,18},{18,2},{3,19},{19,3},{4,20},{20... | collective-permute-start | bytes 196616 | tf_op jit(solution)/shard_map/ppermute | solution.py:402
  17.0 5.2 %collective-permute-start.6 = (f32[1,128,128]{2,1,0:T(8,128)S(1)}, f32[1,128,128]{2,1,0:T(8,128)S(1)}, u32[]{:S(2)}, u32[]{:S(2)}) collective-permute-start(f32[1,128,128]{2,1,0:T(8,128)S(1)} %add_add_fusion.refs_0_), channel_id=1, source_target_pairs={{0,8},{1,9},{2,10},{3,11},{4,12},{5,13},{6,14},{7,15},{8,0},{9,1},... | collective-permute-start | bytes 196616 | tf_op jit(solution)/shard_map/ppermute | solution.py:398
  25.6 1.4 %collective-permute-start.8 = (f32[1,2,128,128]{3,2,1,0:T(8,128)S(1)}, f32[1,2,128,128]{3,2,1,0:T(8,128)S(1)}, u32[]{:S(2)}, u32[]{:S(2)}) collective-permute-start(f32[1,2,128,128]{3,2,1,0:T(8,128)S(1)} %factor.1.factor_ref), channel_id=1, source_target_pairs={{0,1},{1,0},{2,3},{3,2},{4,5},{5,4},{6,7},{7,6},{8,9},{9,8},{10,11... | collective-permute-start | bytes 393224 | tf_op jit(solution)/shard_map/ppermute | solution.py:398

commit v8 on v7

--- a/solution.py
+++ b/solution.py
@@ -320,7 +320,7 @@
 
 
 def factor_kernel(terms, *refs):
-    out_ref = refs[terms]
+    out_ref = refs[-1]
     total = refs[0][...]
     for r in refs[1:terms]:
         total = total + r[...]
@@ -328,16 +328,16 @@
         invert_factor(total[slot], out_ref, slot)
 
 
-def factor(terms):
+def factor(terms, beside):
     count, order, _ = terms[0].shape
     return pl.pallas_call(
         functools.partial(factor_kernel, len(terms)),
         out_shape=jax.ShapeDtypeStruct((count, 2, order, order), jnp.float32),
-        in_specs=whole_vmem(len(terms)),
+        in_specs=whole_vmem(len(terms)) + [pl.BlockSpec(memory_space=pl.ANY)] * len(beside),
         out_specs=pl.BlockSpec(memory_space=pltpu.VMEM),
         compiler_params=pltpu.CompilerParams(vmem_limit_bytes=VMEM_LIMIT),
         name="factor",
-    )(*terms)
+    )(*terms, *beside)
 
 
 def apply_kernel(other, halves, factor_ref, *refs):
@@ -414,7 +414,8 @@
         mine, mine_tail, theirs, theirs_tail = project(snapshots, frequencies, offsets, 2)
         own = [mine, swap_tm(theirs)]
         beside = [swap(mine_tail, size, 1), swap_corner(theirs_tail, size)]
-        rest = [mine_tail, swap_tm(theirs_tail)]
+        rest = [mine_tail, swap(beside[1], size, 1)]
+        alive = [theirs_tail]
     else:
         (coeffs,) = project(snapshots, frequencies, offsets, 1)
         regrouped = lax.all_to_all(coeffs, "tm", split_axis=0, concat_axis=2, tiled=True)
@@ -423,6 +424,7 @@
         ordered = jnp.where(lax.axis_index("space") % 2 == 0, regrouped, flipped)
         own, rest = [ordered[:part]], [ordered[part:]]
         beside = [swap(rest[0], size, 1)]
+        alive = []
     held, total = gram(own, beside, scale)
     terms = [total]
     bit = 2
@@ -432,7 +434,7 @@
         terms = [total] + [swap(total, size, mask) for mask in masks]
         bit *= 4
     terms, rest = lax.optimization_barrier((terms, rest))
-    own = factor(terms)
+    own = factor(terms, alive)
     sent = swap(own, size, 1)
     return apply(sent, rest, apply(own, [held]))
 

time: 28.1 us -> 28.1 us (level)
  starting transfers between devices: 10.6 us -> 9.52 us
  waiting for transfers between devices: 9.18 us -> 10.2 us
    ppermute x2 -> x1, starting transfers between devices: 4.08 us -> 3.03 us  [swap_tm(): return lax.ppermute(value, 'tm', [(0, 1), (1, 0)])]
    ppermute x6 -> x7, waiting for transfers between devices: 5.64 us -> 6.69 us  [swap(): return lax.ppermute(value, 'space', [(i, i ^ mask) for i in range(size)])]
    ppermute x6 -> x7, starting transfers between devices: 6.28 us -> 6.29 us  [swap(): return lax.ppermute(value, 'space', [(i, i ^ mask) for i in range(size)])]
    ppermute x2 -> x1, waiting for transfers between devices: 2.1 us -> 2.1 us  [swap_tm(): return lax.ppermute(value, 'tm', [(0, 1), (1, 0)])]
where the time goes in v8:
time: 28.1 us; the launch traced here: 27.9 us
  waiting for transfers between devices  10.2 us (36%)
  starting transfers between devices  9.52 us (34%)
  Pallas kernels  8.13 us (29%)
    ppermute x7, waiting for transfers between devices, swap(): return lax.ppermute(value, 'space', [(i, i ^ mask) for i in range(size)])  6.69 us
    ppermute x7, starting transfers between devices, swap(): return lax.ppermute(value, 'space', [(i, i ^ mask) for i in range(size)])  6.29 us
    pallas_call x1, Pallas kernels, factor(): pl.pallas_call(functools.partial(factor_kernel, len(terms)), out_shape=ja...  3.34 us
    ppermute x1, starting transfers between devices, swap_tm(): return lax.ppermute(value, 'tm', [(0, 1), (1, 0)])  3.03 us
    pallas_call x1, Pallas kernels, project(): pl.pallas_call(functools.partial(project_kernel, groups), out_shape=shape...  2.56 us
    ppermute x1, waiting for transfers between devices, swap_tm(): return lax.ppermute(value, 'tm', [(0, 1), (1, 0)])  2.1 us
    pallas_call x2, Pallas kernels, apply(): pl.pallas_call(functools.partial(apply_kernel, earlier is not None, halve...  1.91 us
    ppermute x1, waiting for transfers between devices, swap_corner(): return lax.ppermute(value, ('tm', 'space'), pairs)  1.44 us
  transfers between devices with their start and end apart: 9, of which 7 were waited for; matrix products, arithmetic and copies ran while one was open for 0% of the time, Pallas kernels for 3%

profile of v8, /device:TPU:0, one launch (start us, length us, event | category | flops | bytes accessed | tf_op | source)
XLA Modules:
  0.0 27.9 jit_solution(47527626916339533)
XLA Ops:
  0.0 2.6 %project.1 = (bf16[1,2,64,256]{3,2,1,0:T(8,128)(2,1)S(1)}, bf16[1,2,64,256]{3,2,1,0:T(8,128)(2,1)S(1)}, bf16[1,2,64,256]{3,2,1,0:T(8,128)(2,1)S(1)}, bf16[1,2,64,256]{3,2,1,0:T(8,128)(2,1)S(1)}) custom-call(s32[4]{0:T(128)} %freq_in.1, s32[1,64]{1,0:T(1,128)} %bitcast.1, bf16[64,128,256]{2,1,0:T(8,128)(2,1)} %snap_ref.1), custom_call_target="tpu_custom_call" | custom-call | tf_op jit(solution)/shard_map/project/pallas_call | solution.py:119
  2.6 3.0 %collective-permute-start = (bf16[1,2,64,256]{3,2,1,0:T(8,128)(2,1)S(1)}, bf16[1,2,64,256]{3,2,1,0:T(8,128)(2,1)S(1)}, u32[]{:S(2)}, u32[]{:S(2)}) collective-permute-start(bf16[1,2,64,256]{3,2,1,0:T(8,128)(2,1)S(1)} %get-tuple-element.16), channel_id=1, source_target_pairs={{0,16},{16,0},{1,17},{17,1},{2,18},{18,2},{3,19},{19,3},{4,20},{20... | collective-permute-start | bytes 196616 | tf_op jit(solution)/shard_map/ppermute | solution.py:402
  5.6 0.0 collective-permute-start.1
  5.6 0.2 collective-permute-start.2
  5.8 2.1 %collective-permute-done.refs_1_ = bf16[1,2,64,256]{3,2,1,0:T(8,128)(2,1)S(1)} collective-permute-done((bf16[1,2,64,256]{3,2,1,0:T(8,128)(2,1)S(1)}, bf16[1,2,64,256]{3,2,1,0:T(8,128)(2,1)S(1)}, u32[]{:S(2)}, u32[]{:S(2)}) %collective-permute-start) | collective-permute-done | bytes 65568 | tf_op jit(solution)/shard_map/ppermute | solution.py:402
  7.9 0.0 collective-permute-done.1.refs_2_
  7.9 1.4 %collective-permute-done.2.refs_3_ = bf16[1,2,64,256]{3,2,1,0:T(8,128)(2,1)S(1)} collective-permute-done((bf16[1,2,64,256]{3,2,1,0:T(8,128)(2,1)S(1)}, bf16[1,2,64,256]{3,2,1,0:T(8,128)(2,1)S(1)}, u32[]{:S(2)}, u32[]{:S(2)}) %collective-permute-start.2) | collective-permute-done | bytes 65568 | tf_op jit(solution)/shard_map/ppermute | solution.py:407
  9.3 0.3 %gram.1 = (bf16[1,2,128,256]{3,2,1,0:T(8,128)(2,1)S(1)}, f32[1,128,128]{2,1,0:T(8,128)S(1)}) custom-call(bf16[1,2,64,256]{3,2,1,0:T(8,128)(2,1)S(1)} %get-tuple-element.15.refs_0_, bf16[1,2,64,256]{3,2,1,0:T(8,128)(2,1)S(1)} %collective-permute-done.refs_1_, bf16[1,2,64,256]{3,2,1,0:T(8,128)(2,1)S(1)} %collective-permute-done.1.refs_2_, ...), custom_call_target="tpu_custom_call" | custom-call | tf_op jit(solution)/shard_map/gram/pallas_call | solution.py:166
  9.7 2.6 %collective-permute-start.5 = (f32[1,128,128]{2,1,0:T(8,128)S(1)}, f32[1,128,128]{2,1,0:T(8,128)S(1)}, u32[]{:S(2)}, u32[]{:S(2)}) collective-permute-start(f32[1,128,128]{2,1,0:T(8,128)S(1)} %get-tuple-element.19), channel_id=1, source_target_pairs={{0,6},{1,7},{2,4},{3,5},{4,2},{5,3},{6,0},{7,1},{8,14},{9,15},{10,... | collective-permute-start | bytes 196616 | tf_op jit(solution)/shard_map/ppermute | solution.py:398
  12.2 0.4 %collective-permute-start.4 = (f32[1,128,128]{2,1,0:T(8,128)S(1)}, f32[1,128,128]{2,1,0:T(8,128)S(1)}, u32[]{:S(2)}, u32[]{:S(2)}) collective-permute-start(f32[1,128,128]{2,1,0:T(8,128)S(1)} %get-tuple-element.19), channel_id=1, source_target_pairs={{0,4},{1,5},{2,6},{3,7},{4,0},{5,1},{6,2},{7,3},{8,12},{9,13},{10,... | collective-permute-start | bytes 196616 | tf_op jit(solution)/shard_map/ppermute | solution.py:398
  12.7 0.5 %collective-permute-start.3 = (f32[1,128,128]{2,1,0:T(8,128)S(1)}, f32[1,128,128]{2,1,0:T(8,128)S(1)}, u32[]{:S(2)}, u32[]{:S(2)}) collective-permute-start(f32[1,128,128]{2,1,0:T(8,128)S(1)} %get-tuple-element.19), channel_id=1, source_target_pairs={{0,2},{1,3},{2,0},{3,1},{4,6},{5,7},{6,4},{7,5},{8,10},{9,11},{10,... | collective-permute-start | bytes 196616 | tf_op jit(solution)/shard_map/ppermute | solution.py:398
  13.2 0.0 collective-permute-start.7
  13.2 2.0 %collective-permute-done.5 = f32[1,128,128]{2,1,0:T(8,128)S(1)} collective-permute-done((f32[1,128,128]{2,1,0:T(8,128)S(1)}, f32[1,128,128]{2,1,0:T(8,128)S(1)}, u32[]{:S(2)}, u32[]{:S(2)}) %collective-permute-start.5) | collective-permute-done | bytes 65568 | tf_op jit(solution)/shard_map/ppermute | solution.py:398
  15.2 1.3 %collective-permute-done.4 = f32[1,128,128]{2,1,0:T(8,128)S(1)} collective-permute-done((f32[1,128,128]{2,1,0:T(8,128)S(1)}, f32[1,128,128]{2,1,0:T(8,128)S(1)}, u32[]{:S(2)}, u32[]{:S(2)}) %collective-permute-start.4) | collective-permute-done | bytes 65568 | tf_op jit(solution)/shard_map/ppermute | solution.py:398
  16.5 0.4 %collective-permute-done.3 = f32[1,128,128]{2,1,0:T(8,128)S(1)} collective-permute-done((f32[1,128,128]{2,1,0:T(8,128)S(1)}, f32[1,128,128]{2,1,0:T(8,128)S(1)}, u32[]{:S(2)}, u32[]{:S(2)}) %collective-permute-start.3) | collective-permute-done | bytes 65568 | tf_op jit(solution)/shard_map/ppermute | solution.py:398
  17.0 2.7 %collective-permute-start.6 = (f32[1,128,128]{2,1,0:T(8,128)S(1)}, f32[1,128,128]{2,1,0:T(8,128)S(1)}, u32[]{:S(2)}, u32[]{:S(2)}) collective-permute-start(f32[1,128,128]{2,1,0:T(8,128)S(1)} %add_add_fusion.refs_0_), channel_id=1, source_target_pairs={{0,8},{1,9},{2,10},{3,11},{4,12},{5,13},{6,14},{7,15},{8,0},{9,1},... | collective-permute-start | bytes 196616 | tf_op jit(solution)/shard_map/ppermute | solution.py:398
  19.6 0.0 collective-permute-done.7.refs_1_
  19.6 2.6 %collective-permute-done.6.refs_1_ = f32[1,128,128]{2,1,0:T(8,128)S(1)} collective-permute-done((f32[1,128,128]{2,1,0:T(8,128)S(1)}, f32[1,128,128]{2,1,0:T(8,128)S(1)}, u32[]{:S(2)}, u32[]{:S(2)}) %collective-permute-start.6) | collective-permute-done | bytes 65568 | tf_op jit(solution)/shard_map/ppermute | solution.py:398
  22.2 3.3 %factor.1.factor_ref = f32[1,2,128,128]{3,2,1,0:T(8,128)S(1)} custom-call(f32[1,128,128]{2,1,0:T(8,128)S(1)} %add_add_fusion.refs_0_, f32[1,128,128]{2,1,0:T(8,128)S(1)} %collective-permute-done.6.refs_1_, bf16[1,2,64,256]{3,2,1,0:T(8,128)(2,1)S(1)} %get-tuple-element.18.refs_2_), custom_call_target="tpu_custom_call" | custom-call | tf_op jit(solution)/shard_map/factor/pallas_call | solution.py:333
  25.6 0.1 collective-permute-start.8
  25.6 0.9 %apply.2.refs_2_ = f32[2,2,128,256]{3,2,1,0:T(8,128)} custom-call(f32[1,2,128,128]{3,2,1,0:T(8,128)S(1)} %factor.1.factor_ref, bf16[1,2,128,256]{3,2,1,0:T(8,128)(2,1)S(1)} %get-tuple-element.24.refs_0_), custom_call_target="tpu_custom_call" | custom-call | tf_op jit(solution)/shard_map/apply/pallas_call | solution.py:381
  26.6 0.4 %collective-permute-done.8.factor_ref = f32[1,2,128,128]{3,2,1,0:T(8,128)S(1)} collective-permute-done((f32[1,2,128,128]{3,2,1,0:T(8,128)S(1)}, f32[1,2,128,128]{3,2,1,0:T(8,128)S(1)}, u32[]{:S(2)}, u32[]{:S(2)}) %collective-permute-start.8) | collective-permute-done | bytes 131104 | tf_op jit(solution)/shard_map/ppermute | solution.py:398
  27.0 1.0 %apply.3 = f32[2,2,128,256]{3,2,1,0:T(8,128)} custom-call(f32[1,2,128,128]{3,2,1,0:T(8,128)S(1)} %collective-permute-done.8.factor_ref, bf16[1,2,64,256]{3,2,1,0:T(8,128)(2,1)S(1)} %get-tuple-element.22.refs_0_, bf16[1,2,64,256]{3,2,1,0:T(8,128)(2,1)S(1)} %collective-permute-done.7.refs_1_, ...), custom_call_target="tpu_custom_call", output_to_operand_aliasing={{}: (3, {})} | custom-call | tf_op jit(solution)/shard_map/apply/pallas_call | solution.py:381
  (1 shorter events, 0.0 us)
Async XLA Ops:
  2.6 5.3 %collective-permute-start = (bf16[1,2,64,256]{3,2,1,0:T(8,128)(2,1)S(1)}, bf16[1,2,64,256]{3,2,1,0:T(8,128)(2,1)S(1)}, u32[]{:S(2)}, u32[]{:S(2)}) collective-permute-start(bf16[1,2,64,256]{3,2,1,0:T(8,128)(2,1)S(1)} %get-tuple-element.16), channel_id=1, source_target_pairs={{0,16},{16,0},{1,17},{17,1},{2,18},{18,2},{3,19},{19,3},{4,20},{20... | collective-permute-start | bytes 196616 | tf_op jit(solution)/shard_map/ppermute | solution.py:402
  5.6 2.3 %collective-permute-start.1 = (bf16[1,2,64,256]{3,2,1,0:T(8,128)(2,1)S(1)}, bf16[1,2,64,256]{3,2,1,0:T(8,128)(2,1)S(1)}, u32[]{:S(2)}, u32[]{:S(2)}) collective-permute-start(bf16[1,2,64,256]{3,2,1,0:T(8,128)(2,1)S(1)} %get-tuple-element.22.refs_0_), channel_id=1, source_target_pairs={{0,1},{1,0},{2,3},{3,2},{4,5},{5,4},{6,7},{7,6},{8,9},{9,8},{10,11... | collective-permute-start | bytes 196616 | tf_op jit(solution)/shard_map/ppermute | solution.py:398
  5.6 3.7 %collective-permute-start.2 = (bf16[1,2,64,256]{3,2,1,0:T(8,128)(2,1)S(1)}, bf16[1,2,64,256]{3,2,1,0:T(8,128)(2,1)S(1)}, u32[]{:S(2)}, u32[]{:S(2)}) collective-permute-start(bf16[1,2,64,256]{3,2,1,0:T(8,128)(2,1)S(1)} %get-tuple-element.18.refs_2_), channel_id=1, source_target_pairs={{0,17},{1,16},{2,19},{3,18},{4,21},{5,20},{6,23},{7,22},{8,25},{9,... | collective-permute-start | bytes 196616 | tf_op jit(solution)/shard_map/ppermute | solution.py:407
  9.7 5.6 %collective-permute-start.5 = (f32[1,128,128]{2,1,0:T(8,128)S(1)}, f32[1,128,128]{2,1,0:T(8,128)S(1)}, u32[]{:S(2)}, u32[]{:S(2)}) collective-permute-start(f32[1,128,128]{2,1,0:T(8,128)S(1)} %get-tuple-element.19), channel_id=1, source_target_pairs={{0,6},{1,7},{2,4},{3,5},{4,2},{5,3},{6,0},{7,1},{8,14},{9,15},{10,... | collective-permute-start | bytes 196616 | tf_op jit(solution)/shard_map/ppermute | solution.py:398
  12.2 4.3 %collective-permute-start.4 = (f32[1,128,128]{2,1,0:T(8,128)S(1)}, f32[1,128,128]{2,1,0:T(8,128)S(1)}, u32[]{:S(2)}, u32[]{:S(2)}) collective-permute-start(f32[1,128,128]{2,1,0:T(8,128)S(1)} %get-tuple-element.19), channel_id=1, source_target_pairs={{0,4},{1,5},{2,6},{3,7},{4,0},{5,1},{6,2},{7,3},{8,12},{9,13},{10,... | collective-permute-start | bytes 196616 | tf_op jit(solution)/shard_map/ppermute | solution.py:398
  12.7 4.3 %collective-permute-start.3 = (f32[1,128,128]{2,1,0:T(8,128)S(1)}, f32[1,128,128]{2,1,0:T(8,128)S(1)}, u32[]{:S(2)}, u32[]{:S(2)}) collective-permute-start(f32[1,128,128]{2,1,0:T(8,128)S(1)} %get-tuple-element.19), channel_id=1, source_target_pairs={{0,2},{1,3},{2,0},{3,1},{4,6},{5,7},{6,4},{7,5},{8,10},{9,11},{10,... | collective-permute-start | bytes 196616 | tf_op jit(solution)/shard_map/ppermute | solution.py:398
  13.2 6.4 %collective-permute-start.7 = (bf16[1,2,64,256]{3,2,1,0:T(8,128)(2,1)S(1)}, bf16[1,2,64,256]{3,2,1,0:T(8,128)(2,1)S(1)}, u32[]{:S(2)}, u32[]{:S(2)}) collective-permute-start(bf16[1,2,64,256]{3,2,1,0:T(8,128)(2,1)S(1)} %collective-permute-done.2.refs_3_), channel_id=1, source_target_pairs={{0,1},{1,0},{2,3},{3,2},{4,5},{5,4},{6,7},{7,6},{8,9},{9,8},{10,11... | collective-permute-start | bytes 196616 | tf_op jit(solution)/shard_map/ppermute | solution.py:398
  17.0 5.2 %collective-permute-start.6 = (f32[1,128,128]{2,1,0:T(8,128)S(1)}, f32[1,128,128]{2,1,0:T(8,128)S(1)}, u32[]{:S(2)}, u32[]{:S(2)}) collective-permute-start(f32[1,128,128]{2,1,0:T(8,128)S(1)} %add_add_fusion.refs_0_), channel_id=1, source_target_pairs={{0,8},{1,9},{2,10},{3,11},{4,12},{5,13},{6,14},{7,15},{8,0},{9,1},... | collective-permute-start | bytes 196616 | tf_op jit(solution)/shard_map/ppermute | solution.py:398
  25.6 1.4 %collective-permute-start.8 = (f32[1,2,128,128]{3,2,1,0:T(8,128)S(1)}, f32[1,2,128,128]{3,2,1,0:T(8,128)S(1)}, u32[]{:S(2)}, u32[]{:S(2)}) collective-permute-start(f32[1,2,128,128]{3,2,1,0:T(8,128)S(1)} %factor.1.factor_ref), channel_id=1, source_target_pairs={{0,1},{1,0},{2,3},{3,2},{4,5},{5,4},{6,7},{7,6},{8,9},{9,8},{10,11... | collective-permute-start | bytes 393224 | tf_op jit(solution)/shard_map/ppermute | solution.py:398

commit v9 on v7

--- a/solution.py
+++ b/solution.py
@@ -340,9 +340,13 @@
     )(*terms)
 
 
-def apply_kernel(other, halves, factor_ref, *refs):
-    out_ref, data_ref, value_ref, sems = refs[-4:]
-    assemble(refs[:halves], data_ref)
+def apply_kernel(other, later, factor_ref, data_ref, *refs):
+    value_ref, sems = refs[-2:]
+    if other:
+        out_ref = refs[-3]
+    else:
+        out_ref, later_ref = refs[-4:-2]
+        assemble(refs[:later], later_ref)
     part, _, order, cells = data_ref.shape
     bit = lax.rem(lax.axis_index("space"), 2)
     which = 1 - bit if other else bit
@@ -369,22 +373,26 @@
         copy.wait()
 
 
-def apply(factor_part, pieces, earlier=None):
-    halves = len(pieces)
-    part, _, size, cells = pieces[0].shape
-    order = size * halves
-    operands = [factor_part, *pieces]
+def apply(factor_part, held, later=(), earlier=None):
+    part, _, order, cells = held.shape
+    operands = [factor_part, held, *later]
+    shapes = [pltpu.HBM((2 * part, 2, order, cells), jnp.float32)]
+    in_specs = whole_vmem(len(operands))
+    out_specs = [pl.BlockSpec(memory_space=pltpu.HBM)]
     aliases = {}
     if earlier is not None:
         aliases = {len(operands): 0}
         operands.append(pltpu.with_memory_space_constraint(earlier, pltpu.HBM))
+        in_specs += out_specs
+    else:
+        shapes.append(pltpu.VMEM(held.shape, held.dtype))
+        out_specs = out_specs + whole_vmem(1)
     return pl.pallas_call(
-        functools.partial(apply_kernel, earlier is not None, halves),
-        out_shape=pltpu.HBM((2 * part, 2, order, cells), jnp.float32),
-        in_specs=whole_vmem(1 + halves) + [pl.BlockSpec(memory_space=pltpu.HBM)] * len(aliases),
-        out_specs=pl.BlockSpec(memory_space=pltpu.HBM),
+        functools.partial(apply_kernel, earlier is not None, len(later)),
+        out_shape=shapes,
+        in_specs=in_specs,
+        out_specs=out_specs,
         scratch_shapes=[
-            pltpu.VMEM((part, 2, order, cells), jnp.bfloat16),
             pltpu.VMEM((part, 2, order, cells), jnp.float32),
             pltpu.SemaphoreType.DMA((2 * part,)),
         ],
@@ -434,7 +442,8 @@
     terms, rest = lax.optimization_barrier((terms, rest))
     own = factor(terms)
     sent = swap(own, size, 1)
-    return apply(sent, rest, apply(own, [held]))
+    modes, held_rest = apply(own, held, rest)
+    return apply(sent, held_rest, earlier=modes)[0]
 
 
 def solution(mesh):

time: 28.1 us -> 28.1 us (level)
  no operation moved by 1% of the time
where the time goes in v9:
time: 28.1 us; the launch traced here: 27.9 us
  starting transfers between devices  10.6 us (38%)
  waiting for transfers between devices  9.18 us (33%)
  Pallas kernels  8.12 us (29%)
    ppermute x6, starting transfers between devices, swap(): return lax.ppermute(value, 'space', [(i, i ^ mask) for i in range(size)])  6.28 us
    ppermute x6, waiting for transfers between devices, swap(): return lax.ppermute(value, 'space', [(i, i ^ mask) for i in range(size)])  5.64 us
    ppermute x2, starting transfers between devices, swap_tm(): return lax.ppermute(value, 'tm', [(0, 1), (1, 0)])  4.08 us
    pallas_call x1, Pallas kernels, factor(): pl.pallas_call(functools.partial(factor_kernel, len(terms)), out_shape=ja...  3.34 us
    pallas_call x1, Pallas kernels, project(): pl.pallas_call(functools.partial(project_kernel, groups), out_shape=shape...  2.56 us
    ppermute x2, waiting for transfers between devices, swap_tm(): return lax.ppermute(value, 'tm', [(0, 1), (1, 0)])  2.1 us
    pallas_call x2, Pallas kernels, apply(): pl.pallas_call(functools.partial(apply_kernel, earlier is not None, len(l...  1.9 us
    ppermute x1, waiting for transfers between devices, swap_corner(): return lax.ppermute(value, ('tm', 'space'), pairs)  1.44 us
  transfers between devices with their start and end apart: 9, of which 7 were waited for; matrix products, arithmetic and copies ran while one was open for 0% of the time, Pallas kernels for 3%

profile of v9, /device:TPU:0, one launch (start us, length us, event | category | flops | bytes accessed | tf_op | source)
XLA Modules:
  0.0 27.9 jit_solution(11256965208675595563)
XLA Ops:
  0.0 2.6 %project.1 = (bf16[1,2,64,256]{3,2,1,0:T(8,128)(2,1)S(1)}, bf16[1,2,64,256]{3,2,1,0:T(8,128)(2,1)S(1)}, bf16[1,2,64,256]{3,2,1,0:T(8,128)(2,1)S(1)}, bf16[1,2,64,256]{3,2,1,0:T(8,128)(2,1)S(1)}) custom-call(s32[4]{0:T(128)} %freq_in.1, s32[1,64]{1,0:T(1,128)} %bitcast.1, bf16[64,128,256]{2,1,0:T(8,128)(2,1)} %snap_ref.1), custom_call_target="tpu_custom_call" | custom-call | tf_op jit(solution)/shard_map/project/pallas_call | solution.py:119
  2.6 3.0 %collective-permute-start = (bf16[1,2,64,256]{3,2,1,0:T(8,128)(2,1)S(1)}, bf16[1,2,64,256]{3,2,1,0:T(8,128)(2,1)S(1)}, u32[]{:S(2)}, u32[]{:S(2)}) collective-permute-start(bf16[1,2,64,256]{3,2,1,0:T(8,128)(2,1)S(1)} %get-tuple-element.18), channel_id=1, source_target_pairs={{0,16},{16,0},{1,17},{17,1},{2,18},{18,2},{3,19},{19,3},{4,20},{20... | collective-permute-start | bytes 196616 | tf_op jit(solution)/shard_map/ppermute | solution.py:410
  5.6 0.0 collective-permute-start.1
  5.6 0.2 collective-permute-start.2
  5.8 2.1 %collective-permute-done.refs_1_ = bf16[1,2,64,256]{3,2,1,0:T(8,128)(2,1)S(1)} collective-permute-done((bf16[1,2,64,256]{3,2,1,0:T(8,128)(2,1)S(1)}, bf16[1,2,64,256]{3,2,1,0:T(8,128)(2,1)S(1)}, u32[]{:S(2)}, u32[]{:S(2)}) %collective-permute-start) | collective-permute-done | bytes 65568 | tf_op jit(solution)/shard_map/ppermute | solution.py:410
  7.9 0.0 collective-permute-done.1.refs_2_
  7.9 1.4 %collective-permute-done.2.refs_3_ = bf16[1,2,64,256]{3,2,1,0:T(8,128)(2,1)S(1)} collective-permute-done((bf16[1,2,64,256]{3,2,1,0:T(8,128)(2,1)S(1)}, bf16[1,2,64,256]{3,2,1,0:T(8,128)(2,1)S(1)}, u32[]{:S(2)}, u32[]{:S(2)}) %collective-permute-start.2) | collective-permute-done | bytes 65568 | tf_op jit(solution)/shard_map/ppermute | solution.py:415
  9.3 0.3 %gram.1 = (bf16[1,2,128,256]{3,2,1,0:T(8,128)(2,1)S(1)}, f32[1,128,128]{2,1,0:T(8,128)S(1)}) custom-call(bf16[1,2,64,256]{3,2,1,0:T(8,128)(2,1)S(1)} %get-tuple-element.17.refs_0_, bf16[1,2,64,256]{3,2,1,0:T(8,128)(2,1)S(1)} %collective-permute-done.refs_1_, bf16[1,2,64,256]{3,2,1,0:T(8,128)(2,1)S(1)} %collective-permute-done.1.refs_2_, ...), custom_call_target="tpu_custom_call" | custom-call | tf_op jit(solution)/shard_map/gram/pallas_call | solution.py:166
  9.7 2.6 %collective-permute-start.5 = (f32[1,128,128]{2,1,0:T(8,128)S(1)}, f32[1,128,128]{2,1,0:T(8,128)S(1)}, u32[]{:S(2)}, u32[]{:S(2)}) collective-permute-start(f32[1,128,128]{2,1,0:T(8,128)S(1)} %get-tuple-element.21), channel_id=1, source_target_pairs={{0,6},{1,7},{2,4},{3,5},{4,2},{5,3},{6,0},{7,1},{8,14},{9,15},{10,... | collective-permute-start | bytes 196616 | tf_op jit(solution)/shard_map/ppermute | solution.py:406
  12.2 0.4 %collective-permute-start.4 = (f32[1,128,128]{2,1,0:T(8,128)S(1)}, f32[1,128,128]{2,1,0:T(8,128)S(1)}, u32[]{:S(2)}, u32[]{:S(2)}) collective-permute-start(f32[1,128,128]{2,1,0:T(8,128)S(1)} %get-tuple-element.21), channel_id=1, source_target_pairs={{0,4},{1,5},{2,6},{3,7},{4,0},{5,1},{6,2},{7,3},{8,12},{9,13},{10,... | collective-permute-start | bytes 196616 | tf_op jit(solution)/shard_map/ppermute | solution.py:406
  12.7 0.5 %collective-permute-start.3 = (f32[1,128,128]{2,1,0:T(8,128)S(1)}, f32[1,128,128]{2,1,0:T(8,128)S(1)}, u32[]{:S(2)}, u32[]{:S(2)}) collective-permute-start(f32[1,128,128]{2,1,0:T(8,128)S(1)} %get-tuple-element.21), channel_id=1, source_target_pairs={{0,2},{1,3},{2,0},{3,1},{4,6},{5,7},{6,4},{7,5},{8,10},{9,11},{10,... | collective-permute-start | bytes 196616 | tf_op jit(solution)/shard_map/ppermute | solution.py:406
  13.2 1.0 %collective-permute-start.7 = (bf16[1,2,64,256]{3,2,1,0:T(8,128)(2,1)S(1)}, bf16[1,2,64,256]{3,2,1,0:T(8,128)(2,1)S(1)}, u32[]{:S(2)}, u32[]{:S(2)}) collective-permute-start(bf16[1,2,64,256]{3,2,1,0:T(8,128)(2,1)S(1)} %get-tuple-element.20), channel_id=1, source_target_pairs={{0,16},{16,0},{1,17},{17,1},{2,18},{18,2},{3,19},{19,3},{4,20},{20... | collective-permute-start | bytes 196616 | tf_op jit(solution)/shard_map/ppermute | solution.py:410
  14.3 1.0 %collective-permute-done.5 = f32[1,128,128]{2,1,0:T(8,128)S(1)} collective-permute-done((f32[1,128,128]{2,1,0:T(8,128)S(1)}, f32[1,128,128]{2,1,0:T(8,128)S(1)}, u32[]{:S(2)}, u32[]{:S(2)}) %collective-permute-start.5) | collective-permute-done | bytes 65568 | tf_op jit(solution)/shard_map/ppermute | solution.py:406
  15.2 1.3 %collective-permute-done.4 = f32[1,128,128]{2,1,0:T(8,128)S(1)} collective-permute-done((f32[1,128,128]{2,1,0:T(8,128)S(1)}, f32[1,128,128]{2,1,0:T(8,128)S(1)}, u32[]{:S(2)}, u32[]{:S(2)}) %collective-permute-start.4) | collective-permute-done | bytes 65568 | tf_op jit(solution)/shard_map/ppermute | solution.py:406
  16.5 0.4 %collective-permute-done.3 = f32[1,128,128]{2,1,0:T(8,128)S(1)} collective-permute-done((f32[1,128,128]{2,1,0:T(8,128)S(1)}, f32[1,128,128]{2,1,0:T(8,128)S(1)}, u32[]{:S(2)}, u32[]{:S(2)}) %collective-permute-start.3) | collective-permute-done | bytes 65568 | tf_op jit(solution)/shard_map/ppermute | solution.py:406
  17.0 2.7 %collective-permute-start.6 = (f32[1,128,128]{2,1,0:T(8,128)S(1)}, f32[1,128,128]{2,1,0:T(8,128)S(1)}, u32[]{:S(2)}, u32[]{:S(2)}) collective-permute-start(f32[1,128,128]{2,1,0:T(8,128)S(1)} %add_add_fusion.refs_0_), channel_id=1, source_target_pairs={{0,8},{1,9},{2,10},{3,11},{4,12},{5,13},{6,14},{7,15},{8,0},{9,1},... | collective-permute-start | bytes 196616 | tf_op jit(solution)/shard_map/ppermute | solution.py:406
  19.6 0.0 collective-permute-done.7.refs_1_
  19.6 2.6 %collective-permute-done.6.refs_1_ = f32[1,128,128]{2,1,0:T(8,128)S(1)} collective-permute-done((f32[1,128,128]{2,1,0:T(8,128)S(1)}, f32[1,128,128]{2,1,0:T(8,128)S(1)}, u32[]{:S(2)}, u32[]{:S(2)}) %collective-permute-start.6) | collective-permute-done | bytes 65568 | tf_op jit(solution)/shard_map/ppermute | solution.py:406
  22.2 3.3 %factor.1.factor_ref = f32[1,2,128,128]{3,2,1,0:T(8,128)S(1)} custom-call(f32[1,128,128]{2,1,0:T(8,128)S(1)} %add_add_fusion.refs_0_, f32[1,128,128]{2,1,0:T(8,128)S(1)} %collective-permute-done.6.refs_1_), custom_call_target="tpu_custom_call" | custom-call | tf_op jit(solution)/shard_map/factor/pallas_call | solution.py:333
  25.6 0.1 collective-permute-start.8
  25.6 1.0 %apply.2 = (f32[2,2,128,256]{3,2,1,0:T(8,128)}, bf16[1,2,128,256]{3,2,1,0:T(8,128)(2,1)S(1)}) custom-call(f32[1,2,128,128]{3,2,1,0:T(8,128)S(1)} %factor.1.factor_ref, bf16[1,2,128,256]{3,2,1,0:T(8,128)(2,1)S(1)} %get-tuple-element.24.data_ref, bf16[1,2,64,256]{3,2,1,0:T(8,128)(2,1)S(1)} %get-tuple-element.25.refs_0_, ...), custom_call_target="tpu_custom_call" | custom-call | tf_op jit(solution)/shard_map/apply/pallas_call | solution.py:390
  26.6 0.4 %collective-permute-done.8.factor_ref = f32[1,2,128,128]{3,2,1,0:T(8,128)S(1)} collective-permute-done((f32[1,2,128,128]{3,2,1,0:T(8,128)S(1)}, f32[1,2,128,128]{3,2,1,0:T(8,128)S(1)}, u32[]{:S(2)}, u32[]{:S(2)}) %collective-permute-start.8) | collective-permute-done | bytes 131104 | tf_op jit(solution)/shard_map/ppermute | solution.py:406
  27.0 0.9 %apply.3 = f32[2,2,128,256]{3,2,1,0:T(8,128)} custom-call(f32[1,2,128,128]{3,2,1,0:T(8,128)S(1)} %collective-permute-done.8.factor_ref, bf16[1,2,128,256]{3,2,1,0:T(8,128)(2,1)S(1)} %get-tuple-element.27.data_ref, f32[2,2,128,256]{3,2,1,0:T(8,128)} %get-tuple-element.28.refs_0_), custom_call_target="tpu_custom_call", output_to_operand_aliasing={{}: (2, {})} | custom-call | tf_op jit(solution)/shard_map/apply/pallas_call | solution.py:390
  (1 shorter events, 0.0 us)
Async XLA Ops:
  2.6 5.3 %collective-permute-start = (bf16[1,2,64,256]{3,2,1,0:T(8,128)(2,1)S(1)}, bf16[1,2,64,256]{3,2,1,0:T(8,128)(2,1)S(1)}, u32[]{:S(2)}, u32[]{:S(2)}) collective-permute-start(bf16[1,2,64,256]{3,2,1,0:T(8,128)(2,1)S(1)} %get-tuple-element.18), channel_id=1, source_target_pairs={{0,16},{16,0},{1,17},{17,1},{2,18},{18,2},{3,19},{19,3},{4,20},{20... | collective-permute-start | bytes 196616 | tf_op jit(solution)/shard_map/ppermute | solution.py:410
  5.6 2.3 %collective-permute-start.1 = (bf16[1,2,64,256]{3,2,1,0:T(8,128)(2,1)S(1)}, bf16[1,2,64,256]{3,2,1,0:T(8,128)(2,1)S(1)}, u32[]{:S(2)}, u32[]{:S(2)}) collective-permute-start(bf16[1,2,64,256]{3,2,1,0:T(8,128)(2,1)S(1)} %get-tuple-element.25.refs_0_), channel_id=1, source_target_pairs={{0,1},{1,0},{2,3},{3,2},{4,5},{5,4},{6,7},{7,6},{8,9},{9,8},{10,11... | collective-permute-start | bytes 196616 | tf_op jit(solution)/shard_map/ppermute | solution.py:406
  5.6 3.7 %collective-permute-start.2 = (bf16[1,2,64,256]{3,2,1,0:T(8,128)(2,1)S(1)}, bf16[1,2,64,256]{3,2,1,0:T(8,128)(2,1)S(1)}, u32[]{:S(2)}, u32[]{:S(2)}) collective-permute-start(bf16[1,2,64,256]{3,2,1,0:T(8,128)(2,1)S(1)} %get-tuple-element.20), channel_id=1, source_target_pairs={{0,17},{1,16},{2,19},{3,18},{4,21},{5,20},{6,23},{7,22},{8,25},{9,... | collective-permute-start | bytes 196616 | tf_op jit(solution)/shard_map/ppermute | solution.py:415
  9.7 5.6 %collective-permute-start.5 = (f32[1,128,128]{2,1,0:T(8,128)S(1)}, f32[1,128,128]{2,1,0:T(8,128)S(1)}, u32[]{:S(2)}, u32[]{:S(2)}) collective-permute-start(f32[1,128,128]{2,1,0:T(8,128)S(1)} %get-tuple-element.21), channel_id=1, source_target_pairs={{0,6},{1,7},{2,4},{3,5},{4,2},{5,3},{6,0},{7,1},{8,14},{9,15},{10,... | collective-permute-start | bytes 196616 | tf_op jit(solution)/shard_map/ppermute | solution.py:406
  12.2 4.3 %collective-permute-start.4 = (f32[1,128,128]{2,1,0:T(8,128)S(1)}, f32[1,128,128]{2,1,0:T(8,128)S(1)}, u32[]{:S(2)}, u32[]{:S(2)}) collective-permute-start(f32[1,128,128]{2,1,0:T(8,128)S(1)} %get-tuple-element.21), channel_id=1, source_target_pairs={{0,4},{1,5},{2,6},{3,7},{4,0},{5,1},{6,2},{7,3},{8,12},{9,13},{10,... | collective-permute-start | bytes 196616 | tf_op jit(solution)/shard_map/ppermute | solution.py:406
  12.7 4.3 %collective-permute-start.3 = (f32[1,128,128]{2,1,0:T(8,128)S(1)}, f32[1,128,128]{2,1,0:T(8,128)S(1)}, u32[]{:S(2)}, u32[]{:S(2)}) collective-permute-start(f32[1,128,128]{2,1,0:T(8,128)S(1)} %get-tuple-element.21), channel_id=1, source_target_pairs={{0,2},{1,3},{2,0},{3,1},{4,6},{5,7},{6,4},{7,5},{8,10},{9,11},{10,... | collective-permute-start | bytes 196616 | tf_op jit(solution)/shard_map/ppermute | solution.py:406
  13.2 6.4 %collective-permute-start.7 = (bf16[1,2,64,256]{3,2,1,0:T(8,128)(2,1)S(1)}, bf16[1,2,64,256]{3,2,1,0:T(8,128)(2,1)S(1)}, u32[]{:S(2)}, u32[]{:S(2)}) collective-permute-start(bf16[1,2,64,256]{3,2,1,0:T(8,128)(2,1)S(1)} %get-tuple-element.20), channel_id=1, source_target_pairs={{0,16},{16,0},{1,17},{17,1},{2,18},{18,2},{3,19},{19,3},{4,20},{20... | collective-permute-start | bytes 196616 | tf_op jit(solution)/shard_map/ppermute | solution.py:410
  17.0 5.2 %collective-permute-start.6 = (f32[1,128,128]{2,1,0:T(8,128)S(1)}, f32[1,128,128]{2,1,0:T(8,128)S(1)}, u32[]{:S(2)}, u32[]{:S(2)}) collective-permute-start(f32[1,128,128]{2,1,0:T(8,128)S(1)} %add_add_fusion.refs_0_), channel_id=1, source_target_pairs={{0,8},{1,9},{2,10},{3,11},{4,12},{5,13},{6,14},{7,15},{8,0},{9,1},... | collective-permute-start | bytes 196616 | tf_op jit(solution)/shard_map/ppermute | solution.py:406
  25.6 1.4 %collective-permute-start.8 = (f32[1,2,128,128]{3,2,1,0:T(8,128)S(1)}, f32[1,2,128,128]{3,2,1,0:T(8,128)S(1)}, u32[]{:S(2)}, u32[]{:S(2)}) collective-permute-start(f32[1,2,128,128]{3,2,1,0:T(8,128)S(1)} %factor.1.factor_ref), channel_id=1, source_target_pairs={{0,1},{1,0},{2,3},{3,2},{4,5},{5,4},{6,7},{7,6},{8,9},{9,8},{10,11... | collective-permute-start | bytes 393224 | tf_op jit(solution)/shard_map/ppermute | solution.py:406

commit v10 on v9

--- a/solution.py
+++ b/solution.py
@@ -320,7 +320,7 @@
 
 
 def factor_kernel(terms, *refs):
-    out_ref = refs[terms]
+    out_ref = refs[-1]
     total = refs[0][...]
     for r in refs[1:terms]:
         total = total + r[...]
@@ -328,16 +328,16 @@
         invert_factor(total[slot], out_ref, slot)
 
 
-def factor(terms):
+def factor(terms, alive):
     count, order, _ = terms[0].shape
     return pl.pallas_call(
         functools.partial(factor_kernel, len(terms)),
         out_shape=jax.ShapeDtypeStruct((count, 2, order, order), jnp.float32),
-        in_specs=whole_vmem(len(terms)),
+        in_specs=whole_vmem(len(terms)) + [pl.BlockSpec(memory_space=pl.ANY)] * len(alive),
         out_specs=pl.BlockSpec(memory_space=pltpu.VMEM),
         compiler_params=pltpu.CompilerParams(vmem_limit_bytes=VMEM_LIMIT),
         name="factor",
-    )(*terms)
+    )(*terms, *alive)
 
 
 def apply_kernel(other, later, factor_ref, data_ref, *refs):
@@ -422,7 +422,8 @@
         mine, mine_tail, theirs, theirs_tail = project(snapshots, frequencies, offsets, 2)
         own = [mine, swap_tm(theirs)]
         beside = [swap(mine_tail, size, 1), swap_corner(theirs_tail, size)]
-        rest = [mine_tail, swap_tm(theirs_tail)]
+        rest = [mine_tail, swap(beside[1], size, 1)]
+        alive = [theirs_tail]
     else:
         (coeffs,) = project(snapshots, frequencies, offsets, 1)
         regrouped = lax.all_to_all(coeffs, "tm", split_axis=0, concat_axis=2, tiled=True)
@@ -431,6 +432,7 @@
         ordered = jnp.where(lax.axis_index("space") % 2 == 0, regrouped, flipped)
         own, rest = [ordered[:part]], [ordered[part:]]
         beside = [swap(rest[0], size, 1)]
+        alive = []
     held, total = gram(own, beside, scale)
     terms = [total]
     bit = 2
@@ -440,7 +442,7 @@
         terms = [total] + [swap(total, size, mask) for mask in masks]
         bit *= 4
     terms, rest = lax.optimization_barrier((terms, rest))
-    own = factor(terms)
+    own = factor(terms, alive)
     sent = swap(own, size, 1)
     modes, held_rest = apply(own, held, rest)
     return apply(sent, held_rest, earlier=modes)[0]

time: 28.1 us -> 28.1 us (level)
  starting transfers between devices: 10.6 us -> 9.52 us
  waiting for transfers between devices: 9.18 us -> 10.2 us
    ppermute x2 -> x1, starting transfers between devices: 4.08 us -> 3.03 us  [swap_tm(): return lax.ppermute(value, 'tm', [(0, 1), (1, 0)])]
    ppermute x6 -> x7, waiting for transfers between devices: 5.64 us -> 6.68 us  [swap(): return lax.ppermute(value, 'space', [(i, i ^ mask) for i in range(size)])]
    ppermute x6 -> x7, starting transfers between devices: 6.28 us -> 6.29 us  [swap(): return lax.ppermute(value, 'space', [(i, i ^ mask) for i in range(size)])]
    ppermute x2 -> x1, waiting for transfers between devices: 2.1 us -> 2.1 us  [swap_tm(): return lax.ppermute(value, 'tm', [(0, 1), (1, 0)])]
where the time goes in v10:
time: 28.1 us; the launch traced here: 27.9 us
  waiting for transfers between devices  10.2 us (36%)
  starting transfers between devices  9.52 us (34%)
  Pallas kernels  8.12 us (29%)
    ppermute x7, waiting for transfers between devices, swap(): return lax.ppermute(value, 'space', [(i, i ^ mask) for i in range(size)])  6.68 us
    ppermute x7, starting transfers between devices, swap(): return lax.ppermute(value, 'space', [(i, i ^ mask) for i in range(size)])  6.29 us
    pallas_call x1, Pallas kernels, factor(): pl.pallas_call(functools.partial(factor_kernel, len(terms)), out_shape=ja...  3.34 us
    ppermute x1, starting transfers between devices, swap_tm(): return lax.ppermute(value, 'tm', [(0, 1), (1, 0)])  3.03 us
    pallas_call x1, Pallas kernels, project(): pl.pallas_call(functools.partial(project_kernel, groups), out_shape=shape...  2.56 us
    ppermute x1, waiting for transfers between devices, swap_tm(): return lax.ppermute(value, 'tm', [(0, 1), (1, 0)])  2.1 us
    pallas_call x2, Pallas kernels, apply(): pl.pallas_call(functools.partial(apply_kernel, earlier is not None, len(l...  1.9 us
    ppermute x1, waiting for transfers between devices, swap_corner(): return lax.ppermute(value, ('tm', 'space'), pairs)  1.44 us
  transfers between devices with their start and end apart: 9, of which 7 were waited for; matrix products, arithmetic and copies ran while one was open for 0% of the time, Pallas kernels for 3%

profile of v10, /device:TPU:0, one launch (start us, length us, event | category | flops | bytes accessed | tf_op | source)
XLA Modules:
  0.0 27.9 jit_solution(1038190687527693104)
XLA Ops:
  0.0 2.6 %project.1 = (bf16[1,2,64,256]{3,2,1,0:T(8,128)(2,1)S(1)}, bf16[1,2,64,256]{3,2,1,0:T(8,128)(2,1)S(1)}, bf16[1,2,64,256]{3,2,1,0:T(8,128)(2,1)S(1)}, bf16[1,2,64,256]{3,2,1,0:T(8,128)(2,1)S(1)}) custom-call(s32[4]{0:T(128)} %freq_in.1, s32[1,64]{1,0:T(1,128)} %bitcast.1, bf16[64,128,256]{2,1,0:T(8,128)(2,1)} %snap_ref.1), custom_call_target="tpu_custom_call" | custom-call | tf_op jit(solution)/shard_map/project/pallas_call | solution.py:119
  2.6 3.0 %collective-permute-start = (bf16[1,2,64,256]{3,2,1,0:T(8,128)(2,1)S(1)}, bf16[1,2,64,256]{3,2,1,0:T(8,128)(2,1)S(1)}, u32[]{:S(2)}, u32[]{:S(2)}) collective-permute-start(bf16[1,2,64,256]{3,2,1,0:T(8,128)(2,1)S(1)} %get-tuple-element.18), channel_id=1, source_target_pairs={{0,16},{16,0},{1,17},{17,1},{2,18},{18,2},{3,19},{19,3},{4,20},{20... | collective-permute-start | bytes 196616 | tf_op jit(solution)/shard_map/ppermute | solution.py:410
  5.6 0.0 collective-permute-start.1
  5.6 0.2 collective-permute-start.2
  5.8 2.1 %collective-permute-done.refs_1_ = bf16[1,2,64,256]{3,2,1,0:T(8,128)(2,1)S(1)} collective-permute-done((bf16[1,2,64,256]{3,2,1,0:T(8,128)(2,1)S(1)}, bf16[1,2,64,256]{3,2,1,0:T(8,128)(2,1)S(1)}, u32[]{:S(2)}, u32[]{:S(2)}) %collective-permute-start) | collective-permute-done | bytes 65568 | tf_op jit(solution)/shard_map/ppermute | solution.py:410
  7.9 0.0 collective-permute-done.1.refs_2_
  7.9 1.4 %collective-permute-done.2.refs_3_ = bf16[1,2,64,256]{3,2,1,0:T(8,128)(2,1)S(1)} collective-permute-done((bf16[1,2,64,256]{3,2,1,0:T(8,128)(2,1)S(1)}, bf16[1,2,64,256]{3,2,1,0:T(8,128)(2,1)S(1)}, u32[]{:S(2)}, u32[]{:S(2)}) %collective-permute-start.2) | collective-permute-done | bytes 65568 | tf_op jit(solution)/shard_map/ppermute | solution.py:415
  9.3 0.3 %gram.1 = (bf16[1,2,128,256]{3,2,1,0:T(8,128)(2,1)S(1)}, f32[1,128,128]{2,1,0:T(8,128)S(1)}) custom-call(bf16[1,2,64,256]{3,2,1,0:T(8,128)(2,1)S(1)} %get-tuple-element.17.refs_0_, bf16[1,2,64,256]{3,2,1,0:T(8,128)(2,1)S(1)} %collective-permute-done.refs_1_, bf16[1,2,64,256]{3,2,1,0:T(8,128)(2,1)S(1)} %collective-permute-done.1.refs_2_, ...), custom_call_target="tpu_custom_call" | custom-call | tf_op jit(solution)/shard_map/gram/pallas_call | solution.py:166
  9.7 2.6 %collective-permute-start.5 = (f32[1,128,128]{2,1,0:T(8,128)S(1)}, f32[1,128,128]{2,1,0:T(8,128)S(1)}, u32[]{:S(2)}, u32[]{:S(2)}) collective-permute-start(f32[1,128,128]{2,1,0:T(8,128)S(1)} %get-tuple-element.21), channel_id=1, source_target_pairs={{0,6},{1,7},{2,4},{3,5},{4,2},{5,3},{6,0},{7,1},{8,14},{9,15},{10,... | collective-permute-start | bytes 196616 | tf_op jit(solution)/shard_map/ppermute | solution.py:406
  12.2 0.4 %collective-permute-start.4 = (f32[1,128,128]{2,1,0:T(8,128)S(1)}, f32[1,128,128]{2,1,0:T(8,128)S(1)}, u32[]{:S(2)}, u32[]{:S(2)}) collective-permute-start(f32[1,128,128]{2,1,0:T(8,128)S(1)} %get-tuple-element.21), channel_id=1, source_target_pairs={{0,4},{1,5},{2,6},{3,7},{4,0},{5,1},{6,2},{7,3},{8,12},{9,13},{10,... | collective-permute-start | bytes 196616 | tf_op jit(solution)/shard_map/ppermute | solution.py:406
  12.7 0.5 %collective-permute-start.3 = (f32[1,128,128]{2,1,0:T(8,128)S(1)}, f32[1,128,128]{2,1,0:T(8,128)S(1)}, u32[]{:S(2)}, u32[]{:S(2)}) collective-permute-start(f32[1,128,128]{2,1,0:T(8,128)S(1)} %get-tuple-element.21), channel_id=1, source_target_pairs={{0,2},{1,3},{2,0},{3,1},{4,6},{5,7},{6,4},{7,5},{8,10},{9,11},{10,... | collective-permute-start | bytes 196616 | tf_op jit(solution)/shard_map/ppermute | solution.py:406
  13.2 0.0 collective-permute-start.7
  13.2 2.0 %collective-permute-done.5 = f32[1,128,128]{2,1,0:T(8,128)S(1)} collective-permute-done((f32[1,128,128]{2,1,0:T(8,128)S(1)}, f32[1,128,128]{2,1,0:T(8,128)S(1)}, u32[]{:S(2)}, u32[]{:S(2)}) %collective-permute-start.5) | collective-permute-done | bytes 65568 | tf_op jit(solution)/shard_map/ppermute | solution.py:406
  15.2 1.3 %collective-permute-done.4 = f32[1,128,128]{2,1,0:T(8,128)S(1)} collective-permute-done((f32[1,128,128]{2,1,0:T(8,128)S(1)}, f32[1,128,128]{2,1,0:T(8,128)S(1)}, u32[]{:S(2)}, u32[]{:S(2)}) %collective-permute-start.4) | collective-permute-done | bytes 65568 | tf_op jit(solution)/shard_map/ppermute | solution.py:406
  16.5 0.4 %collective-permute-done.3 = f32[1,128,128]{2,1,0:T(8,128)S(1)} collective-permute-done((f32[1,128,128]{2,1,0:T(8,128)S(1)}, f32[1,128,128]{2,1,0:T(8,128)S(1)}, u32[]{:S(2)}, u32[]{:S(2)}) %collective-permute-start.3) | collective-permute-done | bytes 65568 | tf_op jit(solution)/shard_map/ppermute | solution.py:406
  17.0 2.7 %collective-permute-start.6 = (f32[1,128,128]{2,1,0:T(8,128)S(1)}, f32[1,128,128]{2,1,0:T(8,128)S(1)}, u32[]{:S(2)}, u32[]{:S(2)}) collective-permute-start(f32[1,128,128]{2,1,0:T(8,128)S(1)} %add_add_fusion.refs_0_), channel_id=1, source_target_pairs={{0,8},{1,9},{2,10},{3,11},{4,12},{5,13},{6,14},{7,15},{8,0},{9,1},... | collective-permute-start | bytes 196616 | tf_op jit(solution)/shard_map/ppermute | solution.py:406
  19.6 0.0 collective-permute-done.7.refs_1_
  19.6 2.6 %collective-permute-done.6.refs_1_ = f32[1,128,128]{2,1,0:T(8,128)S(1)} collective-permute-done((f32[1,128,128]{2,1,0:T(8,128)S(1)}, f32[1,128,128]{2,1,0:T(8,128)S(1)}, u32[]{:S(2)}, u32[]{:S(2)}) %collective-permute-start.6) | collective-permute-done | bytes 65568 | tf_op jit(solution)/shard_map/ppermute | solution.py:406
  22.2 3.3 %factor.1.factor_ref = f32[1,2,128,128]{3,2,1,0:T(8,128)S(1)} custom-call(f32[1,128,128]{2,1,0:T(8,128)S(1)} %add_add_fusion.refs_0_, f32[1,128,128]{2,1,0:T(8,128)S(1)} %collective-permute-done.6.refs_1_, bf16[1,2,64,256]{3,2,1,0:T(8,128)(2,1)S(1)} %get-tuple-element.20.refs_2_), custom_call_target="tpu_custom_call" | custom-call | tf_op jit(solution)/shard_map/factor/pallas_call | solution.py:333
  25.6 0.1 collective-permute-start.8
  25.6 1.0 %apply.2 = (f32[2,2,128,256]{3,2,1,0:T(8,128)}, bf16[1,2,128,256]{3,2,1,0:T(8,128)(2,1)S(1)}) custom-call(f32[1,2,128,128]{3,2,1,0:T(8,128)S(1)} %factor.1.factor_ref, bf16[1,2,128,256]{3,2,1,0:T(8,128)(2,1)S(1)} %get-tuple-element.24.data_ref, bf16[1,2,64,256]{3,2,1,0:T(8,128)(2,1)S(1)} %get-tuple-element.25.refs_0_, ...), custom_call_target="tpu_custom_call" | custom-call | tf_op jit(solution)/shard_map/apply/pallas_call | solution.py:390
  26.6 0.4 %collective-permute-done.8.factor_ref = f32[1,2,128,128]{3,2,1,0:T(8,128)S(1)} collective-permute-done((f32[1,2,128,128]{3,2,1,0:T(8,128)S(1)}, f32[1,2,128,128]{3,2,1,0:T(8,128)S(1)}, u32[]{:S(2)}, u32[]{:S(2)}) %collective-permute-start.8) | collective-permute-done | bytes 131104 | tf_op jit(solution)/shard_map/ppermute | solution.py:406
  27.0 0.9 %apply.3 = f32[2,2,128,256]{3,2,1,0:T(8,128)} custom-call(f32[1,2,128,128]{3,2,1,0:T(8,128)S(1)} %collective-permute-done.8.factor_ref, bf16[1,2,128,256]{3,2,1,0:T(8,128)(2,1)S(1)} %get-tuple-element.27.data_ref, f32[2,2,128,256]{3,2,1,0:T(8,128)} %get-tuple-element.28.refs_0_), custom_call_target="tpu_custom_call", output_to_operand_aliasing={{}: (2, {})} | custom-call | tf_op jit(solution)/shard_map/apply/pallas_call | solution.py:390
  (1 shorter events, 0.0 us)
Async XLA Ops:
  2.6 5.3 %collective-permute-start = (bf16[1,2,64,256]{3,2,1,0:T(8,128)(2,1)S(1)}, bf16[1,2,64,256]{3,2,1,0:T(8,128)(2,1)S(1)}, u32[]{:S(2)}, u32[]{:S(2)}) collective-permute-start(bf16[1,2,64,256]{3,2,1,0:T(8,128)(2,1)S(1)} %get-tuple-element.18), channel_id=1, source_target_pairs={{0,16},{16,0},{1,17},{17,1},{2,18},{18,2},{3,19},{19,3},{4,20},{20... | collective-permute-start | bytes 196616 | tf_op jit(solution)/shard_map/ppermute | solution.py:410
  5.6 2.3 %collective-permute-start.1 = (bf16[1,2,64,256]{3,2,1,0:T(8,128)(2,1)S(1)}, bf16[1,2,64,256]{3,2,1,0:T(8,128)(2,1)S(1)}, u32[]{:S(2)}, u32[]{:S(2)}) collective-permute-start(bf16[1,2,64,256]{3,2,1,0:T(8,128)(2,1)S(1)} %get-tuple-element.25.refs_0_), channel_id=1, source_target_pairs={{0,1},{1,0},{2,3},{3,2},{4,5},{5,4},{6,7},{7,6},{8,9},{9,8},{10,11... | collective-permute-start | bytes 196616 | tf_op jit(solution)/shard_map/ppermute | solution.py:406
  5.6 3.7 %collective-permute-start.2 = (bf16[1,2,64,256]{3,2,1,0:T(8,128)(2,1)S(1)}, bf16[1,2,64,256]{3,2,1,0:T(8,128)(2,1)S(1)}, u32[]{:S(2)}, u32[]{:S(2)}) collective-permute-start(bf16[1,2,64,256]{3,2,1,0:T(8,128)(2,1)S(1)} %get-tuple-element.20.refs_2_), channel_id=1, source_target_pairs={{0,17},{1,16},{2,19},{3,18},{4,21},{5,20},{6,23},{7,22},{8,25},{9,... | collective-permute-start | bytes 196616 | tf_op jit(solution)/shard_map/ppermute | solution.py:415
  9.7 5.6 %collective-permute-start.5 = (f32[1,128,128]{2,1,0:T(8,128)S(1)}, f32[1,128,128]{2,1,0:T(8,128)S(1)}, u32[]{:S(2)}, u32[]{:S(2)}) collective-permute-start(f32[1,128,128]{2,1,0:T(8,128)S(1)} %get-tuple-element.21), channel_id=1, source_target_pairs={{0,6},{1,7},{2,4},{3,5},{4,2},{5,3},{6,0},{7,1},{8,14},{9,15},{10,... | collective-permute-start | bytes 196616 | tf_op jit(solution)/shard_map/ppermute | solution.py:406
  12.2 4.3 %collective-permute-start.4 = (f32[1,128,128]{2,1,0:T(8,128)S(1)}, f32[1,128,128]{2,1,0:T(8,128)S(1)}, u32[]{:S(2)}, u32[]{:S(2)}) collective-permute-start(f32[1,128,128]{2,1,0:T(8,128)S(1)} %get-tuple-element.21), channel_id=1, source_target_pairs={{0,4},{1,5},{2,6},{3,7},{4,0},{5,1},{6,2},{7,3},{8,12},{9,13},{10,... | collective-permute-start | bytes 196616 | tf_op jit(solution)/shard_map/ppermute | solution.py:406
  12.7 4.3 %collective-permute-start.3 = (f32[1,128,128]{2,1,0:T(8,128)S(1)}, f32[1,128,128]{2,1,0:T(8,128)S(1)}, u32[]{:S(2)}, u32[]{:S(2)}) collective-permute-start(f32[1,128,128]{2,1,0:T(8,128)S(1)} %get-tuple-element.21), channel_id=1, source_target_pairs={{0,2},{1,3},{2,0},{3,1},{4,6},{5,7},{6,4},{7,5},{8,10},{9,11},{10,... | collective-permute-start | bytes 196616 | tf_op jit(solution)/shard_map/ppermute | solution.py:406
  13.2 6.4 %collective-permute-start.7 = (bf16[1,2,64,256]{3,2,1,0:T(8,128)(2,1)S(1)}, bf16[1,2,64,256]{3,2,1,0:T(8,128)(2,1)S(1)}, u32[]{:S(2)}, u32[]{:S(2)}) collective-permute-start(bf16[1,2,64,256]{3,2,1,0:T(8,128)(2,1)S(1)} %collective-permute-done.2.refs_3_), channel_id=1, source_target_pairs={{0,1},{1,0},{2,3},{3,2},{4,5},{5,4},{6,7},{7,6},{8,9},{9,8},{10,11... | collective-permute-start | bytes 196616 | tf_op jit(solution)/shard_map/ppermute | solution.py:406
  17.0 5.2 %collective-permute-start.6 = (f32[1,128,128]{2,1,0:T(8,128)S(1)}, f32[1,128,128]{2,1,0:T(8,128)S(1)}, u32[]{:S(2)}, u32[]{:S(2)}) collective-permute-start(f32[1,128,128]{2,1,0:T(8,128)S(1)} %add_add_fusion.refs_0_), channel_id=1, source_target_pairs={{0,8},{1,9},{2,10},{3,11},{4,12},{5,13},{6,14},{7,15},{8,0},{9,1},... | collective-permute-start | bytes 196616 | tf_op jit(solution)/shard_map/ppermute | solution.py:406
  25.6 1.4 %collective-permute-start.8 = (f32[1,2,128,128]{3,2,1,0:T(8,128)S(1)}, f32[1,2,128,128]{3,2,1,0:T(8,128)S(1)}, u32[]{:S(2)}, u32[]{:S(2)}) collective-permute-start(f32[1,2,128,128]{3,2,1,0:T(8,128)S(1)} %factor.1.factor_ref), channel_id=1, source_target_pairs={{0,1},{1,0},{2,3},{3,2},{4,5},{5,4},{6,7},{7,6},{8,9},{9,8},{10,11... | collective-permute-start | bytes 393224 | tf_op jit(solution)/shard_map/ppermute | solution.py:406
